TPU v7x, 256 devices: a whole 4x4x8 slice. The times are simulated.
256 devices in a mesh: cluster: 128 (over z, x_hi, y, core), narrow: 2 (over x_lo).
Axes of the slice: x: 4 (x_hi: 2, x_lo: 2; x = x_hi * 2 + x_lo), y: 4, z: 8, core: 2. Of those that a mesh axis runs over, the one named last changes fastest.
Arguments:
- panels: float32 [98, 131072], P(None, ('cluster', 'narrow')), may hold values from -103.4 to 103.4, as said below
- test_points: float32 [14, 131072], P(None, ('cluster', 'narrow')), may hold values from -103.4 to 103.4, as said below
- currents: float32 [512, 131072], P(None, ('cluster', 'narrow')), may hold values from -6 to 6
- near_mask: int32 [1024, 7], P(('cluster', 'narrow')), may hold values from 0 to 1, as said below
Outputs:
- product: float32 [512, 131072], P(None, ('cluster', 'narrow'))
Inputs may be any that keep to these rules, and one draw needn't show every extreme that they name: Rows of panels are 7 channels of 14 points (channel * 14 + point): position x, y, z, weighted basis vector x, y, z, weighted divergence. Positions of block b lie near angle 2 pi b / 1024 on a circle. Rows of test_points are 7 channels of the two centroids (channel * 2 + centroid), channels as in panels. `near_mask`: column c marks source offset c - 3. Column 3 is 1 in every row. Every block of some clusters of the first half of the cluster axis has all columns 1; in the other blocks only the columns of offsets -1 and 1 may be 1 besides it.
All inputs are finite; a program needn't handle non-finite values.
Results may differ from a plain program's by a relative error of at most 0.0003.
Values sent between devices are 32-bit elements; how exact they have to be, the bound alone decides.
A program may use at most 128 MiB of HBM per device.

v0:
```python
import jax
import jax.numpy as jnp
from jax import lax
from jax.sharding import PartitionSpec as P

WAVES = ((2.0, 0.0), (1.0, 3.0))
CONTRAST = 0.5
SOFTEN = 0.04


def with_halo(block, sides, width):
    for axis, dim in sides:
        count = lax.axis_size(axis)
        forward = [(i, i + 1) for i in range(count - 1)]
        forward.append((count - 1, 0))
        backward = [(target, source) for source, target in forward]
        low = lax.ppermute(
            lax.slice_in_dim(block, block.shape[dim] - width, None, axis=dim), axis, forward
        )
        high = lax.ppermute(lax.slice_in_dim(block, 0, width, axis=dim), axis, backward)
        block = jnp.concatenate([low, block, high], axis=dim)
    return block


def tile_ops(tester_geom, source_geom):
    npoints = source_geom.shape[0] // 7
    ncentres = tester_geom.shape[0] // 7
    source = source_geom.reshape(7, npoints, source_geom.shape[1])
    tester = tester_geom.reshape(7, ncentres, tester_geom.shape[1])
    summed = jnp.zeros((6, tester.shape[2], source.shape[2]), jnp.float32)
    for centre in range(ncentres):
        deltas = [
            tester[component, centre][None, :, None] - source[component][:, None, :]
            for component in range(3)
        ]
        distance = jnp.sqrt(
            deltas[0] * deltas[0] + deltas[1] * deltas[1] + deltas[2] * deltas[2] + SOFTEN
        )
        tvector = [tester[3 + component, centre][None, :, None] for component in range(3)]
        svector = [source[3 + component][:, None, :] for component in range(3)]
        dotted = tvector[0] * svector[0] + tvector[1] * svector[1] + tvector[2] * svector[2]
        charge = tester[6, centre][None, :, None] * source[6][:, None, :]
        crossed = (
            deltas[0] * (svector[1] * tvector[2] - svector[2] * tvector[1])
            + deltas[1] * (svector[2] * tvector[0] - svector[0] * tvector[2])
            + deltas[2] * (svector[0] * tvector[1] - svector[1] * tvector[0])
        )
        media = []
        for wave_real, wave_imag in WAVES:
            decay = jnp.exp(-wave_imag * distance) / distance
            green_real = decay * jnp.cos(wave_real * distance)
            green_imag = decay * jnp.sin(wave_real * distance)
            coef_real = (wave_real * wave_real - wave_imag * wave_imag) * dotted - charge
            coef_imag = 2.0 * wave_real * wave_imag * dotted
            ell_real = coef_real * green_real - coef_imag * green_imag
            ell_imag = coef_real * green_imag + coef_imag * green_real
            factor_real = -wave_imag * distance - 1.0
            factor_imag = wave_real * distance
            scaled = crossed / (distance * distance)
            kay_real = scaled * (factor_real * green_real - factor_imag * green_imag)
            kay_imag = scaled * (factor_real * green_imag + factor_imag * green_real)
            media.append(
                (
                    jnp.sum(ell_real, 0),
                    jnp.sum(ell_imag, 0),
                    jnp.sum(kay_real, 0),
                    jnp.sum(kay_imag, 0),
                )
            )
        first, second = media
        stacked = jnp.stack(
            [
                first[0] + second[0],
                first[1] + second[1],
                first[2] + second[2],
                first[3] + second[3],
                first[0] + CONTRAST * second[0],
                first[1] + CONTRAST * second[1],
            ]
        )
        summed = summed + stacked
    return summed


def apply_tile(operators, flowing):
    rows = flowing.shape[0] // 4
    product = jnp.einsum("mij,cj->mci", operators, flowing, precision=lax.Precision.HIGHEST)

    def select(which, group):
        return product[which, group * rows : (group + 1) * rows]

    out_jreal = select(0, 0) - select(1, 1) - select(2, 2) + select(3, 3)
    out_jimag = select(1, 0) + select(0, 1) - select(3, 2) - select(2, 3)
    out_mreal = select(2, 0) - select(3, 1) + select(4, 2) - select(5, 3)
    out_mimag = select(3, 0) + select(2, 1) + select(5, 2) + select(4, 3)
    return jnp.concatenate([out_jreal, out_jimag, out_mreal, out_mimag], 0)


def body(panels, test_points, currents, near_mask):
    blocks_dev = near_mask.shape[0]
    span = near_mask.shape[1]
    reach = span // 2
    blocksize = test_points.shape[1] // blocks_dev
    geo_rows = panels.shape[0]
    batch_tiles = 4
    stacked_local = jnp.concatenate([panels, currents], 0)
    cluster_cols = lax.all_gather(stacked_local, "narrow", axis=1, tiled=True)
    window = with_halo(cluster_cols, (("cluster", 1),), reach * blocksize)
    position = lax.axis_index("narrow")
    flagged = near_mask.reshape(-1)
    ranking = jnp.cumsum(flagged) - 1
    slot_ids = jnp.arange(flagged.shape[0], dtype=jnp.int32)
    count = jnp.sum(flagged)

    def slot_at(rank_value):
        return jnp.sum(jnp.where((ranking == rank_value) & (flagged > 0), slot_ids, 0))

    def tile_inputs(slot):
        test_block = slot // span
        offset = slot % span
        tester = lax.dynamic_slice_in_dim(test_points, test_block * blocksize, blocksize, 1)
        columns = lax.dynamic_slice_in_dim(
            window, (position * blocks_dev + test_block + offset) * blocksize, blocksize, 1
        )
        return (test_block, tester, columns)

    def add_into(result, test_block, term):
        segment = lax.dynamic_slice_in_dim(result, test_block * blocksize, blocksize, 1)
        return lax.dynamic_update_slice_in_dim(result, segment + term, test_block * blocksize, 1)

    def one_tile(rank_value):
        test_block, tester, columns = tile_inputs(slot_at(rank_value))
        return (test_block, apply_tile(tile_ops(tester, columns[:geo_rows]), columns[geo_rows:]))

    result = jnp.zeros((currents.shape[0], test_points.shape[1]), jnp.float32)

    def group_step(group, running):
        ranks = group * batch_tiles + jnp.arange(batch_tiles, dtype=jnp.int32)
        live = (ranks < count).astype(jnp.float32)
        test_blocks, terms = jax.vmap(one_tile)(ranks)
        for member in range(batch_tiles):
            running = add_into(running, test_blocks[member], terms[member] * live[member])
        return running

    result = lax.fori_loop(0, (count + batch_tiles - 1) // batch_tiles, group_step, result)
    return result


def solution(mesh):
    return jax.shard_map(
        body,
        mesh=mesh,
        in_specs=(
            P(None, ("cluster", "narrow")),
            P(None, ("cluster", "narrow")),
            P(None, ("cluster", "narrow")),
            P(("cluster", "narrow"), None),
        ),
        out_specs=P(None, ("cluster", "narrow")),
        check_vma=False,
    )
```

profile of v0, /device:TPU:125, one launch (start us, length us, event | category | flops | bytes accessed | tf_op | source)
XLA Modules:
  0.0 852.5 jit_solution(17095894633585107569)
XLA Ops:
  6.5 2.4 pad_maximum_fusion.2
  9.0 44.4 %all-gather.2.cloned.1.call-done = f32[610,1024]{1,0:T(8,128)} async-done(((f32[610,512]{1,0:T(8,128)}), f32[610,1024]{1,0:T(8,128)}) %all-gather.2.cloned.1.call-update) | async-done | bytes 2498576 | tf_op jit(solution)/shard_map/all_gather | solution.py:107
  53.5 2.5 fusion.65
  56.0 3.3 collective-permute-start
  60.9 9.3 %collective-permute-done = f32[610,384]{1,0:T(8,128)S(1)} collective-permute-done((f32[610,384]{1,0:T(8,128)}, f32[610,384]{1,0:T(8,128)S(1)}, u32[]{:S(2)}, u32[]{:S(2)}) %collective-permute-start) | collective-permute-done | bytes 936992 | tf_op jit(solution)/shard_map/ppermute | solution.py:17
  70.2 7.9 collective-permute-done.1
  78.1 4.1 pad_maximum_fusion.1
  82.3 762.4 %while.22 = (s32[]{:T(128)}, f32[512,512]{1,0:T(8,128)S(1)}, s32[]{:T(128)}, s32[28]{0:T(128)S(1)}, s32[28]{0:T(128)S(1)}, /*index=5*/s32[]{:T(128)}, f32[610,17...) while((s32[]{:T(128)}, f32[512,512]{1,0:T(8,128)S(1)}, ...), condition=%wide.region_20.21_spmd.clone, body=%wide.region_2.20_spmd.clone.sunk | while | flops 2572550656 | bytes 37368140 | solution.py:145
  82.8 10.3 %while.23 = (s32[]{:T(128)}, f32[610,1792]{1,0:T(8,128)}, s32[4,2]{0,1:T(2,128)S(1)}, f32[4,610,128]{2,1,0:T(8,128)S(1)}, s32[]{:T(128)}) while((s32[]{:T(128)}, f32[610,1792]{1,0:T(8,128)}, s32[4,2]{0,1:T(2,128)S(1)}, f32[4,610,128]{2,1,0:T(8,128)S(1)}, s32[]{:T(128)}) %tuple.129), condition=%wide.while_cond, body=%wide.while_body.sunk | while | flops 2 | bytes 627809 | solution.py:122
  83.4 1.9 bitcast_dynamic-update-slice_fusion.14
  86.0 1.9 bitcast_dynamic-update-slice_fusion.14
  88.6 1.9 bitcast_dynamic-update-slice_fusion.14
  91.2 1.9 bitcast_dynamic-update-slice_fusion.14
  93.3 8.9 %while.24 = (s32[]{:T(128)}, f32[14,512]{1,0:T(8,128)}, s32[4,2]{0,1:T(2,128)S(1)}, f32[4,14,128]{2,0,1:T(4,128)S(1)}, s32[]{:T(128)}, /*index=5*/s32[]{:T(128)}) while((s32[]{:T(128)}, f32[14,512]{1,0:T(8,128)}, s32[4,2]{0,1:T(2,128)S(1)}, f32[4,14,128]{2,0,1:T(4,128)S(1)}, s32[]{:T(128)}, /*index=5*/s32[]{:T(128)}) %tuple.132), condition=%wide.while_cond.1, body=%wide.while_body.1.sunk | while | flops 2 | bytes 43113 | solution.py:121
  102.2 37.8 %multiply_reduce_fusion.9 = (f32[4,128,128]{2,1,0:T(8,128)S(1)}, f32[4,128,128]{2,1,0:T(8,128)S(1)}, f32[4,128,128]{2,1,0:T(8,128)S(1)}, f32[4,128,128]{2,1,0:T(...) fusion(f32[4,14,128]{2,1,0:T(8,128)S(1)} %copy.108, ...), kind=kLoop, calls=%fused_computation.52.clone.1 | loop fusion | flops 76546048 | bytes 2312192 | tf_op jit(solution)/shard_map/while/body/vmap()/reduce_sum | solution.py:67
  140.2 37.9 %add_reduce_fusion.6 = (f32[4,128,128]{2,1,0:T(8,128)S(1)}, f32[4,128,128]{2,1,0:T(8,128)S(1)}, f32[4,128,128]{2,1,0:T(8,128)S(1)}, f32[4,128,128]{2,1,0:T(8,128...) fusion(f32[4,128]{1,0:T(4,128)S(1)} %get-tuple-element.483, ...), kind=kLoop, calls=%fused_computation.40.clone.1 | loop fusion | flops 76546048 | bytes 2312192 | tf_op jit(solution)/shard_map/while/body/vmap()/reduce_sum | solution.py:65
  178.3 5.4 convolution_bitcast_fusion.2
  191.6 10.3 %while.23 = (s32[]{:T(128)}, f32[610,1792]{1,0:T(8,128)}, s32[4,2]{0,1:T(2,128)S(1)}, f32[4,610,128]{2,1,0:T(8,128)S(1)}, s32[]{:T(128)}) while((s32[]{:T(128)}, f32[610,1792]{1,0:T(8,128)}, s32[4,2]{0,1:T(2,128)S(1)}, f32[4,610,128]{2,1,0:T(8,128)S(1)}, s32[]{:T(128)}) %tuple.129), condition=%wide.while_cond, body=%wide.while_body.sunk | while | flops 2 | bytes 627809 | solution.py:122
  192.3 1.9 bitcast_dynamic-update-slice_fusion.14
  202.2 8.9 %while.24 = (s32[]{:T(128)}, f32[14,512]{1,0:T(8,128)}, s32[4,2]{0,1:T(2,128)S(1)}, f32[4,14,128]{2,0,1:T(4,128)S(1)}, s32[]{:T(128)}, /*index=5*/s32[]{:T(128)}) while((s32[]{:T(128)}, f32[14,512]{1,0:T(8,128)}, s32[4,2]{0,1:T(2,128)S(1)}, f32[4,14,128]{2,0,1:T(4,128)S(1)}, s32[]{:T(128)}, /*index=5*/s32[]{:T(128)}) %tuple.132), condition=%wide.while_cond.1, body=%wide.while_body.1.sunk | while | flops 2 | bytes 43113 | solution.py:121
  211.1 37.8 %multiply_reduce_fusion.9 = (f32[4,128,128]{2,1,0:T(8,128)S(1)}, f32[4,128,128]{2,1,0:T(8,128)S(1)}, f32[4,128,128]{2,1,0:T(8,128)S(1)}, f32[4,128,128]{2,1,0:T(...) fusion(f32[4,14,128]{2,1,0:T(8,128)S(1)} %copy.108, ...), kind=kLoop, calls=%fused_computation.52.clone.1 | loop fusion | flops 76546048 | bytes 2312192 | tf_op jit(solution)/shard_map/while/body/vmap()/reduce_sum | solution.py:67
  249.1 37.9 %add_reduce_fusion.6 = (f32[4,128,128]{2,1,0:T(8,128)S(1)}, f32[4,128,128]{2,1,0:T(8,128)S(1)}, f32[4,128,128]{2,1,0:T(8,128)S(1)}, f32[4,128,128]{2,1,0:T(8,128...) fusion(f32[4,128]{1,0:T(4,128)S(1)} %get-tuple-element.483, ...), kind=kLoop, calls=%fused_computation.40.clone.1 | loop fusion | flops 76546048 | bytes 2312192 | tf_op jit(solution)/shard_map/while/body/vmap()/reduce_sum | solution.py:65
  287.2 5.4 convolution_bitcast_fusion.2
  300.5 10.3 %while.23 = (s32[]{:T(128)}, f32[610,1792]{1,0:T(8,128)}, s32[4,2]{0,1:T(2,128)S(1)}, f32[4,610,128]{2,1,0:T(8,128)S(1)}, s32[]{:T(128)}) while((s32[]{:T(128)}, f32[610,1792]{1,0:T(8,128)}, s32[4,2]{0,1:T(2,128)S(1)}, f32[4,610,128]{2,1,0:T(8,128)S(1)}, s32[]{:T(128)}) %tuple.129), condition=%wide.while_cond, body=%wide.while_body.sunk | while | flops 2 | bytes 627809 | solution.py:122
  311.0 8.9 %while.24 = (s32[]{:T(128)}, f32[14,512]{1,0:T(8,128)}, s32[4,2]{0,1:T(2,128)S(1)}, f32[4,14,128]{2,0,1:T(4,128)S(1)}, s32[]{:T(128)}, /*index=5*/s32[]{:T(128)}) while((s32[]{:T(128)}, f32[14,512]{1,0:T(8,128)}, s32[4,2]{0,1:T(2,128)S(1)}, f32[4,14,128]{2,0,1:T(4,128)S(1)}, s32[]{:T(128)}, /*index=5*/s32[]{:T(128)}) %tuple.132), condition=%wide.while_cond.1, body=%wide.while_body.1.sunk | while | flops 2 | bytes 43113 | solution.py:121
  319.9 37.8 %multiply_reduce_fusion.9 = (f32[4,128,128]{2,1,0:T(8,128)S(1)}, f32[4,128,128]{2,1,0:T(8,128)S(1)}, f32[4,128,128]{2,1,0:T(8,128)S(1)}, f32[4,128,128]{2,1,0:T(...) fusion(f32[4,14,128]{2,1,0:T(8,128)S(1)} %copy.108, ...), kind=kLoop, calls=%fused_computation.52.clone.1 | loop fusion | flops 76546048 | bytes 2312192 | tf_op jit(solution)/shard_map/while/body/vmap()/reduce_sum | solution.py:67
  357.9 37.9 %add_reduce_fusion.6 = (f32[4,128,128]{2,1,0:T(8,128)S(1)}, f32[4,128,128]{2,1,0:T(8,128)S(1)}, f32[4,128,128]{2,1,0:T(8,128)S(1)}, f32[4,128,128]{2,1,0:T(8,128...) fusion(f32[4,128]{1,0:T(4,128)S(1)} %get-tuple-element.483, ...), kind=kLoop, calls=%fused_computation.40.clone.1 | loop fusion | flops 76546048 | bytes 2312192 | tf_op jit(solution)/shard_map/while/body/vmap()/reduce_sum | solution.py:65
  396.1 5.4 convolution_bitcast_fusion.2
  409.4 10.3 %while.23 = (s32[]{:T(128)}, f32[610,1792]{1,0:T(8,128)}, s32[4,2]{0,1:T(2,128)S(1)}, f32[4,610,128]{2,1,0:T(8,128)S(1)}, s32[]{:T(128)}) while((s32[]{:T(128)}, f32[610,1792]{1,0:T(8,128)}, s32[4,2]{0,1:T(2,128)S(1)}, f32[4,610,128]{2,1,0:T(8,128)S(1)}, s32[]{:T(128)}) %tuple.129), condition=%wide.while_cond, body=%wide.while_body.sunk | while | flops 2 | bytes 627809 | solution.py:122
  419.9 8.9 %while.24 = (s32[]{:T(128)}, f32[14,512]{1,0:T(8,128)}, s32[4,2]{0,1:T(2,128)S(1)}, f32[4,14,128]{2,0,1:T(4,128)S(1)}, s32[]{:T(128)}, /*index=5*/s32[]{:T(128)}) while((s32[]{:T(128)}, f32[14,512]{1,0:T(8,128)}, s32[4,2]{0,1:T(2,128)S(1)}, f32[4,14,128]{2,0,1:T(4,128)S(1)}, s32[]{:T(128)}, /*index=5*/s32[]{:T(128)}) %tuple.132), condition=%wide.while_cond.1, body=%wide.while_body.1.sunk | while | flops 2 | bytes 43113 | solution.py:121
  428.8 37.8 %multiply_reduce_fusion.9 = (f32[4,128,128]{2,1,0:T(8,128)S(1)}, f32[4,128,128]{2,1,0:T(8,128)S(1)}, f32[4,128,128]{2,1,0:T(8,128)S(1)}, f32[4,128,128]{2,1,0:T(...) fusion(f32[4,14,128]{2,1,0:T(8,128)S(1)} %copy.108, ...), kind=kLoop, calls=%fused_computation.52.clone.1 | loop fusion | flops 76546048 | bytes 2312192 | tf_op jit(solution)/shard_map/while/body/vmap()/reduce_sum | solution.py:67
  466.8 37.9 %add_reduce_fusion.6 = (f32[4,128,128]{2,1,0:T(8,128)S(1)}, f32[4,128,128]{2,1,0:T(8,128)S(1)}, f32[4,128,128]{2,1,0:T(8,128)S(1)}, f32[4,128,128]{2,1,0:T(8,128...) fusion(f32[4,128]{1,0:T(4,128)S(1)} %get-tuple-element.483, ...), kind=kLoop, calls=%fused_computation.40.clone.1 | loop fusion | flops 76546048 | bytes 2312192 | tf_op jit(solution)/shard_map/while/body/vmap()/reduce_sum | solution.py:65
  504.9 5.4 convolution_bitcast_fusion.2
  518.2 10.3 %while.23 = (s32[]{:T(128)}, f32[610,1792]{1,0:T(8,128)}, s32[4,2]{0,1:T(2,128)S(1)}, f32[4,610,128]{2,1,0:T(8,128)S(1)}, s32[]{:T(128)}) while((s32[]{:T(128)}, f32[610,1792]{1,0:T(8,128)}, s32[4,2]{0,1:T(2,128)S(1)}, f32[4,610,128]{2,1,0:T(8,128)S(1)}, s32[]{:T(128)}) %tuple.129), condition=%wide.while_cond, body=%wide.while_body.sunk | while | flops 2 | bytes 627809 | solution.py:122
  528.8 8.9 %while.24 = (s32[]{:T(128)}, f32[14,512]{1,0:T(8,128)}, s32[4,2]{0,1:T(2,128)S(1)}, f32[4,14,128]{2,0,1:T(4,128)S(1)}, s32[]{:T(128)}, /*index=5*/s32[]{:T(128)}) while((s32[]{:T(128)}, f32[14,512]{1,0:T(8,128)}, s32[4,2]{0,1:T(2,128)S(1)}, f32[4,14,128]{2,0,1:T(4,128)S(1)}, s32[]{:T(128)}, /*index=5*/s32[]{:T(128)}) %tuple.132), condition=%wide.while_cond.1, body=%wide.while_body.1.sunk | while | flops 2 | bytes 43113 | solution.py:121
  537.7 37.8 %multiply_reduce_fusion.9 = (f32[4,128,128]{2,1,0:T(8,128)S(1)}, f32[4,128,128]{2,1,0:T(8,128)S(1)}, f32[4,128,128]{2,1,0:T(8,128)S(1)}, f32[4,128,128]{2,1,0:T(...) fusion(f32[4,14,128]{2,1,0:T(8,128)S(1)} %copy.108, ...), kind=kLoop, calls=%fused_computation.52.clone.1 | loop fusion | flops 76546048 | bytes 2312192 | tf_op jit(solution)/shard_map/while/body/vmap()/reduce_sum | solution.py:67
  575.7 37.9 %add_reduce_fusion.6 = (f32[4,128,128]{2,1,0:T(8,128)S(1)}, f32[4,128,128]{2,1,0:T(8,128)S(1)}, f32[4,128,128]{2,1,0:T(8,128)S(1)}, f32[4,128,128]{2,1,0:T(8,128...) fusion(f32[4,128]{1,0:T(4,128)S(1)} %get-tuple-element.483, ...), kind=kLoop, calls=%fused_computation.40.clone.1 | loop fusion | flops 76546048 | bytes 2312192 | tf_op jit(solution)/shard_map/while/body/vmap()/reduce_sum | solution.py:65
  613.8 5.4 convolution_bitcast_fusion.2
  627.1 10.3 %while.23 = (s32[]{:T(128)}, f32[610,1792]{1,0:T(8,128)}, s32[4,2]{0,1:T(2,128)S(1)}, f32[4,610,128]{2,1,0:T(8,128)S(1)}, s32[]{:T(128)}) while((s32[]{:T(128)}, f32[610,1792]{1,0:T(8,128)}, s32[4,2]{0,1:T(2,128)S(1)}, f32[4,610,128]{2,1,0:T(8,128)S(1)}, s32[]{:T(128)}) %tuple.129), condition=%wide.while_cond, body=%wide.while_body.sunk | while | flops 2 | bytes 627809 | solution.py:122
  637.7 8.8 %while.24 = (s32[]{:T(128)}, f32[14,512]{1,0:T(8,128)}, s32[4,2]{0,1:T(2,128)S(1)}, f32[4,14,128]{2,0,1:T(4,128)S(1)}, s32[]{:T(128)}, /*index=5*/s32[]{:T(128)}) while((s32[]{:T(128)}, f32[14,512]{1,0:T(8,128)}, s32[4,2]{0,1:T(2,128)S(1)}, f32[4,14,128]{2,0,1:T(4,128)S(1)}, s32[]{:T(128)}, /*index=5*/s32[]{:T(128)}) %tuple.132), condition=%wide.while_cond.1, body=%wide.while_body.1.sunk | while | flops 2 | bytes 43113 | solution.py:121
  646.5 37.8 %multiply_reduce_fusion.9 = (f32[4,128,128]{2,1,0:T(8,128)S(1)}, f32[4,128,128]{2,1,0:T(8,128)S(1)}, f32[4,128,128]{2,1,0:T(8,128)S(1)}, f32[4,128,128]{2,1,0:T(...) fusion(f32[4,14,128]{2,1,0:T(8,128)S(1)} %copy.108, ...), kind=kLoop, calls=%fused_computation.52.clone.1 | loop fusion | flops 76546048 | bytes 2312192 | tf_op jit(solution)/shard_map/while/body/vmap()/reduce_sum | solution.py:67
  684.5 37.9 %add_reduce_fusion.6 = (f32[4,128,128]{2,1,0:T(8,128)S(1)}, f32[4,128,128]{2,1,0:T(8,128)S(1)}, f32[4,128,128]{2,1,0:T(8,128)S(1)}, f32[4,128,128]{2,1,0:T(8,128...) fusion(f32[4,128]{1,0:T(4,128)S(1)} %get-tuple-element.483, ...), kind=kLoop, calls=%fused_computation.40.clone.1 | loop fusion | flops 76546048 | bytes 2312192 | tf_op jit(solution)/shard_map/while/body/vmap()/reduce_sum | solution.py:65
  722.6 5.4 convolution_bitcast_fusion.2
  735.9 10.3 %while.23 = (s32[]{:T(128)}, f32[610,1792]{1,0:T(8,128)}, s32[4,2]{0,1:T(2,128)S(1)}, f32[4,610,128]{2,1,0:T(8,128)S(1)}, s32[]{:T(128)}) while((s32[]{:T(128)}, f32[610,1792]{1,0:T(8,128)}, s32[4,2]{0,1:T(2,128)S(1)}, f32[4,610,128]{2,1,0:T(8,128)S(1)}, s32[]{:T(128)}) %tuple.129), condition=%wide.while_cond, body=%wide.while_body.sunk | while | flops 2 | bytes 627809 | solution.py:122
  746.5 8.8 %while.24 = (s32[]{:T(128)}, f32[14,512]{1,0:T(8,128)}, s32[4,2]{0,1:T(2,128)S(1)}, f32[4,14,128]{2,0,1:T(4,128)S(1)}, s32[]{:T(128)}, /*index=5*/s32[]{:T(128)}) while((s32[]{:T(128)}, f32[14,512]{1,0:T(8,128)}, s32[4,2]{0,1:T(2,128)S(1)}, f32[4,14,128]{2,0,1:T(4,128)S(1)}, s32[]{:T(128)}, /*index=5*/s32[]{:T(128)}) %tuple.132), condition=%wide.while_cond.1, body=%wide.while_body.1.sunk | while | flops 2 | bytes 43113 | solution.py:121
  755.3 37.8 %multiply_reduce_fusion.9 = (f32[4,128,128]{2,1,0:T(8,128)S(1)}, f32[4,128,128]{2,1,0:T(8,128)S(1)}, f32[4,128,128]{2,1,0:T(8,128)S(1)}, f32[4,128,128]{2,1,0:T(...) fusion(f32[4,14,128]{2,1,0:T(8,128)S(1)} %copy.108, ...), kind=kLoop, calls=%fused_computation.52.clone.1 | loop fusion | flops 76546048 | bytes 2312192 | tf_op jit(solution)/shard_map/while/body/vmap()/reduce_sum | solution.py:67
  793.3 37.9 %add_reduce_fusion.6 = (f32[4,128,128]{2,1,0:T(8,128)S(1)}, f32[4,128,128]{2,1,0:T(8,128)S(1)}, f32[4,128,128]{2,1,0:T(8,128)S(1)}, f32[4,128,128]{2,1,0:T(8,128...) fusion(f32[4,128]{1,0:T(4,128)S(1)} %get-tuple-element.483, ...), kind=kLoop, calls=%fused_computation.40.clone.1 | loop fusion | flops 76546048 | bytes 2312192 | tf_op jit(solution)/shard_map/while/body/vmap()/reduce_sum | solution.py:65
  831.4 5.4 convolution_bitcast_fusion.2
  (526 shorter events, 166.0 us)
Async XLA Ops:
  6.5 52.7 %copy-start.1 = (s32[4,7]{1,0:T(4,128)S(1)}, s32[4,7]{1,0:T(4,128)}, u32[]{:S(2)}) copy-start(s32[4,7]{1,0:T(4,128)} %param.9) | copy-start | bytes 340
  6.5 46.9 %all-gather.2.cloned.1.call-start = ((), (), s32[]{:S(2)}) async-start(), calls=%async_computation | async-start | bytes 3784704 | tf_op jit(solution)/shard_map/all_gather | solution.py:107
  56.0 14.2 %collective-permute-start = (f32[610,384]{1,0:T(8,128)}, f32[610,384]{1,0:T(8,128)S(1)}, u32[]{:S(2)}, u32[]{:S(2)}) collective-permute-start(f32[610,384]{1,0:T(8,128)} %get-tuple-element.308), channel_id=1, source_target_pairs={{0,2},{2,4},{4,6},{6,8},{8,10},{10,12},{12,14},{14,16},{16,18},{18... | collective-permute-start | bytes 2810888 | tf_op jit(solution)/shard_map/ppermute | solution.py:17
  59.2 18.9 %collective-permute-start.1 = (f32[610,384]{1,0:T(8,128)S(1)}, f32[610,384]{1,0:T(8,128)S(1)}, u32[]{:S(2)}, u32[]{:S(2)}) collective-permute-start(f32[610,384]{1,0:T(8,128)S(1)} %get-tuple-element.309), channel_id=1, source_target_pairs={{2,0},{4,2},{6,4},{8,6},{10,8},{12,10},{14,12},{16,14},{18,16},{20... | collective-permute-start | bytes 2810888 | tf_op jit(solution)/shard_map/ppermute | solution.py:20
  844.7 1.0 copy-start
Sparse Core Ops, SparseCore 0:
  9.2 44.2 all-gather.1
where the time goes:
time: 856 us; the launch traced here: 852 us
  other arithmetic  567 us (66%)
  local copies, waits for them, and re-layouts  147 us (17%)
  waiting for transfers between devices  61.7 us (7%)
  matrix products  37.5 us (4%)
  loops' own time  21.6 us (3%)
  between operations  14.1 us (2%)
    reduce_sum x7, other arithmetic, tile_ops(): jnp.sum(ell_imag, 0)  265 us
    reduce_sum x7, other arithmetic, tile_ops(): jnp.sum(kay_imag, 0)  265 us
    gather x224, local copies, waits for them, and re-layouts  133 us
    all_gather x1, waiting for transfers between devices, body(): cluster_cols = lax.all_gather(stacked_local, 'narrow', axis=1, tiled=True)  44.4 us
    dot_general x7, matrix products, apply_tile(): jnp.einsum('mij,cj->mci', operators, flowing, precision=lax.Precision.HIG...  37.5 us
    another operation x1, loops' own time, body(): lax.fori_loop(0, (count + batch_tiles - 1) // batch_tiles, group_step, re...  20.3 us
    dynamic_update_slice x28, other arithmetic, add_into(): lax.dynamic_update_slice_in_dim(result, segment + term, test_block * bloc...  19.5 us
  transfers between devices with their start and end apart: 3, of which 3 were waited for; matrix products, arithmetic and copies ran while one was open for 0% of the time, Pallas kernels for 0%

commit v1 on v0

v1 whole, which is shorter than its diff:
```python
import functools
import itertools
import math

import jax
import jax.numpy as jnp
from jax import lax
from jax.experimental import pallas as pl
from jax.experimental.pallas import tpu as pltpu
from jax.sharding import PartitionSpec as P

F32 = jnp.float32
BF16 = jnp.bfloat16
BLK = 128
QP = 14
REACH = 3
SPAN = 7
TPB = 4
GROWS = 98
NRHS = 128
SOFTEN = 0.04

Z_MAX = 14.0
DEGREE = 4
COS_HALF = (2.828426289053651, -0.35355064760758376, 0.007364148070439611, -6.107114702262049e-05, 2.4846120790492805e-07)
SIN_HALF = (1.4142135239177973, -0.05892543897495882, 0.0007364984722676873, -4.370137027858996e-06, 1.4053654408325383e-08)

TERMS = []
for _total in range(DEGREE + 1):
    for _j in range(_total + 1):
        _l = _total - _j
        for _a in itertools.product(range(_l + 1), repeat=3):
            if sum(_a) == _l:
                TERMS.append((_j, _a))
NTERM = 72
assert len(TERMS) <= NTERM
ONE = TERMS.index((0, (0, 0, 0)))
LIN = [TERMS.index((0, tuple(int(c == k) for c in range(3)))) for k in range(3)]
SQR = TERMS.index((1, (0, 0, 0)))
KDIM = 256
NOUT = 7
JC = 16
NCH = BLK // JC
MROWS = JC * QP


def powers_of(vec):
    one = None
    table = {(0, 0, 0): one}
    for total in range(1, DEGREE + 1):
        for a in itertools.product(range(total + 1), repeat=3):
            if sum(a) != total:
                continue
            axis = next(c for c in range(3) if a[c] > 0)
            prev = tuple(a[c] - (c == axis) for c in range(3))
            table[a] = vec[axis] if table[prev] is None else table[prev] * vec[axis]
    return table


def split2(value):
    high = value.astype(BF16).astype(F32)
    return high, value - high


def source_features(stage, fts, sf, centre, y):
    mono = powers_of(y)
    square = y[0] * y[0] + y[1] * y[1] + y[2] * y[2]
    sq = [None, square, square * square]
    sq.append(sq[2] * square)
    sq.append(sq[2] * sq[2])
    ones = jnp.ones_like(square)

    def put(row, value):
        fts[row * 16 : row * 16 + QP, :] = value

    for k, (j, a) in enumerate(TERMS):
        const = (-2.0) ** sum(a) / (math.prod(math.factorial(v) for v in a) * math.factorial(j))
        value = mono[a]
        if sq[j] is not None:
            value = sq[j] if value is None else value * sq[j]
        if value is None:
            value = ones
        put(k, value * const if const != 1.0 else value)
    base = NTERM
    s = [stage[(3 + c) * QP : (4 + c) * QP, :] for c in range(3)]
    d = stage[6 * QP : 7 * QP, :]
    for c in range(3):
        put(base + c, s[c])
    put(base + 3, d)
    for c in range(3):
        c1, c2 = (c + 1) % 3, (c + 2) % 3
        put(base + 4 + c, y[c1] * s[c2] - y[c2] * s[c1])
    extra = base + 8
    for half in range(2):
        for c in range(3):
            put(extra + 4 * half + c, y[c] * -2.0)
        put(extra + 4 * half + 3, square)
    rows = lax.broadcasted_iota(jnp.int32, (8, BLK), 0)
    for q in range(QP):
        main = fts[pl.ds(q, NTERM, stride=16), :]
        bil = fts[pl.ds(base * 16 + q, 8, stride=16), :]
        ext = fts[pl.ds(extra * 16 + q, 8, stride=16), :]
        mh, ml = split2(main)
        bh, bl = split2(bil)
        eh, rest = split2(ext)
        em, el = split2(rest)
        zrow = jnp.where(rows < 4, em, eh)
        zrow2 = jnp.where(rows < 4, el, jnp.where(rows == 4, 1.0, 0.0))
        full = jnp.concatenate([mh, mh, ml, bh, bh, bl, zrow, zrow2], 0)
        turned = full.T.astype(BF16)
        for ch in range(NCH):
            sf[ch * MROWS + q * JC : ch * MROWS + (q + 1) * JC, :] = turned[ch * JC : (ch + 1) * JC, :]


def horner(coefs, m, w):
    der = [coefs[k] * math.factorial(k) / math.factorial(k - m) for k in range(m, len(coefs))]
    value = None
    for c in reversed(der):
        value = c if value is None else value * w + c
    return value


OFF_C, OFF_S, OFF_Z = 0, NTERM, 2 * NTERM
OFF_B = 3 * NTERM
OFF_E = OFF_B + 32
TROWS = OFF_E + 16


def test_features(xt, ftt, centre):
    x = [xt[c] - centre[c] for c in range(3)]
    t = [xt[3 + c] for c in range(3)]
    e = xt[6]
    w = x[0] * x[0] + x[1] * x[1] + x[2] * x[2] + SOFTEN
    mono = powers_of(x)

    def put(row, value):
        ftt[row * 8 : row * 8 + 8, :] = value

    for off, coefs in ((OFF_C, COS_HALF), (OFF_S, SIN_HALF)):
        der = [horner(coefs, m, w) for m in range(DEGREE + 1)]
        for k, (j, a) in enumerate(TERMS):
            level = der[j + sum(a)]
            value = level if mono[a] is None else mono[a] * level
            put(off + k, jnp.broadcast_to(value, w.shape))
    put(OFF_Z + ONE, w)
    put(OFF_Z + SQR, jnp.ones_like(w))
    for c in range(3):
        put(OFF_Z + LIN[c], x[c])
    charge = e * -0.25
    for c in range(3):
        put(OFF_B + c, t[c])
        put(OFF_B + 8 + c, t[c] * -2.0)
        put(OFF_B + 16 + c, t[c] * 1.5)
        c1, c2 = (c + 1) % 3, (c + 2) % 3
        put(OFF_B + 24 + c, (t[c1] * x[c2] - t[c2] * x[c1]) * -0.25)
        put(OFF_B + 28 + c, t[c] * 0.25)
    put(OFF_B + 3, charge)
    put(OFF_B + 11, charge)
    for half in range(2):
        for c in range(3):
            put(OFF_E + 4 * half + c, x[c])
        put(OFF_E + 4 * half + 3, jnp.ones_like(w))
    for c in range(4):
        put(OFF_E + 8 + c, x[c] if c < 3 else jnp.ones_like(w))
    put(OFF_E + 12, w)


def test_matrix(ftt, tf, b):
    rows = lax.broadcasted_iota(jnp.int32, (8, BLK), 0)
    zero8 = jnp.zeros((8, BLK), F32)
    for a in range(2):
        ba = 2 * b + a

        def take(off, n):
            return ftt[pl.ds(off * 8 + ba, n, stride=8), :]

        for out, off in ((0, OFF_Z), (1, OFF_C), (2, OFF_S)):
            high, low = split2(take(off, NTERM))
            lanes = slice(out * 256 + a * BLK, out * 256 + (a + 1) * BLK)
            tf[0:224, lanes] = jnp.concatenate([high, low, high, zero8], 0).astype(BF16)
        eh, rest = split2(take(OFF_E, 8))
        em, el = split2(rest)
        fh, rest2 = split2(take(OFF_E + 8, 8))
        fm, fl = split2(rest2)
        first = jnp.where(rows < 4, em, el)
        second = jnp.where(rows < 4, fh, jnp.where(rows == 4, fl, 0.0))
        tf[240:256, a * BLK : (a + 1) * BLK] = jnp.concatenate([first, second], 0).astype(BF16)
        for m in range(4):
            high, low = split2(take(OFF_B + 8 * m, 8))
            out = 3 + m
            lanes = slice(out * 256 + a * BLK, out * 256 + (a + 1) * BLK)
            tf[208:240, lanes] = jnp.concatenate([zero8, high, low, high], 0).astype(BF16)


EXP_RATE = -3.0 / math.log(2.0)


def pair_terms(z, cos_h, sin_h, k1, k2, k6, kk):
    inv = lax.rsqrt(z)
    dist = z * inv
    s0 = sin_h * dist
    c = 4.0 - s0 * s0
    s = s0 * cos_h
    c2 = c * c - 8.0
    s2 = c * s
    decay = jnp.exp2(dist * EXP_RATE)
    p = decay * c
    q = decay * s
    half = inv * 0.5
    c2r = c2 * half
    s2r = s2 * half
    pr = p * inv
    qr = q * inv
    weight = kk * (inv * inv)
    l1r = k1 * c2r
    l1i = k1 * s2r
    l2r = k2 * pr - k6 * qr
    l2i = k2 * qr + k6 * pr
    kr = weight * (((c2r + pr) + (s2 + 3.0 * p)) + q)
    ki = weight * (((s2r + qr) + (3.0 * q - c2)) - p)
    return l1r, l1i, l2r, l2i, kr, ki


def chunk_sums(buf, ops, chunk):
    for g in range(JC // 8):
        acc = None
        for q in range(QP):
            for a in range(2):
                row = q * JC + g * 8
                vals = [buf[row : row + 8, o * 256 + a * BLK : o * 256 + (a + 1) * BLK] for o in range(NOUT)]
                terms = pair_terms(*vals)
                acc = list(terms) if acc is None else [u + v for u, v in zip(acc, terms)]
        start = pl.multiple_of(chunk * JC + g * 8, 8)
        for m in range(6):
            ops[m, pl.ds(start, 8), :] = acc[m]


def fast_tile(ftt, tf, sf, bufs, ops, b):
    test_matrix(ftt, tf, b)

    def product(chunk, buf):
        rows = pl.ds(pl.multiple_of(chunk * MROWS, 16), MROWS)
        buf[...] = jnp.dot(sf[rows, :], tf[...], preferred_element_type=F32)

    product(0, bufs[0])

    def step(n, carry):
        product(2 * n + 1, bufs[1])
        chunk_sums(bufs[0], ops, 2 * n)
        product((2 * n + 2) % NCH, bufs[0])
        chunk_sums(bufs[1], ops, 2 * n + 1)
        return carry

    lax.fori_loop(0, NCH // 2, step, 0)


def direct_tile(stage, raw, xt, ops, b):
    for c in range(7):
        raw[c * 16 : c * 16 + QP, :] = stage[c * QP : (c + 1) * QP, :]
    raw[7 * 16 : 8 * 16, :] = jnp.zeros((16, BLK), F32)
    for m in range(6):
        ops[m] = jnp.zeros((BLK, BLK), F32)

    def point(q, carry):
        rows8 = raw[pl.ds(q, 8, stride=16), :]
        turned = jnp.concatenate([rows8, jnp.zeros((BLK - 8, BLK), F32)], 0).T
        src = [turned[:, c : c + 1] for c in range(7)]

        def centroid(a, carry2):
            tst = [xt[c, pl.ds(2 * b + a, 1), :] for c in range(7)]
            dl = [tst[c] - src[c] for c in range(3)]
            dist = jnp.sqrt(dl[0] * dl[0] + dl[1] * dl[1] + dl[2] * dl[2] + SOFTEN)
            dotted = tst[3] * src[3] + tst[4] * src[4] + tst[5] * src[5]
            charge = tst[6] * src[6]
            crossed = (
                dl[0] * (src[4] * tst[5] - src[5] * tst[4])
                + dl[1] * (src[5] * tst[3] - src[3] * tst[5])
                + dl[2] * (src[3] * tst[4] - src[4] * tst[3])
            )
            scaled = crossed / (dist * dist)
            kr = ki = None
            for m, (wr, wi) in enumerate(((2.0, 0.0), (1.0, 3.0))):
                decay = jnp.exp(-wi * dist) / dist
                gr = decay * jnp.cos(wr * dist)
                gi = decay * jnp.sin(wr * dist)
                cr = (wr * wr - wi * wi) * dotted - charge
                ci = 2.0 * wr * wi * dotted
                ops[2 * m] += cr * gr - ci * gi
                ops[2 * m + 1] += cr * gi + ci * gr
                fr = -wi * dist - 1.0
                fi = wr * dist
                ops[4] += scaled * (fr * gr - fi * gi)
                ops[5] += scaled * (fr * gi + fi * gr)
            return carry2

        return lax.fori_loop(0, 2, centroid, carry)

    lax.fori_loop(0, QP, point, 0)


def apply_operators(ops, xs, wh, wl, acc, b):
    def put(ref, value, places):
        neg = -value
        for row, col, sign in places:
            ref[row * BLK : (row + 1) * BLK, col * BLK : (col + 1) * BLK] = value if sign > 0 else neg

    def both(value, places):
        high = value.astype(BF16)
        low = (value - high.astype(F32)).astype(BF16)
        put(wh, high, places)
        put(wl, low, places)

    l1r, l1i, l2r, l2i = (ops[m] for m in range(4))
    both(l1r + l2r, ((0, 0, 1), (1, 1, 1)))
    both(l1i + l2i, ((0, 1, 1), (1, 0, -1)))
    both(l1r + 0.5 * l2r, ((2, 2, 1), (3, 3, 1)))
    both(l1i + 0.5 * l2i, ((2, 3, 1), (3, 2, -1)))
    both(ops[4], ((0, 2, 1), (1, 3, 1), (2, 0, -1), (3, 1, -1)))
    both(ops[5], ((0, 3, 1), (1, 2, -1), (2, 1, -1), (3, 0, 1)))
    first = jnp.dot(xs[...], wh[...], preferred_element_type=F32)
    second = jnp.dot(xs[0:BLK, :], wl[...], preferred_element_type=F32)
    acc[b] += first[0:BLK] + first[BLK:] + second


def near_kernel(groups, with_base, *refs):
    mask, test = refs[0], refs[1]
    pos = 2
    sources = []
    for _ in groups:
        sources.append((refs[pos], refs[pos + 1]))
        pos += 2
    base = None
    if with_base:
        base = refs[pos]
        pos += 1
    out = refs[pos]
    stage, xt, fts, ftt, tf, sf, buf0, buf1, ops, xs, wh, wl, acc, raw, flags = refs[pos + 1 :]

    tf[...] = jnp.zeros_like(tf)
    ftt[...] = jnp.zeros_like(ftt)
    fts[...] = jnp.zeros_like(fts)
    for c in range(7):
        for b in range(TPB):
            xt[c, 2 * b : 2 * b + 2, :] = test[2 * c : 2 * c + 2, b * BLK : (b + 1) * BLK]
    for b in range(TPB):
        for g in range(4):
            if base is None:
                acc[b, :, g * BLK : (g + 1) * BLK] = jnp.zeros((BLK, BLK), F32)
            else:
                acc[b, :, g * BLK : (g + 1) * BLK] = base[g * NRHS : (g + 1) * NRHS, b * BLK : (b + 1) * BLK]

    total = sum(count for count, _ in groups)

    def source(n, carry):
        rel = jnp.int32(0)
        seen = 0
        for count, begin in groups:
            rel = jnp.where(n >= seen, n - seen + begin, rel)
            seen += count

        def wanted(b):
            column = rel - b + REACH
            inside = (column >= 0) & (column < SPAN)
            return inside & (mask[b, jnp.clip(column, 0, SPAN - 1)] > 0)

        any_wanted = wanted(0)
        for b in range(1, TPB):
            any_wanted = any_wanted | wanted(b)

        @pl.when(any_wanted)
        def _():
            seen = 0
            for (count, begin), (pan, cur) in zip(groups, sources):

                def load(seen=seen, pan=pan, cur=cur):
                    lanes = pl.ds(pl.multiple_of((n - seen) * BLK, BLK), BLK)
                    stage[...] = pan[:, lanes]
                    for g in range(4):
                        value = cur[g * NRHS : (g + 1) * NRHS, lanes]
                        high = value.astype(BF16)
                        xs[0:BLK, g * BLK : (g + 1) * BLK] = high
                        xs[BLK : 2 * BLK, g * BLK : (g + 1) * BLK] = (value - high.astype(F32)).astype(BF16)

                if len(groups) == 1:
                    load()
                else:
                    pl.when((n >= seen) & (n < seen + count))(load)
                seen += count

            place = [stage[c * QP : (c + 1) * QP, :] for c in range(3)]
            low = [jnp.min(jnp.min(v, 0, keepdims=True), 1, keepdims=True) for v in place]
            high = [jnp.max(jnp.max(v, 0, keepdims=True), 1, keepdims=True) for v in place]
            centre = [(u + v) * 0.5 for u, v in zip(low, high)]
            bound = jnp.full((8, BLK), SOFTEN, F32)
            for c in range(3):
                far = jnp.maximum(jnp.abs(xt[c] - low[c]), jnp.abs(xt[c] - high[c]))
                bound = bound + far * far
            for b in range(TPB):
                flags[b] = (jnp.max(bound[2 * b : 2 * b + 2]) <= Z_MAX).astype(jnp.int32)
            source_features(stage, fts, sf, centre, [place[c] - centre[c] for c in range(3)])
            test_features(xt, ftt, centre)

            def tile(b, carry2):
                @pl.when(wanted(b))
                def _():
                    @pl.when(flags[b] > 0)
                    def _():
                        fast_tile(ftt, tf, sf, (buf0, buf1), ops, b)

                    @pl.when(flags[b] == 0)
                    def _():
                        direct_tile(stage, raw, xt, ops, b)

                    apply_operators(ops, xs, wh, wl, acc, b)

                return carry2

            lax.fori_loop(0, TPB, tile, 0)

        return carry

    lax.fori_loop(0, total, source, 0)
    for b in range(TPB):
        for g in range(4):
            out[g * NRHS : (g + 1) * NRHS, b * BLK : (b + 1) * BLK] = acc[b, :, g * BLK : (g + 1) * BLK]


def near_call(mask, test, sources, begins, base=None):
    groups = tuple((cur.shape[1] // BLK, begin) for (_, cur), begin in zip(sources, begins))
    operands = [mask, test]
    for pan, cur in sources:
        operands += [pan, cur]
    if base is not None:
        operands.append(base)
    vmem = pl.BlockSpec(memory_space=pltpu.VMEM)
    return pl.pallas_call(
        functools.partial(near_kernel, groups, base is not None),
        out_shape=jax.ShapeDtypeStruct((4 * NRHS, TPB * BLK), F32),
        in_specs=[pl.BlockSpec(memory_space=pltpu.SMEM)] + [vmem] * (len(operands) - 1),
        out_specs=vmem,
        scratch_shapes=[
            pltpu.VMEM((GROWS, BLK), F32),
            pltpu.VMEM((7, 8, BLK), F32),
            pltpu.VMEM(((NTERM + 16) * 16, BLK), F32),
            pltpu.VMEM((TROWS * 8, BLK), F32),
            pltpu.VMEM((KDIM, NOUT * 256), BF16),
            pltpu.VMEM((NCH * MROWS, KDIM), BF16),
            pltpu.VMEM((MROWS, NOUT * 256), F32),
            pltpu.VMEM((MROWS, NOUT * 256), F32),
            pltpu.VMEM((6, BLK, BLK), F32),
            pltpu.VMEM((2 * BLK, 4 * BLK), BF16),
            pltpu.VMEM((4 * BLK, 4 * BLK), BF16),
            pltpu.VMEM((4 * BLK, 4 * BLK), BF16),
            pltpu.VMEM((TPB, BLK, 4 * BLK), F32),
            pltpu.VMEM((8 * 16, BLK), F32),
            pltpu.SMEM((TPB,), jnp.int32),
        ],
        compiler_params=pltpu.CompilerParams(vmem_limit_bytes=48 * 1024 * 1024),
        cost_estimate=pl.CostEstimate(flops=2 * 10**10, bytes_accessed=4 * 10**6, transcendentals=0),
    )(*operands)


def body(panels, test_points, currents, near_mask):
    count = lax.axis_size("cluster") * lax.axis_size("narrow")
    axes = ("cluster", "narrow")
    forward = [(i, (i + 1) % count) for i in range(count)]
    backward = [(target, source) for source, target in forward]
    width = REACH * BLK
    size = panels.shape[1]
    lows = [lax.ppermute(v[:, size - width :], axes, forward) for v in (panels, currents)]
    highs = [lax.ppermute(v[:, :width], axes, backward) for v in (panels, currents)]
    own = near_call(near_mask, test_points, [(panels, currents)], (0,))
    return near_call(near_mask, test_points, [tuple(lows), tuple(highs)], (-REACH, TPB), own)


def solution(mesh):
    return jax.shard_map(
        body,
        mesh=mesh,
        in_specs=(
            P(None, ("cluster", "narrow")),
            P(None, ("cluster", "narrow")),
            P(None, ("cluster", "narrow")),
            P(("cluster", "narrow"), None),
        ),
        out_specs=P(None, ("cluster", "narrow")),
        check_vma=False,
    )
```

time: 856 us -> 164 us (0.19)
  the two profiles are of different devices: /device:TPU:125 before, /device:TPU:5 now
where the time goes in v1:
time: 164 us; the launch traced here: 162 us
  Pallas kernels  156 us (95%)
  starting transfers between devices  3.73 us (2%)
  local copies, waits for them, and re-layouts  2.6 us (2%)
    pallas_call x2, Pallas kernels, near_call(): pl.pallas_call(functools.partial(near_kernel, groups, base is not None),...  156 us
    ppermute x2, starting transfers between devices, body(): lax.ppermute(v[:, :width], axes, backward)  3.32 us
  transfers between devices with their start and end apart: 4, of which 0 were waited for; matrix products, arithmetic and copies ran while one was open for 1% of the time, Pallas kernels for 54%

profile of v1, /device:TPU:5, one launch (start us, length us, event | category | flops | bytes accessed | tf_op | source)
XLA Modules:
  0.0 162.1 jit_solution(5115450323051293095)
XLA Ops:
  0.0 1.0 fusion.1
  1.0 1.6 collective-permute-start.2
  2.6 0.0 copy-start
  2.6 0.0 copy-start.1
  2.6 0.0 copy-start.2
  2.6 0.0 collective-permute-start
  2.6 1.6 fusion
  4.2 0.0 copy-start.3
  4.2 1.7 %collective-permute-start.3 = (f32[512,384]{1,0:T(8,128)S(1)}, f32[512,384]{1,0:T(8,128)S(1)}, u32[]{:S(2)}, u32[]{:S(2)}) collective-permute-start(f32[512,384]{1,0:T(8,128)S(1)} %get-tuple-element.5), channel_id=1, source_target_pairs={{1,0},{2,1},{3,2},{4,3},{5,4},{6,5},{7,6},{8,7},{9,8},{10,9},{11,1... | collective-permute-start | bytes 2359304 | tf_op jit(solution)/shard_map/ppermute | solution.py:471
  5.9 0.4 collective-permute-start.1
  6.3 0.0 copy-done
  6.3 0.0 copy-done.1
  6.4 0.0 copy-done.2
  6.4 0.0 copy-done.3
  6.4 87.0 %shard_map.46.refs_6_ = f32[512,512]{1,0:T(8,128)S(1)} custom-call(s32[4,7]{1,0:T(4,128)S(1)} %copy-done.3, f32[14,512]{1,0:T(8,128)S(1)} %copy-done.2, f32[98,512]{1,0:T(8,128)S(1)} %copy-done.1, f32[512,512]{1,0:T(8,128)S(1)} %copy-done), custom_call_target="tpu_custom_call" | custom-call | flops 20000000000 | bytes 4000000 | tf_op jit(solution)/shard_map/pallas_call | solution.py:436
  93.4 0.0 collective-permute-done.2.refs_4_
  93.4 0.0 collective-permute-done.refs_2_
  93.4 0.0 collective-permute-done.3.refs_5_
  93.4 0.0 collective-permute-done.1.refs_3_
  93.4 68.7 %shard_map.47 = f32[512,512]{1,0:T(8,128)} custom-call(s32[4,7]{1,0:T(4,128)S(1)} %copy-done.3, f32[14,512]{1,0:T(8,128)S(1)} %copy-done.2, f32[98,384]{1,0:T(8,128)S(1)} %collective-permute-done.refs_2_, f32[512,384]{1,0:T(8,128)S(1)} %collective-permute-done.1.refs_3_, f32[98,384]{1,0:T(8,128)S(1)} %collective-permute-done.2.refs_4_, ...), custom_call_target="tpu_custom_call" | custom-call | flops 20000000000 | bytes 4000000 | tf_op jit(solution)/shard_map/pallas_call | solution.py:436
Async XLA Ops:
  1.0 92.3 %collective-permute-start.2 = (f32[98,384]{1,0:T(8,128)S(1)}, f32[98,384]{1,0:T(8,128)S(1)}, u32[]{:S(2)}, u32[]{:S(2)}) collective-permute-start(f32[98,384]{1,0:T(8,128)S(1)} %get-tuple-element.7), channel_id=1, source_target_pairs={{1,0},{2,1},{3,2},{4,3},{5,4},{6,5},{7,6},{8,7},{9,8},{10,9},{11,1... | collective-permute-start | bytes 451592 | tf_op jit(solution)/shard_map/ppermute | solution.py:471
  2.6 3.7 %copy-start = (f32[512,512]{1,0:T(8,128)S(1)}, f32[512,512]{1,0:T(8,128)}, u32[]{:S(2)}) copy-start(f32[512,512]{1,0:T(8,128)} %refs_3_.1) | copy-start | bytes 3145732
  2.6 3.7 %copy-start.1 = (f32[98,512]{1,0:T(8,128)S(1)}, f32[98,512]{1,0:T(8,128)}, u32[]{:S(2)}) copy-start(f32[98,512]{1,0:T(8,128)} %refs_2_.1) | copy-start | bytes 602116
  2.6 3.7 %copy-start.2 = (f32[14,512]{1,0:T(8,128)S(1)}, f32[14,512]{1,0:T(8,128)}, u32[]{:S(2)}) copy-start(f32[14,512]{1,0:T(8,128)} %refs_1_.3) | copy-start | bytes 86020
  2.6 90.8 %collective-permute-start = (f32[98,384]{1,0:T(8,128)S(1)}, f32[98,384]{1,0:T(8,128)S(1)}, u32[]{:S(2)}, u32[]{:S(2)}) collective-permute-start(f32[98,384]{1,0:T(8,128)S(1)} %get-tuple-element.8), channel_id=1, source_target_pairs={{0,1},{1,2},{2,3},{3,4},{4,5},{5,6},{6,7},{7,8},{8,9},{9,10},{10,1... | collective-permute-start | bytes 451592 | tf_op jit(solution)/shard_map/ppermute | solution.py:470
  4.2 2.2 %copy-start.3 = (s32[4,7]{1,0:T(4,128)S(1)}, s32[4,7]{1,0:T(4,128)}, u32[]{:S(2)}) copy-start(s32[4,7]{1,0:T(4,128)} %refs_0_.3) | copy-start | bytes 340
  4.2 89.2 %collective-permute-start.3 = (f32[512,384]{1,0:T(8,128)S(1)}, f32[512,384]{1,0:T(8,128)S(1)}, u32[]{:S(2)}, u32[]{:S(2)}) collective-permute-start(f32[512,384]{1,0:T(8,128)S(1)} %get-tuple-element.5), channel_id=1, source_target_pairs={{1,0},{2,1},{3,2},{4,3},{5,4},{6,5},{7,6},{8,7},{9,8},{10,9},{11,1... | collective-permute-start | bytes 2359304 | tf_op jit(solution)/shard_map/ppermute | solution.py:471
  5.9 87.5 %collective-permute-start.1 = (f32[512,384]{1,0:T(8,128)S(1)}, f32[512,384]{1,0:T(8,128)S(1)}, u32[]{:S(2)}, u32[]{:S(2)}) collective-permute-start(f32[512,384]{1,0:T(8,128)S(1)} %get-tuple-element.6), channel_id=1, source_target_pairs={{0,1},{1,2},{2,3},{3,4},{4,5},{5,6},{6,7},{7,8},{8,9},{9,10},{10,1... | collective-permute-start | bytes 2359304 | tf_op jit(solution)/shard_map/ppermute | solution.py:470

commit v2 on v1

--- a/solution.py
+++ b/solution.py
@@ -322,86 +322,88 @@
     acc[b] += first[0:BLK] + first[BLK:] + second
 
 
-def near_kernel(groups, with_base, *refs):
-    mask, test = refs[0], refs[1]
-    pos = 2
-    sources = []
-    for _ in groups:
-        sources.append((refs[pos], refs[pos + 1]))
-        pos += 2
-    base = None
-    if with_base:
-        base = refs[pos]
-        pos += 1
-    out = refs[pos]
-    stage, xt, fts, ftt, tf, sf, buf0, buf1, ops, xs, wh, wl, acc, raw, flags = refs[pos + 1 :]
-
-    tf[...] = jnp.zeros_like(tf)
-    ftt[...] = jnp.zeros_like(ftt)
-    fts[...] = jnp.zeros_like(fts)
-    for c in range(7):
-        for b in range(TPB):
-            xt[c, 2 * b : 2 * b + 2, :] = test[2 * c : 2 * c + 2, b * BLK : (b + 1) * BLK]
+CROW = 104
+XROW = CROW + 4 * NRHS
+OUTER_ROWS = XROW + 64 + 8
+FAR_ROWS = XROW + 32 + 8
+MATE_ROWS = XROW
+FULL = TPB * SPAN
+
+
+def is_even():
+    return lax.axis_index("narrow") == 0
+
+
+def mirrored(even, block):
+    return jnp.where(even, block, TPB - 1 - block)
+
+
+def load_of(mask):
+    total = mask[0, 0]
     for b in range(TPB):
-        for g in range(4):
-            if base is None:
-                acc[b, :, g * BLK : (g + 1) * BLK] = jnp.zeros((BLK, BLK), F32)
-            else:
-                acc[b, :, g * BLK : (g + 1) * BLK] = base[g * NRHS : (g + 1) * NRHS, b * BLK : (b + 1) * BLK]
-
-    total = sum(count for count, _ in groups)
+        for c in range(SPAN):
+            if b or c:
+                total = total + mask[b, c]
+    return total
+
+
+def number(ref, row):
+    return jnp.max(ref[row : row + 8, 0:BLK]).astype(jnp.int32)
+
+
+def shares(load_near, load_far):
+    goal = lax.div(FULL + load_near + load_far + 1, 3)
+    return jnp.clip(goal - load_near, 6, 9), jnp.clip(goal - load_far, 0, 8)
+
+
+def pack_kernel(mask, panels, test, currents, mate, outer, far, load):
+    even = is_even()
+    for ref, count, begin in (
+        (mate, 3, jnp.where(even, BLK, 0)),
+        (outer, 1, jnp.where(even, 0, 3 * BLK)),
+        (far, 2, jnp.where(even, 2 * BLK, 0)),
+    ):
+        lanes = pl.ds(pl.multiple_of(begin, BLK), count * BLK)
+        ref[0:GROWS, :] = panels[:, lanes]
+        ref[CROW:XROW, :] = currents[:, lanes]
+    value = load_of(mask).astype(F32)
+    for b in range(TPB):
+        points = test[:, b * BLK : (b + 1) * BLK]
+        outer[XROW + 16 * b : XROW + 16 * b + 14, :] = points
+        row = XROW + 16 * (b // 2)
+        far[row : row + 14, (b % 2) * BLK : (b % 2 + 1) * BLK] = points
+    outer[XROW + 64 : XROW + 72, :] = jnp.full((8, BLK), value, F32)
+    far[XROW + 32 : XROW + 40, :] = jnp.full((8, 2 * BLK), value, F32)
+    load[...] = jnp.full((8, BLK), value, F32)
+
+
+def engine(scratch, steps, wanted, load_source, accset):
+    stage, xt, fts, ftt, tf, sf, buf0, buf1, ops, xs, wh, wl, acc, raw, flags = scratch
 
     def source(n, carry):
-        rel = jnp.int32(0)
-        seen = 0
-        for count, begin in groups:
-            rel = jnp.where(n >= seen, n - seen + begin, rel)
-            seen += count
-
-        def wanted(b):
-            column = rel - b + REACH
-            inside = (column >= 0) & (column < SPAN)
-            return inside & (mask[b, jnp.clip(column, 0, SPAN - 1)] > 0)
-
-        any_wanted = wanted(0)
+        any_wanted = wanted(n, 0)
         for b in range(1, TPB):
-            any_wanted = any_wanted | wanted(b)
+            any_wanted = any_wanted | wanted(n, b)
 
         @pl.when(any_wanted)
         def _():
-            seen = 0
-            for (count, begin), (pan, cur) in zip(groups, sources):
-
-                def load(seen=seen, pan=pan, cur=cur):
-                    lanes = pl.ds(pl.multiple_of((n - seen) * BLK, BLK), BLK)
-                    stage[...] = pan[:, lanes]
-                    for g in range(4):
-                        value = cur[g * NRHS : (g + 1) * NRHS, lanes]
-                        high = value.astype(BF16)
-                        xs[0:BLK, g * BLK : (g + 1) * BLK] = high
-                        xs[BLK : 2 * BLK, g * BLK : (g + 1) * BLK] = (value - high.astype(F32)).astype(BF16)
-
-                if len(groups) == 1:
-                    load()
-                else:
-                    pl.when((n >= seen) & (n < seen + count))(load)
-                seen += count
-
+            load_source(n)
+            points = xt.at[accset(n)]
             place = [stage[c * QP : (c + 1) * QP, :] for c in range(3)]
             low = [jnp.min(jnp.min(v, 0, keepdims=True), 1, keepdims=True) for v in place]
             high = [jnp.max(jnp.max(v, 0, keepdims=True), 1, keepdims=True) for v in place]
             centre = [(u + v) * 0.5 for u, v in zip(low, high)]
             bound = jnp.full((8, BLK), SOFTEN, F32)
             for c in range(3):
-                far = jnp.maximum(jnp.abs(xt[c] - low[c]), jnp.abs(xt[c] - high[c]))
+                far = jnp.maximum(jnp.abs(points[c] - low[c]), jnp.abs(points[c] - high[c]))
                 bound = bound + far * far
             for b in range(TPB):
                 flags[b] = (jnp.max(bound[2 * b : 2 * b + 2]) <= Z_MAX).astype(jnp.int32)
             source_features(stage, fts, sf, centre, [place[c] - centre[c] for c in range(3)])
-            test_features(xt, ftt, centre)
+            test_features(points, ftt, centre)
 
             def tile(b, carry2):
-                @pl.when(wanted(b))
+                @pl.when(wanted(n, b))
                 def _():
                     @pl.when(flags[b] > 0)
                     def _():
@@ -409,9 +411,9 @@
 
                     @pl.when(flags[b] == 0)
                     def _():
-                        direct_tile(stage, raw, xt, ops, b)
-
-                    apply_operators(ops, xs, wh, wl, acc, b)
+                        direct_tile(stage, raw, points, ops, b)
+
+                    apply_operators(ops, xs, wh, wl, acc, TPB * accset(n) + b)
 
                 return carry2
 
@@ -419,58 +421,220 @@
 
         return carry
 
-    lax.fori_loop(0, total, source, 0)
+    tf[...] = jnp.zeros_like(tf)
+    ftt[...] = jnp.zeros_like(ftt)
+    fts[...] = jnp.zeros_like(fts)
+    lax.fori_loop(0, steps, source, 0)
+
+
+def fill(scratch, pan, cur, row, slot):
+    stage, xs = scratch[0], scratch[9]
+    lanes = pl.ds(pl.multiple_of(slot * BLK, BLK), BLK)
+    stage[...] = pan[0:GROWS, lanes]
+    for g in range(4):
+        value = cur[row + g * NRHS : row + (g + 1) * NRHS, lanes]
+        high = value.astype(BF16)
+        xs[0:BLK, g * BLK : (g + 1) * BLK] = high
+        xs[BLK : 2 * BLK, g * BLK : (g + 1) * BLK] = (value - high.astype(F32)).astype(BF16)
+
+
+def fill_tests(xt, which, blocks):
+    for c in range(7):
+        for b in range(TPB):
+            xt[which, c, 2 * b : 2 * b + 2, :] = blocks(b, 2 * c)
+
+
+def own_tests(test):
+    return lambda b, row: test[row : row + 2, b * BLK : (b + 1) * BLK]
+
+
+def clear(acc, count):
+    for b in range(count):
+        acc[b] = jnp.zeros((BLK, 4 * BLK), F32)
+
+
+def write_out(out, acc, blocks):
+    for col, b in enumerate(blocks):
+        for g in range(4):
+            out[g * NRHS : (g + 1) * NRHS, col * BLK : (col + 1) * BLK] = acc[b, :, g * BLK : (g + 1) * BLK]
+
+
+def first_kernel(mask, test, panels, currents, out, *scratch):
+    even = is_even()
+    full = load_of(mask) == FULL
+    fill_tests(scratch[1], 0, own_tests(test))
+    clear(scratch[12], TPB)
+
+    def wanted(n, b):
+        return (full & (mirrored(even, n) == 1)) | (jnp.logical_not(full) & (n == b))
+
+    engine(scratch, TPB, wanted, lambda n: fill(scratch, panels, currents, 0, n), lambda n: 0)
+    write_out(out, scratch[12], range(TPB))
+
+
+def help_kernel(mask, panels, currents, outer, far, load_mate, after, out_near, out_far, *scratch):
+    even = is_even()
+    odd = jnp.logical_not(even)
+    own, mate = load_of(mask), number(load_mate, 0)
+    near_full = number(outer, XROW + 64) == FULL
+    far_full = number(far, XROW + 32) == FULL
+    share_near, _ = shares(own, mate)
+    _, share_far = shares(mate, own)
+    xt, acc = scratch[1], scratch[12]
+    fill_tests(xt, 0, lambda b, row: outer[XROW + 16 * b + row : XROW + 16 * b + row + 2, :])
+    fill_tests(
+        xt,
+        1,
+        lambda b, row: far[
+            XROW + 16 * (b // 2) + row : XROW + 16 * (b // 2) + row + 2, (b % 2) * BLK : (b % 2 + 1) * BLK
+        ],
+    )
+    clear(acc, 2 * TPB)
+
+    def wanted(n, b):
+        v_near, v_far = mirrored(odd, b), mirrored(even, b)
+        of_own = (n < 3) & (v_near <= 2 - n)
+        of_outer = (n == 3) & (v_near < share_near - 6)
+        of_far = (n > 3) & ((n - 4) * TPB + v_far < share_far)
+        return (near_full & (of_own | of_outer)) | (far_full & of_far)
+
+    def load_source(n):
+        @pl.when(n < 3)
+        def _():
+            fill(scratch, panels, currents, 0, mirrored(even, n))
+
+        @pl.when(n == 3)
+        def _():
+            fill(scratch, outer, outer, CROW, 0)
+
+        @pl.when(n > 3)
+        def _():
+            fill(scratch, far, far, CROW, jnp.where(even, 5 - n, n - 4))
+
+    engine(scratch, 6, wanted, load_source, lambda n: jnp.where(n > 3, 1, 0))
+    shift = jnp.where(even, 1, 0)
+    write_out(out_near, acc, [b + shift for b in range(TPB - 1)])
+    write_out(out_far, acc, range(TPB, 2 * TPB))
+
+
+def rest_kernel(mask, test, panels, currents, outer, mate, load_far, part, after, out, *scratch):
+    even = is_even()
+    full = load_of(mask) == FULL
+    share_near, share_far = shares(number(outer, XROW + 64), number(load_far, 0))
+    acc = scratch[12]
+    fill_tests(scratch[1], 0, own_tests(test))
     for b in range(TPB):
         for g in range(4):
-            out[g * NRHS : (g + 1) * NRHS, b * BLK : (b + 1) * BLK] = acc[b, :, g * BLK : (g + 1) * BLK]
-
-
-def near_call(mask, test, sources, begins, base=None):
-    groups = tuple((cur.shape[1] // BLK, begin) for (_, cur), begin in zip(sources, begins))
-    operands = [mask, test]
-    for pan, cur in sources:
-        operands += [pan, cur]
-    if base is not None:
-        operands.append(base)
+            acc[b, :, g * BLK : (g + 1) * BLK] = part[g * NRHS : (g + 1) * NRHS, b * BLK : (b + 1) * BLK]
+
+    def wanted(n, b):
+        rel = jnp.where(n < 4, n, jnp.where(n == 4, jnp.where(even, -1, 4), jnp.where(even, n - 1, n - 8)))
+        column = rel - b + REACH
+        inside = (column >= 0) & (column < SPAN)
+        sparse = inside & (mask[b, jnp.clip(column, 0, SPAN - 1)] > 0) & (rel != b)
+        u, v = mirrored(even, rel), mirrored(even, b)
+        given = (u == 1) | ((u == 0) & (v < share_near - 6))
+        given = given | ((u == 3) & (v < share_far)) | ((u == 2) & (TPB + v < share_far))
+        dense = inside & (u >= 0) & jnp.logical_not(given)
+        return (full & dense) | (jnp.logical_not(full) & sparse)
+
+    def load_source(n):
+        @pl.when(n < 4)
+        def _():
+            fill(scratch, panels, currents, 0, n)
+
+        @pl.when(n == 4)
+        def _():
+            fill(scratch, outer, outer, CROW, 0)
+
+        @pl.when(n > 4)
+        def _():
+            fill(scratch, mate, mate, CROW, n - 5)
+
+    engine(scratch, 8, wanted, load_source, lambda n: 0)
+    write_out(out, acc, range(TPB))
+
+
+def scratch_for(sets):
+    return [
+        pltpu.VMEM((GROWS, BLK), F32),
+        pltpu.VMEM((sets, 7, 8, BLK), F32),
+        pltpu.VMEM(((NTERM + 16) * 16, BLK), F32),
+        pltpu.VMEM((TROWS * 8, BLK), F32),
+        pltpu.VMEM((KDIM, NOUT * 256), BF16),
+        pltpu.VMEM((NCH * MROWS, KDIM), BF16),
+        pltpu.VMEM((MROWS, NOUT * 256), F32),
+        pltpu.VMEM((MROWS, NOUT * 256), F32),
+        pltpu.VMEM((6, BLK, BLK), F32),
+        pltpu.VMEM((2 * BLK, 4 * BLK), BF16),
+        pltpu.VMEM((4 * BLK, 4 * BLK), BF16),
+        pltpu.VMEM((4 * BLK, 4 * BLK), BF16),
+        pltpu.VMEM((sets * TPB, BLK, 4 * BLK), F32),
+        pltpu.VMEM((8 * 16, BLK), F32),
+        pltpu.SMEM((TPB,), jnp.int32),
+    ]
+
+
+def call(kernel, outs, operands, sets=0, unread=0, tiles=1):
     vmem = pl.BlockSpec(memory_space=pltpu.VMEM)
+    anywhere = pl.BlockSpec(memory_space=pl.ANY)
+    several = len(outs) > 1
+    plain = len(operands) - 1 - unread
     return pl.pallas_call(
-        functools.partial(near_kernel, groups, base is not None),
-        out_shape=jax.ShapeDtypeStruct((4 * NRHS, TPB * BLK), F32),
-        in_specs=[pl.BlockSpec(memory_space=pltpu.SMEM)] + [vmem] * (len(operands) - 1),
-        out_specs=vmem,
-        scratch_shapes=[
-            pltpu.VMEM((GROWS, BLK), F32),
-            pltpu.VMEM((7, 8, BLK), F32),
-            pltpu.VMEM(((NTERM + 16) * 16, BLK), F32),
-            pltpu.VMEM((TROWS * 8, BLK), F32),
-            pltpu.VMEM((KDIM, NOUT * 256), BF16),
-            pltpu.VMEM((NCH * MROWS, KDIM), BF16),
-            pltpu.VMEM((MROWS, NOUT * 256), F32),
-            pltpu.VMEM((MROWS, NOUT * 256), F32),
-            pltpu.VMEM((6, BLK, BLK), F32),
-            pltpu.VMEM((2 * BLK, 4 * BLK), BF16),
-            pltpu.VMEM((4 * BLK, 4 * BLK), BF16),
-            pltpu.VMEM((4 * BLK, 4 * BLK), BF16),
-            pltpu.VMEM((TPB, BLK, 4 * BLK), F32),
-            pltpu.VMEM((8 * 16, BLK), F32),
-            pltpu.SMEM((TPB,), jnp.int32),
-        ],
+        kernel,
+        out_shape=[jax.ShapeDtypeStruct(s, F32) for s in outs] if several else jax.ShapeDtypeStruct(outs[0], F32),
+        in_specs=[pl.BlockSpec(memory_space=pltpu.SMEM)] + [vmem] * plain + [anywhere] * unread,
+        out_specs=[vmem] * len(outs) if several else vmem,
+        scratch_shapes=scratch_for(sets) if sets else [],
         compiler_params=pltpu.CompilerParams(vmem_limit_bytes=48 * 1024 * 1024),
-        cost_estimate=pl.CostEstimate(flops=2 * 10**10, bytes_accessed=4 * 10**6, transcendentals=0),
+        cost_estimate=pl.CostEstimate(flops=tiles * 5 * 10**9, bytes_accessed=4 * 10**6, transcendentals=0),
     )(*operands)
 
 
 def body(panels, test_points, currents, near_mask):
     count = lax.axis_size("cluster") * lax.axis_size("narrow")
     axes = ("cluster", "narrow")
-    forward = [(i, (i + 1) % count) for i in range(count)]
-    backward = [(target, source) for source, target in forward]
-    width = REACH * BLK
-    size = panels.shape[1]
-    lows = [lax.ppermute(v[:, size - width :], axes, forward) for v in (panels, currents)]
-    highs = [lax.ppermute(v[:, :width], axes, backward) for v in (panels, currents)]
-    own = near_call(near_mask, test_points, [(panels, currents)], (0,))
-    return near_call(near_mask, test_points, [tuple(lows), tuple(highs)], (-REACH, TPB), own)
+    swap = [(i, i ^ 1) for i in range(count)]
+    across = [(i, (i - 1) % count if i % 2 == 0 else (i + 1) % count) for i in range(count)]
+    away = [(i, (i - 2) % count if i % 2 == 0 else (i + 2) % count) for i in range(count)]
+    back = [(target, source) for source, target in away]
+    width = TPB * BLK
+    wide = 4 * NRHS
+    mate, outer, far, load = call(
+        pack_kernel,
+        [(MATE_ROWS, 3 * BLK), (OUTER_ROWS, BLK), (FAR_ROWS, 2 * BLK), (8, BLK)],
+        [near_mask, panels, test_points, currents],
+    )
+    load_mate = lax.ppermute(load, axes, swap)
+    load_far = lax.ppermute(load, axes, back)
+    outer = lax.ppermute(outer, axes, across)
+    far = lax.ppermute(far, axes, away)
+    mate = lax.ppermute(mate, axes, swap)
+    part = call(first_kernel, [(wide, width)], [near_mask, test_points, panels, currents], 1, tiles=4)
+    to_near, to_far = call(
+        help_kernel,
+        [(wide, width - BLK), (wide, width)],
+        [near_mask, panels, currents, outer, far, load_mate, part],
+        2,
+        unread=1,
+        tiles=7,
+    )
+    from_near = lax.ppermute(to_near, axes, across)
+    from_far = lax.ppermute(to_far, axes, back)
+    rest = call(
+        rest_kernel,
+        [(wide, width)],
+        [near_mask, test_points, panels, currents, outer, mate, load_far, part, to_near],
+        1,
+        unread=1,
+        tiles=8,
+    )
+    padded = jnp.where(
+        lax.axis_index("narrow") == 0,
+        jnp.pad(from_near, ((0, 0), (0, BLK))),
+        jnp.pad(from_near, ((0, 0), (BLK, 0))),
+    )
+    return rest + from_far + padded
 
 
 def solution(mesh):

time: 164 us -> 157 us (0.957)
  the two profiles are of different devices: /device:TPU:5 before, /device:TPU:81 now
where the time goes in v2:
time: 157 us
  Pallas kernels  93.9 us (60%)
  starting transfers between devices  55.3 us (35%)
  local copies, waits for them, and re-layouts  6.44 us (4%)
    pallas_call x4, Pallas kernels, call(): pl.pallas_call(kernel, out_shape=[jax.ShapeDtypeStruct(s, F32) for s in o...  93.9 us
    ppermute x1, starting transfers between devices, body(): from_near = lax.ppermute(to_near, axes, across)  35 us
    ppermute x1, starting transfers between devices, body(): from_far = lax.ppermute(to_far, axes, back)  13.4 us
    unnamed x22, local copies, waits for them, and re-layouts  6.44 us
    ppermute x1, starting transfers between devices, body(): mate = lax.ppermute(mate, axes, swap)  3.84 us
  transfers between devices with their start and end apart: 7, of which 0 were waited for; matrix products, arithmetic and copies ran while one was open for 0% of the time, Pallas kernels for 59%

profile of v2, /device:TPU:81, one launch (start us, length us, event | category | flops | bytes accessed | tf_op | source)
XLA Modules:
  0.0 157.1 jit_solution(8604187109156172687)
XLA Ops:
  0.0 0.0 copy-start
  0.0 1.2 copy-done
  1.2 0.0 copy-start.2
  1.2 0.9 copy-done.2
  2.2 0.0 copy-start.4
  2.2 0.8 copy-done.4
  2.9 0.0 copy-start.6
  2.9 0.7 copy-done.6
  3.6 1.7 %shard_map.46 = (f32[616,384]{1,0:T(8,128)S(1)}, f32[688,128]{1,0:T(8,128)}, f32[656,256]{1,0:T(8,128)}, f32[8,128]{1,0:T(8,128)S(1)}) custom-call(s32[4,7]{1,0:T(4,128)S(1)} %copy-done.6, f32[98,512]{1,0:T(8,128)S(1)} %copy-done.2, f32[14,512]{1,0:T(8,128)S(1)} %copy-done.4, f32[512,512]{1,0:T(8,128)S(1)} %copy-done), custom_call_target="tpu_custom_call" | custom-call | flops 5000000000 | bytes 4000000 | tf_op jit(solution)/shard_map/pallas_call | solution.py:583
  5.3 1.2 collective-permute-start.4
  6.5 1.8 %collective-permute-start.2 = (f32[8,128]{1,0:T(8,128)S(1)}, f32[8,128]{1,0:T(8,128)S(1)}, u32[]{:S(2)}, u32[]{:S(2)}) collective-permute-start(f32[8,128]{1,0:T(8,128)S(1)} %get-tuple-element.13), channel_id=1, source_target_pairs={{254,0},{3,1},{0,2},{5,3},{2,4},{7,5},{4,6},{9,7},{6,8},{11,9},{8,... | collective-permute-start | bytes 12296 | tf_op jit(solution)/shard_map/ppermute | solution.py:609
  8.3 0.0 collective-permute-start
  8.3 0.0 collective-permute-start.3
  8.3 0.0 copy-start.1
  8.3 0.0 copy-start.3
  8.3 3.8 %collective-permute-start.1 = (f32[616,384]{1,0:T(8,128)S(1)}, f32[616,384]{1,0:T(8,128)S(1)}, u32[]{:S(2)}, u32[]{:S(2)}) collective-permute-start(f32[616,384]{1,0:T(8,128)S(1)} %get-tuple-element.12), channel_id=1, source_target_pairs={{0,1},{1,0},{2,3},{3,2},{4,5},{5,4},{6,7},{7,6},{8,9},{9,8},{10,11... | collective-permute-start | bytes 2838536 | tf_op jit(solution)/shard_map/ppermute | solution.py:612
  12.2 22.5 %shard_map.47.after.part = f32[512,512]{1,0:T(8,128)S(1)} custom-call(s32[4,7]{1,0:T(4,128)S(1)} %copy-done.6, f32[14,512]{1,0:T(8,128)S(1)} %copy-done.4, f32[98,512]{1,0:T(8,128)S(1)} %copy-done.2, f32[512,512]{1,0:T(8,128)S(1)} %copy-done), custom_call_target="tpu_custom_call" | custom-call | flops 20000000000 | bytes 4000000 | tf_op jit(solution)/shard_map/pallas_call | solution.py:583
  34.7 0.0 copy-start.8
  34.7 1.0 copy-done.8
  35.6 0.0 copy-start.7
  35.6 0.0 copy-start.5
  35.6 0.0 collective-permute-done.4.load_mate
  35.6 0.0 collective-permute-done.outer
  35.6 0.0 collective-permute-done.3.far
  35.7 0.0 copy-done.1
  35.7 0.0 copy-done.3
  35.7 0.6 copy-done.7
  36.3 0.0 copy-start.9
  36.3 1.2 copy-done.9
  37.5 0.0 copy-start.10
  37.5 2.0 %shard_map.48 = (f32[512,384]{1,0:T(8,128)S(1)}, f32[512,512]{1,0:T(8,128)S(1)}) custom-call(s32[4,7]{1,0:T(4,128)S(1)} %copy-done.7, f32[98,512]{1,0:T(8,128)S(1)} %copy-done.3, f32[512,512]{1,0:T(8,128)S(1)} %copy-done.1, f32[688,128]{1,0:T(8,128)S(1)} %collective-permute-done.outer, f32[656,256]{1,0:T(8,128)} %collective-permute-done.3.far, ...), custom_call_target="tpu_custom_call" | custom-call | flops 35000000512 | bytes 4000000 | tf_op jit(solution)/shard_map/pallas_call | solution.py:583
  39.5 35.0 %collective-permute-start.6 = (f32[512,384]{1,0:T(8,128)S(1)}, f32[512,384]{1,0:T(8,128)S(1)}, u32[]{:S(2)}, u32[]{:S(2)}) collective-permute-start(f32[512,384]{1,0:T(8,128)S(1)} %get-tuple-element.15.after), channel_id=1, source_target_pairs={{0,255},{1,2},{2,1},{3,4},{4,3},{5,6},{6,5},{7,8},{8,7},{9,10},{10... | collective-permute-start | bytes 2359304 | tf_op jit(solution)/shard_map/ppermute | solution.py:622
  74.6 13.4 %collective-permute-start.5 = (f32[512,512]{1,0:T(8,128)S(1)}, f32[512,512]{1,0:T(8,128)S(1)}, u32[]{:S(2)}, u32[]{:S(2)}) collective-permute-start(f32[512,512]{1,0:T(8,128)S(1)} %get-tuple-element.16), channel_id=1, source_target_pairs={{254,0},{3,1},{0,2},{5,3},{2,4},{7,5},{4,6},{9,7},{6,8},{11,9},{8,... | collective-permute-start | bytes 3145736 | tf_op jit(solution)/shard_map/ppermute | solution.py:623
  88.0 0.0 collective-permute-done.2.load_far
  88.0 0.0 collective-permute-done.1.mate
  88.0 0.0 copy-done.5
  88.0 0.0 copy-done.10
  88.0 67.7 %shard_map.49 = f32[512,512]{1,0:T(8,128)S(1)} custom-call(s32[4,7]{1,0:T(4,128)S(1)} %copy-done.7, f32[14,512]{1,0:T(8,128)S(1)} %copy-done.5, f32[98,512]{1,0:T(8,128)S(1)} %copy-done.3, f32[512,512]{1,0:T(8,128)S(1)} %copy-done.1, f32[688,128]{1,0:T(8,128)S(1)} %collective-permute-done.outer, f32[616,384]{1,0:T(8,128)S(1)} %collective-permute-done.1.mate, ...), custom_call_target="tpu_custom_call" | custom-call | flops 40000000000 | bytes 4000000 | tf_op jit(solution)/shard_map/pallas_call | solution.py:583
  155.7 0.0 collective-permute-done.6
  155.8 0.0 collective-permute-done.5
  155.8 1.3 select_add_fusion
Async XLA Ops:
  0.0 1.2 copy-start
  1.2 0.9 copy-start.2
  2.2 0.8 copy-start.4
  2.9 0.7 copy-start.6
  5.3 30.4 %collective-permute-start.4 = (f32[8,128]{1,0:T(8,128)S(1)}, f32[8,128]{1,0:T(8,128)S(1)}, u32[]{:S(2)}, u32[]{:S(2)}) collective-permute-start(f32[8,128]{1,0:T(8,128)S(1)} %get-tuple-element.13), channel_id=1, source_target_pairs={{0,1},{1,0},{2,3},{3,2},{4,5},{5,4},{6,7},{7,6},{8,9},{9,8},{10,11... | collective-permute-start | bytes 12296 | tf_op jit(solution)/shard_map/ppermute | solution.py:608
  6.5 81.5 %collective-permute-start.2 = (f32[8,128]{1,0:T(8,128)S(1)}, f32[8,128]{1,0:T(8,128)S(1)}, u32[]{:S(2)}, u32[]{:S(2)}) collective-permute-start(f32[8,128]{1,0:T(8,128)S(1)} %get-tuple-element.13), channel_id=1, source_target_pairs={{254,0},{3,1},{0,2},{5,3},{2,4},{7,5},{4,6},{9,7},{6,8},{11,9},{8,... | collective-permute-start | bytes 12296 | tf_op jit(solution)/shard_map/ppermute | solution.py:609
  8.3 27.3 %collective-permute-start = (f32[688,128]{1,0:T(8,128)}, f32[688,128]{1,0:T(8,128)S(1)}, u32[]{:S(2)}, u32[]{:S(2)}) collective-permute-start(f32[688,128]{1,0:T(8,128)} %get-tuple-element.11), channel_id=1, source_target_pairs={{0,255},{1,2},{2,1},{3,4},{4,3},{5,6},{6,5},{7,8},{8,7},{9,10},{10... | collective-permute-start | bytes 1056776 | tf_op jit(solution)/shard_map/ppermute | solution.py:610
  8.3 27.3 %collective-permute-start.3 = (f32[656,256]{1,0:T(8,128)}, f32[656,256]{1,0:T(8,128)}, u32[]{:S(2)}, u32[]{:S(2)}) collective-permute-start(f32[656,256]{1,0:T(8,128)} %get-tuple-element.14), channel_id=1, source_target_pairs={{0,254},{1,3},{2,0},{3,5},{4,2},{5,7},{6,4},{7,9},{8,6},{9,11},{10... | collective-permute-start | bytes 2015240 | tf_op jit(solution)/shard_map/ppermute | solution.py:611
  8.3 27.3 %copy-start.1 = (f32[512,512]{1,0:T(8,128)S(1)}, f32[512,512]{1,0:T(8,128)}, u32[]{:S(2)}) copy-start(f32[512,512]{1,0:T(8,128)} %currents.7) | copy-start | bytes 3145732
  8.3 27.3 %copy-start.3 = (f32[98,512]{1,0:T(8,128)S(1)}, f32[98,512]{1,0:T(8,128)}, u32[]{:S(2)}) copy-start(f32[98,512]{1,0:T(8,128)} %panels.7) | copy-start | bytes 602116
  8.3 79.6 %collective-permute-start.1 = (f32[616,384]{1,0:T(8,128)S(1)}, f32[616,384]{1,0:T(8,128)S(1)}, u32[]{:S(2)}, u32[]{:S(2)}) collective-permute-start(f32[616,384]{1,0:T(8,128)S(1)} %get-tuple-element.12), channel_id=1, source_target_pairs={{0,1},{1,0},{2,3},{3,2},{4,5},{5,4},{6,7},{7,6},{8,9},{9,8},{10,11... | collective-permute-start | bytes 2838536 | tf_op jit(solution)/shard_map/ppermute | solution.py:612
  34.7 1.0 copy-start.8
  35.6 0.7 copy-start.7
  35.6 52.3 %copy-start.5 = (f32[14,512]{1,0:T(8,128)S(1)}, f32[14,512]{1,0:T(8,128)}, u32[]{:S(2)}) copy-start(f32[14,512]{1,0:T(8,128)} %test.5) | copy-start | bytes 86020
  36.3 1.2 copy-start.9
  37.5 50.4 %copy-start.10 = (f32[512,512]{1,0:T(8,128)S(1)}, f32[512,512]{1,0:T(8,128)}, u32[]{:S(2)}) copy-start(f32[512,512]{1,0:T(8,128)} %copy-done.8) | copy-start | bytes 3145732
  39.5 116.2 %collective-permute-start.6 = (f32[512,384]{1,0:T(8,128)S(1)}, f32[512,384]{1,0:T(8,128)S(1)}, u32[]{:S(2)}, u32[]{:S(2)}) collective-permute-start(f32[512,384]{1,0:T(8,128)S(1)} %get-tuple-element.15.after), channel_id=1, source_target_pairs={{0,255},{1,2},{2,1},{3,4},{4,3},{5,6},{6,5},{7,8},{8,7},{9,10},{10... | collective-permute-start | bytes 2359304 | tf_op jit(solution)/shard_map/ppermute | solution.py:622
  74.6 81.2 %collective-permute-start.5 = (f32[512,512]{1,0:T(8,128)S(1)}, f32[512,512]{1,0:T(8,128)S(1)}, u32[]{:S(2)}, u32[]{:S(2)}) collective-permute-start(f32[512,512]{1,0:T(8,128)S(1)} %get-tuple-element.16), channel_id=1, source_target_pairs={{254,0},{3,1},{0,2},{5,3},{2,4},{7,5},{4,6},{9,7},{6,8},{11,9},{8,... | collective-permute-start | bytes 3145736 | tf_op jit(solution)/shard_map/ppermute | solution.py:623

commit v3 on v2

--- a/solution.py
+++ b/solution.py
@@ -221,34 +221,45 @@
     return l1r, l1i, l2r, l2i, kr, ki
 
 
-def chunk_sums(buf, ops, chunk):
-    for g in range(JC // 8):
-        acc = None
-        for q in range(QP):
-            for a in range(2):
+AHEAD = 6
+
+
+def fast_tile(ftt, tf, sf, bufs, ops, b, flag):
+    test_matrix(ftt, tf, b)
+    spare = pl.multiple_of(MROWS - 8 + 8 * flag, 8)
+
+    def piece(chunk, buf, o):
+        rows = pl.ds(pl.multiple_of(chunk * MROWS, 16), MROWS)
+        lanes = slice(o * 256, (o + 1) * 256)
+        buf[0:MROWS, lanes] = jnp.dot(sf[rows, :], tf[:, lanes], preferred_element_type=F32)
+
+    def phase(chunk, buf, next_chunk, next_buf):
+        work = [(g, q, a) for g in range(JC // 8) for q in range(QP) for a in range(2)]
+        per = -(-len(work) // NOUT)
+        acc, history = None, []
+        for o in range(NOUT):
+            piece(next_chunk, next_buf, o)
+            for g, q, a in work[o * per : (o + 1) * per]:
+                if q == 0 and a == 0:
+                    acc = None
                 row = q * JC + g * 8
-                vals = [buf[row : row + 8, o * 256 + a * BLK : o * 256 + (a + 1) * BLK] for o in range(NOUT)]
+                if len(history) >= AHEAD:
+                    buf[pl.ds(spare, 8), 0:BLK] = history[-AHEAD]
+                vals = [buf[row : row + 8, k * 256 + a * BLK : k * 256 + (a + 1) * BLK] for k in range(NOUT)]
                 terms = pair_terms(*vals)
                 acc = list(terms) if acc is None else [u + v for u, v in zip(acc, terms)]
-        start = pl.multiple_of(chunk * JC + g * 8, 8)
-        for m in range(6):
-            ops[m, pl.ds(start, 8), :] = acc[m]
-
-
-def fast_tile(ftt, tf, sf, bufs, ops, b):
-    test_matrix(ftt, tf, b)
-
-    def product(chunk, buf):
-        rows = pl.ds(pl.multiple_of(chunk * MROWS, 16), MROWS)
-        buf[...] = jnp.dot(sf[rows, :], tf[...], preferred_element_type=F32)
-
-    product(0, bufs[0])
+                history.append(acc[5])
+                if q == QP - 1 and a == 1:
+                    start = pl.multiple_of(chunk * JC + g * 8, 8)
+                    for m in range(6):
+                        ops[m, pl.ds(start, 8), :] = acc[m]
+
+    for o in range(NOUT):
+        piece(0, bufs[0], o)
 
     def step(n, carry):
-        product(2 * n + 1, bufs[1])
-        chunk_sums(bufs[0], ops, 2 * n)
-        product((2 * n + 2) % NCH, bufs[0])
-        chunk_sums(bufs[1], ops, 2 * n + 1)
+        phase(2 * n, bufs[0], 2 * n + 1, bufs[1])
+        phase(2 * n + 1, bufs[1], lax.rem(2 * n + 2, NCH), bufs[0])
         return carry
 
     lax.fori_loop(0, NCH // 2, step, 0)
@@ -326,7 +337,7 @@
 XROW = CROW + 4 * NRHS
 OUTER_ROWS = XROW + 64 + 8
 FAR_ROWS = XROW + 32 + 8
-MATE_ROWS = XROW
+MATE_ROWS = XROW + 8
 FULL = TPB * SPAN
 
 
@@ -374,6 +385,7 @@
         far[row : row + 14, (b % 2) * BLK : (b % 2 + 1) * BLK] = points
     outer[XROW + 64 : XROW + 72, :] = jnp.full((8, BLK), value, F32)
     far[XROW + 32 : XROW + 40, :] = jnp.full((8, 2 * BLK), value, F32)
+    mate[XROW : XROW + 8, :] = jnp.full((8, 3 * BLK), value, F32)
     load[...] = jnp.full((8, BLK), value, F32)
 
 
@@ -407,7 +419,7 @@
                 def _():
                     @pl.when(flags[b] > 0)
                     def _():
-                        fast_tile(ftt, tf, sf, (buf0, buf1), ops, b)
+                        fast_tile(ftt, tf, sf, (buf0, buf1), ops, b, flags[b])
 
                     @pl.when(flags[b] == 0)
                     def _():
@@ -472,14 +484,41 @@
     write_out(out, scratch[12], range(TPB))
 
 
-def help_kernel(mask, panels, currents, outer, far, load_mate, after, out_near, out_far, *scratch):
+QUOTA = 7
+HELP_STEPS = 6
+OWN_STEPS = 8
+
+
+def own_place(even, n):
+    return jnp.where(n < 4, n, jnp.where(n == 4, jnp.where(even, -1, 4), jnp.where(even, n - 1, n - 8)))
+
+
+def load_own(scratch, panels, currents, outer, mate, n):
+    @pl.when(n < 4)
+    def _():
+        fill(scratch, panels, currents, 0, n)
+
+    @pl.when(n == 4)
+    def _():
+        fill(scratch, outer, outer, CROW, 0)
+
+    @pl.when(n > 4)
+    def _():
+        fill(scratch, mate, mate, CROW, n - 5)
+
+
+def second_kernel(
+    mask, test, panels, currents, outer, far, mate, load_far, part, out_near, out_far, out_own, todo, *scratch
+):
+    plan, scratch = scratch[-1], scratch[:-1]
     even = is_even()
     odd = jnp.logical_not(even)
-    own, mate = load_of(mask), number(load_mate, 0)
-    near_full = number(outer, XROW + 64) == FULL
-    far_full = number(far, XROW + 32) == FULL
-    share_near, _ = shares(own, mate)
-    _, share_far = shares(mate, own)
+    own_load, mate_load = load_of(mask), number(mate, XROW)
+    near_load, far_load = number(outer, XROW + 64), number(far, XROW + 32)
+    share_near, _ = shares(own_load, mate_load)
+    _, share_far = shares(mate_load, own_load)
+    give_near, give_far = shares(near_load, number(load_far, 0))
+    full = own_load == FULL
     xt, acc = scratch[1], scratch[12]
     fill_tests(xt, 0, lambda b, row: outer[XROW + 16 * b + row : XROW + 16 * b + row + 2, :])
     fill_tests(
@@ -489,14 +528,40 @@
             XROW + 16 * (b // 2) + row : XROW + 16 * (b // 2) + row + 2, (b % 2) * BLK : (b % 2 + 1) * BLK
         ],
     )
+    fill_tests(xt, 2, own_tests(test))
     clear(acc, 2 * TPB)
-
-    def wanted(n, b):
+    for b in range(TPB):
+        for g in range(4):
+            acc[2 * TPB + b, :, g * BLK : (g + 1) * BLK] = part[g * NRHS : (g + 1) * NRHS, b * BLK : (b + 1) * BLK]
+
+    def plan_help(i, used):
+        n, b = lax.div(i, TPB), lax.rem(i, TPB)
         v_near, v_far = mirrored(odd, b), mirrored(even, b)
         of_own = (n < 3) & (v_near <= 2 - n)
         of_outer = (n == 3) & (v_near < share_near - 6)
         of_far = (n > 3) & ((n - 4) * TPB + v_far < share_far)
-        return (near_full & (of_own | of_outer)) | (far_full & of_far)
+        wanted = ((near_load == FULL) & (of_own | of_outer)) | ((far_load == FULL) & of_far)
+        plan[i] = wanted.astype(jnp.int32)
+        return used + wanted.astype(jnp.int32)
+
+    def plan_own(i, used):
+        n, b = lax.div(i, TPB), lax.rem(i, TPB)
+        rel = own_place(even, n)
+        column = rel - b + REACH
+        inside = (column >= 0) & (column < SPAN)
+        sparse = inside & (mask[b, jnp.clip(column, 0, SPAN - 1)] > 0) & (rel != b)
+        u, v = mirrored(even, rel), mirrored(even, b)
+        given = (u == 1) | ((u == 0) & (v < give_near - 6))
+        given = given | ((u == 3) & (v < give_far)) | ((u == 2) & (TPB + v < give_far))
+        dense = inside & (u >= 0) & jnp.logical_not(given)
+        wanted = (full & dense) | (jnp.logical_not(full) & sparse)
+        now = wanted & (used < QUOTA)
+        plan[HELP_STEPS * TPB + i] = now.astype(jnp.int32)
+        todo[n, b] = (wanted & jnp.logical_not(now)).astype(jnp.int32)
+        return used + now.astype(jnp.int32)
+
+    used = lax.fori_loop(0, HELP_STEPS * TPB, plan_help, jnp.int32(0))
+    lax.fori_loop(0, OWN_STEPS * TPB, plan_own, used)
 
     def load_source(n):
         @pl.when(n < 3)
@@ -507,51 +572,40 @@
         def _():
             fill(scratch, outer, outer, CROW, 0)
 
-        @pl.when(n > 3)
+        @pl.when((n > 3) & (n < HELP_STEPS))
         def _():
             fill(scratch, far, far, CROW, jnp.where(even, 5 - n, n - 4))
 
-    engine(scratch, 6, wanted, load_source, lambda n: jnp.where(n > 3, 1, 0))
+        @pl.when(n >= HELP_STEPS)
+        def _():
+            load_own(scratch, panels, currents, outer, mate, n - HELP_STEPS)
+
+    engine(
+        scratch,
+        HELP_STEPS + OWN_STEPS,
+        lambda n, b: plan[n * TPB + b] > 0,
+        load_source,
+        lambda n: jnp.where(n < 4, 0, jnp.where(n < HELP_STEPS, 1, 2)),
+    )
     shift = jnp.where(even, 1, 0)
     write_out(out_near, acc, [b + shift for b in range(TPB - 1)])
     write_out(out_far, acc, range(TPB, 2 * TPB))
-
-
-def rest_kernel(mask, test, panels, currents, outer, mate, load_far, part, after, out, *scratch):
-    even = is_even()
-    full = load_of(mask) == FULL
-    share_near, share_far = shares(number(outer, XROW + 64), number(load_far, 0))
+    write_out(out_own, acc, range(2 * TPB, 3 * TPB))
+
+
+def rest_kernel(todo, test, panels, currents, outer, mate, part, after, out, *scratch):
     acc = scratch[12]
     fill_tests(scratch[1], 0, own_tests(test))
     for b in range(TPB):
         for g in range(4):
             acc[b, :, g * BLK : (g + 1) * BLK] = part[g * NRHS : (g + 1) * NRHS, b * BLK : (b + 1) * BLK]
-
-    def wanted(n, b):
-        rel = jnp.where(n < 4, n, jnp.where(n == 4, jnp.where(even, -1, 4), jnp.where(even, n - 1, n - 8)))
-        column = rel - b + REACH
-        inside = (column >= 0) & (column < SPAN)
-        sparse = inside & (mask[b, jnp.clip(column, 0, SPAN - 1)] > 0) & (rel != b)
-        u, v = mirrored(even, rel), mirrored(even, b)
-        given = (u == 1) | ((u == 0) & (v < share_near - 6))
-        given = given | ((u == 3) & (v < share_far)) | ((u == 2) & (TPB + v < share_far))
-        dense = inside & (u >= 0) & jnp.logical_not(given)
-        return (full & dense) | (jnp.logical_not(full) & sparse)
-
-    def load_source(n):
-        @pl.when(n < 4)
-        def _():
-            fill(scratch, panels, currents, 0, n)
-
-        @pl.when(n == 4)
-        def _():
-            fill(scratch, outer, outer, CROW, 0)
-
-        @pl.when(n > 4)
-        def _():
-            fill(scratch, mate, mate, CROW, n - 5)
-
-    engine(scratch, 8, wanted, load_source, lambda n: 0)
+    engine(
+        scratch,
+        OWN_STEPS,
+        lambda n, b: todo[n, b] > 0,
+        lambda n: load_own(scratch, panels, currents, outer, mate, n),
+        lambda n: 0,
+    )
     write_out(out, acc, range(TPB))
 
 
@@ -563,8 +617,8 @@
         pltpu.VMEM((TROWS * 8, BLK), F32),
         pltpu.VMEM((KDIM, NOUT * 256), BF16),
         pltpu.VMEM((NCH * MROWS, KDIM), BF16),
-        pltpu.VMEM((MROWS, NOUT * 256), F32),
-        pltpu.VMEM((MROWS, NOUT * 256), F32),
+        pltpu.VMEM((MROWS + 8, NOUT * 256), F32),
+        pltpu.VMEM((MROWS + 8, NOUT * 256), F32),
         pltpu.VMEM((6, BLK, BLK), F32),
         pltpu.VMEM((2 * BLK, 4 * BLK), BF16),
         pltpu.VMEM((4 * BLK, 4 * BLK), BF16),
@@ -575,18 +629,25 @@
     ]
 
 
-def call(kernel, outs, operands, sets=0, unread=0, tiles=1):
+def call(kernel, outs, operands, sets=0, unread=0, tiles=1, table=False):
     vmem = pl.BlockSpec(memory_space=pltpu.VMEM)
+    smem = pl.BlockSpec(memory_space=pltpu.SMEM)
     anywhere = pl.BlockSpec(memory_space=pl.ANY)
-    several = len(outs) > 1
     plain = len(operands) - 1 - unread
+    shapes = [jax.ShapeDtypeStruct(s, F32) for s in outs]
+    specs = [vmem] * len(outs)
+    scratch = scratch_for(sets) if sets else []
+    if table:
+        shapes.append(jax.ShapeDtypeStruct((OWN_STEPS, TPB), jnp.int32))
+        specs.append(smem)
+        scratch.append(pltpu.SMEM(((HELP_STEPS + OWN_STEPS) * TPB,), jnp.int32))
     return pl.pallas_call(
         kernel,
-        out_shape=[jax.ShapeDtypeStruct(s, F32) for s in outs] if several else jax.ShapeDtypeStruct(outs[0], F32),
-        in_specs=[pl.BlockSpec(memory_space=pltpu.SMEM)] + [vmem] * plain + [anywhere] * unread,
-        out_specs=[vmem] * len(outs) if several else vmem,
-        scratch_shapes=scratch_for(sets) if sets else [],
-        compiler_params=pltpu.CompilerParams(vmem_limit_bytes=48 * 1024 * 1024),
+        out_shape=shapes,
+        in_specs=[smem] + [vmem] * plain + [anywhere] * unread,
+        out_specs=specs,
+        scratch_shapes=scratch,
+        compiler_params=pltpu.CompilerParams(vmem_limit_bytes=52 * 1024 * 1024),
         cost_estimate=pl.CostEstimate(flops=tiles * 5 * 10**9, bytes_accessed=4 * 10**6, transcendentals=0),
     )(*operands)
 
@@ -605,26 +666,25 @@
         [(MATE_ROWS, 3 * BLK), (OUTER_ROWS, BLK), (FAR_ROWS, 2 * BLK), (8, BLK)],
         [near_mask, panels, test_points, currents],
     )
-    load_mate = lax.ppermute(load, axes, swap)
     load_far = lax.ppermute(load, axes, back)
     outer = lax.ppermute(outer, axes, across)
     far = lax.ppermute(far, axes, away)
     mate = lax.ppermute(mate, axes, swap)
-    part = call(first_kernel, [(wide, width)], [near_mask, test_points, panels, currents], 1, tiles=4)
-    to_near, to_far = call(
-        help_kernel,
-        [(wide, width - BLK), (wide, width)],
-        [near_mask, panels, currents, outer, far, load_mate, part],
-        2,
-        unread=1,
+    (part,) = call(first_kernel, [(wide, width)], [near_mask, test_points, panels, currents], 1, tiles=4)
+    to_near, to_far, part, todo = call(
+        second_kernel,
+        [(wide, width - BLK), (wide, width), (wide, width)],
+        [near_mask, test_points, panels, currents, outer, far, mate, load_far, part],
+        3,
         tiles=7,
+        table=True,
     )
     from_near = lax.ppermute(to_near, axes, across)
     from_far = lax.ppermute(to_far, axes, back)
-    rest = call(
+    (rest,) = call(
         rest_kernel,
         [(wide, width)],
-        [near_mask, test_points, panels, currents, outer, mate, load_far, part, to_near],
+        [todo, test_points, panels, currents, outer, mate, part, to_near],
         1,
         unread=1,
         tiles=8,

time: 157 us -> 130 us (0.83)
  the two profiles are of different devices: /device:TPU:81 before, /device:TPU:2 now
where the time goes in v3:
time: 130 us; the launch traced here: 129 us
  Pallas kernels  98.7 us (76%)
  starting transfers between devices  22.7 us (17%)
  local copies, waits for them, and re-layouts  5.42 us (4%)
  other arithmetic  2.51 us (2%)
    pallas_call x4, Pallas kernels, call(): pl.pallas_call(kernel, out_shape=shapes, in_specs=[smem] + [vmem] * plain...  98.7 us
    ppermute x1, starting transfers between devices, body(): from_far = lax.ppermute(to_far, axes, back)  12.7 us
    ppermute x1, starting transfers between devices, body(): load_far = lax.ppermute(load, axes, back)  6.79 us
    unnamed x18, local copies, waits for them, and re-layouts  5.42 us
  transfers between devices with their start and end apart: 6, of which 0 were waited for; matrix products, arithmetic and copies ran while one was open for 0% of the time, Pallas kernels for 41%

profile of v3, /device:TPU:2, one launch (start us, length us, event | category | flops | bytes accessed | tf_op | source)
XLA Modules:
  0.0 129.4 jit_solution(8314609600683121176)
XLA Ops:
  0.0 0.0 copy-start.1
  0.0 0.9 copy-done.1
  0.9 0.0 copy-start.3
  0.9 0.8 copy-done.3
  1.7 0.0 copy-start.5
  1.7 0.7 copy-done.5
  2.4 0.0 copy-start.4
  2.4 2.3 %shard_map.46 = (f32[624,384]{1,0:T(8,128)}, f32[688,128]{1,0:T(8,128)S(1)}, f32[656,256]{1,0:T(8,128)S(1)}, f32[8,128]{1,0:T(8,128)S(1)}) custom-call(s32[4,7]{1,0:T(4,128)S(1)} %copy-done.5, f32[98,512]{1,0:T(8,128)S(1)} %copy-done.1, f32[14,512]{1,0:T(8,128)S(1)} %copy-done.3, f32[512,512]{1,0:T(8,128)} %currents.7), custom_call_target="tpu_custom_call" | custom-call | flops 5000000000 | bytes 4000000 | tf_op jit(solution)/shard_map/pallas_call | solution.py:644
  4.7 2.3 %collective-permute-start.2 = (f32[624,384]{1,0:T(8,128)}, f32[624,384]{1,0:T(8,128)S(1)}, u32[]{:S(2)}, u32[]{:S(2)}) collective-permute-start(f32[624,384]{1,0:T(8,128)} %get-tuple-element.15), channel_id=1, source_target_pairs={{0,1},{1,0},{2,3},{3,2},{4,5},{5,4},{6,7},{7,6},{8,9},{9,8},{10,11... | collective-permute-start | bytes 2875400 | tf_op jit(solution)/shard_map/ppermute | solution.py:672
  7.0 0.0 collective-permute-start
  7.0 0.9 collective-permute-start.1
  7.9 0.0 copy-start.2
  7.9 6.8 %collective-permute-start.3 = (f32[8,128]{1,0:T(8,128)S(1)}, f32[8,128]{1,0:T(8,128)S(1)}, u32[]{:S(2)}, u32[]{:S(2)}) collective-permute-start(f32[8,128]{1,0:T(8,128)S(1)} %get-tuple-element.16), channel_id=1, source_target_pairs={{254,0},{3,1},{0,2},{5,3},{2,4},{7,5},{4,6},{9,7},{6,8},{11,9},{8,... | collective-permute-start | bytes 12296 | tf_op jit(solution)/shard_map/ppermute | solution.py:669
  14.7 0.0 copy-done.4
  14.7 23.5 %shard_map.47.part = f32[512,512]{1,0:T(8,128)S(1)} custom-call(s32[4,7]{1,0:T(4,128)S(1)} %copy-done.5, f32[14,512]{1,0:T(8,128)S(1)} %copy-done.4, f32[98,512]{1,0:T(8,128)S(1)} %copy-done.1, f32[512,512]{1,0:T(8,128)} %currents.7), custom_call_target="tpu_custom_call" | custom-call | flops 20000000000 | bytes 4000000 | tf_op jit(solution)/shard_map/pallas_call | solution.py:644
  38.2 0.0 copy-start.7
  38.2 1.0 copy-done.7
  39.2 0.0 copy-start.6
  39.2 0.0 collective-permute-done.3.load_far
  39.2 0.0 collective-permute-done.outer
  39.2 0.0 collective-permute-done.1.far
  39.2 0.0 collective-permute-done.2.mate
  39.2 0.0 copy-start.8
  39.2 0.9 copy-done.8
  40.2 0.0 copy-done.2
  40.2 0.0 copy-done.6
  40.2 42.6 %shard_map.48 = (f32[512,384]{1,0:T(8,128)}, f32[512,512]{1,0:T(8,128)}, f32[512,512]{1,0:T(8,128)}, s32[8,4]{1,0:T(8,128)S(1)}) custom-call(s32[4,7]{1,0:T(4,128)S(1)} %copy-done.6, f32[14,512]{1,0:T(8,128)S(1)} %copy-done.4, f32[98,512]{1,0:T(8,128)S(1)} %copy-done.2, f32[512,512]{1,0:T(8,128)} %currents.7, f32[688,128]{1,0:T(8,128)S(1)} %collective-permute-done.outer, ...), custom_call_target="tpu_custom_call" | custom-call | flops 35000000512 | bytes 4000000 | tf_op jit(solution)/shard_map/pallas_call | solution.py:644
  82.8 0.1 collective-permute-start.5
  82.9 12.7 %collective-permute-start.4 = (f32[512,512]{1,0:T(8,128)}, f32[512,512]{1,0:T(8,128)S(1)}, u32[]{:S(2)}, u32[]{:S(2)}) collective-permute-start(f32[512,512]{1,0:T(8,128)} %get-tuple-element.20), channel_id=1, source_target_pairs={{254,0},{3,1},{0,2},{5,3},{2,4},{7,5},{4,6},{9,7},{6,8},{11,9},{8,... | collective-permute-start | bytes 3145736 | tf_op jit(solution)/shard_map/ppermute | solution.py:683
  95.6 0.0 copy-start
  95.6 1.1 copy-done
  96.7 30.1 %shard_map.49 = f32[512,512]{1,0:T(8,128)} custom-call(s32[8,4]{1,0:T(8,128)S(1)} %get-tuple-element.17.todo, f32[14,512]{1,0:T(8,128)S(1)} %copy-done.4, f32[98,512]{1,0:T(8,128)S(1)} %copy-done.2, f32[512,512]{1,0:T(8,128)} %currents.7, f32[688,128]{1,0:T(8,128)S(1)} %collective-permute-done.outer, f32[624,384]{1,0:T(8,128)} %copy-done.8, ...), custom_call_target="tpu_custom_call" | custom-call | flops 40000000000 | bytes 4000000 | tf_op jit(solution)/shard_map/pallas_call | solution.py:644
  126.9 0.0 collective-permute-done.5
  126.9 0.0 collective-permute-done.4
  126.9 2.5 %select_add_fusion = f32[512,512]{1,0:T(8,128)} fusion(f32[512,384]{1,0:T(8,128)S(1)} %collective-permute-done.5, f32[512,512]{1,0:T(8,128)} %shard_map.49, f32[512,512]{1,0:T(8,128)S(1)} %collective-permute-done.4, pred[]{:T(512)S(6)} %eq.3), kind=kLoop, calls=%fused_computation | loop fusion | flops 786432 | bytes 3932161 | tf_op jit(solution)/shard_map/add | solution.py:697
Async XLA Ops:
  0.0 0.9 copy-start.1
  0.9 0.8 copy-start.3
  1.7 0.7 copy-start.5
  2.4 12.3 %copy-start.4 = (f32[14,512]{1,0:T(8,128)S(1)}, f32[14,512]{1,0:T(8,128)}, u32[]{:S(2)}) copy-start(f32[14,512]{1,0:T(8,128)} %test.7) | copy-start | bytes 86020
  4.7 34.5 %collective-permute-start.2 = (f32[624,384]{1,0:T(8,128)}, f32[624,384]{1,0:T(8,128)S(1)}, u32[]{:S(2)}, u32[]{:S(2)}) collective-permute-start(f32[624,384]{1,0:T(8,128)} %get-tuple-element.15), channel_id=1, source_target_pairs={{0,1},{1,0},{2,3},{3,2},{4,5},{5,4},{6,7},{7,6},{8,9},{9,8},{10,11... | collective-permute-start | bytes 2875400 | tf_op jit(solution)/shard_map/ppermute | solution.py:672
  7.0 32.2 %collective-permute-start = (f32[688,128]{1,0:T(8,128)S(1)}, f32[688,128]{1,0:T(8,128)S(1)}, u32[]{:S(2)}, u32[]{:S(2)}) collective-permute-start(f32[688,128]{1,0:T(8,128)S(1)} %get-tuple-element.13), channel_id=1, source_target_pairs={{0,255},{1,2},{2,1},{3,4},{4,3},{5,6},{6,5},{7,8},{8,7},{9,10},{10... | collective-permute-start | bytes 1056776 | tf_op jit(solution)/shard_map/ppermute | solution.py:670
  7.0 32.2 %collective-permute-start.1 = (f32[656,256]{1,0:T(8,128)S(1)}, f32[656,256]{1,0:T(8,128)S(1)}, u32[]{:S(2)}, u32[]{:S(2)}) collective-permute-start(f32[656,256]{1,0:T(8,128)S(1)} %get-tuple-element.14), channel_id=1, source_target_pairs={{0,254},{1,3},{2,0},{3,5},{4,2},{5,7},{6,4},{7,9},{8,6},{9,11},{10... | collective-permute-start | bytes 2015240 | tf_op jit(solution)/shard_map/ppermute | solution.py:671
  7.9 32.3 %copy-start.2 = (f32[98,512]{1,0:T(8,128)S(1)}, f32[98,512]{1,0:T(8,128)}, u32[]{:S(2)}) copy-start(f32[98,512]{1,0:T(8,128)} %panels.7) | copy-start | bytes 602116
  7.9 31.3 %collective-permute-start.3 = (f32[8,128]{1,0:T(8,128)S(1)}, f32[8,128]{1,0:T(8,128)S(1)}, u32[]{:S(2)}, u32[]{:S(2)}) collective-permute-start(f32[8,128]{1,0:T(8,128)S(1)} %get-tuple-element.16), channel_id=1, source_target_pairs={{254,0},{3,1},{0,2},{5,3},{2,4},{7,5},{4,6},{9,7},{6,8},{11,9},{8,... | collective-permute-start | bytes 12296 | tf_op jit(solution)/shard_map/ppermute | solution.py:669
  38.2 1.0 copy-start.7
  39.2 1.0 copy-start.6
  39.2 0.9 copy-start.8
  82.8 44.0 %collective-permute-start.5 = (f32[512,384]{1,0:T(8,128)}, f32[512,384]{1,0:T(8,128)S(1)}, u32[]{:S(2)}, u32[]{:S(2)}) collective-permute-start(f32[512,384]{1,0:T(8,128)} %get-tuple-element.19.after), channel_id=1, source_target_pairs={{0,255},{1,2},{2,1},{3,4},{4,3},{5,6},{6,5},{7,8},{8,7},{9,10},{10... | collective-permute-start | bytes 2359304 | tf_op jit(solution)/shard_map/ppermute | solution.py:682
  82.9 43.9 %collective-permute-start.4 = (f32[512,512]{1,0:T(8,128)}, f32[512,512]{1,0:T(8,128)S(1)}, u32[]{:S(2)}, u32[]{:S(2)}) collective-permute-start(f32[512,512]{1,0:T(8,128)} %get-tuple-element.20), channel_id=1, source_target_pairs={{254,0},{3,1},{0,2},{5,3},{2,4},{7,5},{4,6},{9,7},{6,8},{11,9},{8,... | collective-permute-start | bytes 3145736 | tf_op jit(solution)/shard_map/ppermute | solution.py:683
  95.6 1.1 copy-start

commit v4 on v3

--- a/solution.py
+++ b/solution.py
@@ -107,7 +107,7 @@
         zrow = jnp.where(rows < 4, em, eh)
         zrow2 = jnp.where(rows < 4, el, jnp.where(rows == 4, 1.0, 0.0))
         full = jnp.concatenate([mh, mh, ml, bh, bh, bl, zrow, zrow2], 0)
-        turned = full.T.astype(BF16)
+        turned = full.astype(BF16).T
         for ch in range(NCH):
             sf[ch * MROWS + q * JC : ch * MROWS + (q + 1) * JC, :] = turned[ch * JC : (ch + 1) * JC, :]
 
@@ -367,26 +367,38 @@
     return jnp.clip(goal - load_near, 6, 9), jnp.clip(goal - load_far, 0, 8)
 
 
-def pack_kernel(mask, panels, test, currents, mate, outer, far, load):
+PACK_COPIES = 5
+
+
+def pack_kernel(mask, panels_at, test_at, currents, mate, outer, far, load, panels, test, sems):
     even = is_even()
-    for ref, count, begin in (
-        (mate, 3, jnp.where(even, BLK, 0)),
+    places = (
         (outer, 1, jnp.where(even, 0, 3 * BLK)),
         (far, 2, jnp.where(even, 2 * BLK, 0)),
-    ):
-        lanes = pl.ds(pl.multiple_of(begin, BLK), count * BLK)
-        ref[0:GROWS, :] = panels[:, lanes]
-        ref[CROW:XROW, :] = currents[:, lanes]
+        (mate, 3, jnp.where(even, BLK, 0)),
+    )
+    lanes = [pl.ds(pl.multiple_of(begin, BLK), count * BLK) for _, count, begin in places]
+    copies = [pltpu.make_async_copy(panels_at, panels, sems.at[0]), pltpu.make_async_copy(test_at, test, sems.at[1])]
+    for k in range(3):
+        copies.append(pltpu.make_async_copy(currents.at[:, lanes[k]], places[k][0].at[CROW:XROW, :], sems.at[2 + k]))
+    for each in copies:
+        each.start()
     value = load_of(mask).astype(F32)
+    outer[XROW + 64 : XROW + 72, :] = jnp.full((8, BLK), value, F32)
+    far[XROW + 32 : XROW + 40, :] = jnp.full((8, 2 * BLK), value, F32)
+    mate[XROW : XROW + 8, :] = jnp.full((8, 3 * BLK), value, F32)
+    load[...] = jnp.full((8, BLK), value, F32)
+    copies[0].wait()
+    copies[1].wait()
+    for k in range(3):
+        places[k][0][0:GROWS, :] = panels[:, lanes[k]]
     for b in range(TPB):
         points = test[:, b * BLK : (b + 1) * BLK]
         outer[XROW + 16 * b : XROW + 16 * b + 14, :] = points
         row = XROW + 16 * (b // 2)
         far[row : row + 14, (b % 2) * BLK : (b % 2 + 1) * BLK] = points
-    outer[XROW + 64 : XROW + 72, :] = jnp.full((8, BLK), value, F32)
-    far[XROW + 32 : XROW + 40, :] = jnp.full((8, 2 * BLK), value, F32)
-    mate[XROW : XROW + 8, :] = jnp.full((8, 3 * BLK), value, F32)
-    load[...] = jnp.full((8, BLK), value, F32)
+    for each in copies[2:]:
+        each.wait()
 
 
 def engine(scratch, steps, wanted, load_source, accset):
@@ -629,7 +641,7 @@
     ]
 
 
-def call(kernel, outs, operands, sets=0, unread=0, tiles=1, table=False):
+def call(kernel, outs, operands, sets=0, unread=0, tiles=1, table=False, copies=0):
     vmem = pl.BlockSpec(memory_space=pltpu.VMEM)
     smem = pl.BlockSpec(memory_space=pltpu.SMEM)
     anywhere = pl.BlockSpec(memory_space=pl.ANY)
@@ -637,6 +649,12 @@
     shapes = [jax.ShapeDtypeStruct(s, F32) for s in outs]
     specs = [vmem] * len(outs)
     scratch = scratch_for(sets) if sets else []
+    if copies:
+        scratch += [
+            pltpu.VMEM((GROWS, TPB * BLK), F32),
+            pltpu.VMEM((14, TPB * BLK), F32),
+            pltpu.SemaphoreType.DMA((copies,)),
+        ]
     if table:
         shapes.append(jax.ShapeDtypeStruct((OWN_STEPS, TPB), jnp.int32))
         specs.append(smem)
@@ -647,7 +665,7 @@
         in_specs=[smem] + [vmem] * plain + [anywhere] * unread,
         out_specs=specs,
         scratch_shapes=scratch,
-        compiler_params=pltpu.CompilerParams(vmem_limit_bytes=52 * 1024 * 1024),
+        compiler_params=pltpu.CompilerParams(vmem_limit_bytes=(60 if copies else 26) * 1024 * 1024),
         cost_estimate=pl.CostEstimate(flops=tiles * 5 * 10**9, bytes_accessed=4 * 10**6, transcendentals=0),
     )(*operands)
 
@@ -665,6 +683,8 @@
         pack_kernel,
         [(MATE_ROWS, 3 * BLK), (OUTER_ROWS, BLK), (FAR_ROWS, 2 * BLK), (8, BLK)],
         [near_mask, panels, test_points, currents],
+        unread=3,
+        copies=PACK_COPIES,
     )
     load_far = lax.ppermute(load, axes, back)
     outer = lax.ppermute(outer, axes, across)

time: 130 us -> 115 us (0.88)
  the two profiles are of different devices: /device:TPU:2 before, /device:TPU:74 now
where the time goes in v4:
time: 115 us
  Pallas kernels  90.5 us (79%)
  starting transfers between devices  16.1 us (14%)
  waiting for transfers between devices  4.47 us (4%)
  local copies, waits for them, and re-layouts  2.22 us (2%)
  other arithmetic  1.3 us (1%)
    pallas_call x4, Pallas kernels, call(): pl.pallas_call(kernel, out_shape=shapes, in_specs=[smem] + [vmem] * plain...  90.5 us
    ppermute x1, starting transfers between devices, body(): from_far = lax.ppermute(to_far, axes, back)  10.9 us
    ppermute x1, waiting for transfers between devices, body(): outer = lax.ppermute(outer, axes, across)  4.46 us
  transfers between devices with their start and end apart: 6, of which 1 were waited for; matrix products, arithmetic and copies ran while one was open for 0% of the time, Pallas kernels for 41%

profile of v4, /device:TPU:74, one launch (start us, length us, event | category | flops | bytes accessed | tf_op | source)
XLA Modules:
  0.0 114.7 jit_solution(4617305399577811841)
XLA Ops:
  0.0 0.0 copy-start.1
  0.0 0.0 copy-start.2
  0.0 0.0 copy-start
  0.0 3.7 %shard_map.46 = (f32[624,384]{1,0:T(8,128)}, f32[688,128]{1,0:T(8,128)}, f32[656,256]{1,0:T(8,128)}, f32[8,128]{1,0:T(8,128)}) custom-call(s32[4,7]{1,0:T(4,128)} %mask.5, f32[98,512]{1,0:T(8,128)} %panels.5, f32[14,512]{1,0:T(8,128)} %test.5, f32[512,512]{1,0:T(8,128)} %currents.7), custom_call_target="tpu_custom_call" | custom-call | flops 5000000000 | bytes 4000000 | tf_op jit(solution)/shard_map/pallas_call | solution.py:662
  3.7 0.0 copy-start.6
  3.7 0.8 collective-permute-start.2
  4.5 0.0 copy-start.3
  4.5 0.5 collective-permute-start
  5.0 2.0 %collective-permute-start.1 = (f32[656,256]{1,0:T(8,128)}, f32[656,256]{1,0:T(8,128)S(1)}, u32[]{:S(2)}, u32[]{:S(2)}) collective-permute-start(f32[656,256]{1,0:T(8,128)} %get-tuple-element.14), channel_id=1, source_target_pairs={{0,254},{1,3},{2,0},{3,5},{4,2},{5,7},{6,4},{7,9},{8,6},{9,11},{10... | collective-permute-start | bytes 2015240 | tf_op jit(solution)/shard_map/ppermute | solution.py:691
  7.0 0.0 copy-done.6
  7.0 0.1 collective-permute-start.3
  7.0 0.0 copy-done.1
  7.0 0.0 copy-done.2
  7.0 0.0 copy-done
  7.0 0.0 copy-done.3
  7.0 20.9 %shard_map.47.part = f32[512,512]{1,0:T(8,128)S(1)} custom-call(s32[4,7]{1,0:T(4,128)S(1)} %copy-done.3, f32[14,512]{1,0:T(8,128)S(1)} %copy-done.2, f32[98,512]{1,0:T(8,128)S(1)} %copy-done.1, f32[512,512]{1,0:T(8,128)S(1)} %copy-done), custom_call_target="tpu_custom_call" | custom-call | flops 20000000000 | bytes 4000000 | tf_op jit(solution)/shard_map/pallas_call | solution.py:662
  27.9 0.0 copy-start.4
  28.0 1.0 copy-done.4
  28.9 0.0 collective-permute-done.3.load_far
  28.9 4.5 %collective-permute-done.outer = f32[688,128]{1,0:T(8,128)S(1)} collective-permute-done((f32[688,128]{1,0:T(8,128)}, f32[688,128]{1,0:T(8,128)S(1)}, u32[]{:S(2)}, u32[]{:S(2)}) %collective-permute-start) | collective-permute-done | bytes 352288 | tf_op jit(solution)/shard_map/ppermute | solution.py:690
  33.4 0.0 collective-permute-done.1.far
  33.4 0.0 collective-permute-done.2.mate
  33.4 0.0 copy-start.5
  33.4 1.2 %copy-done.5 = f32[512,512]{1,0:T(8,128)S(1)} copy-done((f32[512,512]{1,0:T(8,128)S(1)}, f32[512,512]{1,0:T(8,128)}, u32[]{:S(2)}) %copy-start.5) | copy-done | bytes 1048600
  34.6 39.5 %shard_map.48 = (f32[512,384]{1,0:T(8,128)S(1)}, f32[512,512]{1,0:T(8,128)S(1)}, f32[512,512]{1,0:T(8,128)S(1)}, s32[8,4]{1,0:T(8,128)S(1)}) custom-call(s32[4,7]{1,0:T(4,128)S(1)} %copy-done.3, f32[14,512]{1,0:T(8,128)S(1)} %copy-done.2, f32[98,512]{1,0:T(8,128)S(1)} %copy-done.1, f32[512,512]{1,0:T(8,128)S(1)} %copy-done, ...), custom_call_target="tpu_custom_call" | custom-call | flops 35000000512 | bytes 4000000 | tf_op jit(solution)/shard_map/pallas_call | solution.py:662
  74.1 1.9 %collective-permute-start.5 = (f32[512,384]{1,0:T(8,128)S(1)}, f32[512,384]{1,0:T(8,128)S(1)}, u32[]{:S(2)}, u32[]{:S(2)}) collective-permute-start(f32[512,384]{1,0:T(8,128)S(1)} %get-tuple-element.19.after), channel_id=1, source_target_pairs={{0,255},{1,2},{2,1},{3,4},{4,3},{5,6},{6,5},{7,8},{8,7},{9,10},{10... | collective-permute-start | bytes 2359304 | tf_op jit(solution)/shard_map/ppermute | solution.py:702
  76.0 10.9 %collective-permute-start.4 = (f32[512,512]{1,0:T(8,128)S(1)}, f32[512,512]{1,0:T(8,128)S(1)}, u32[]{:S(2)}, u32[]{:S(2)}) collective-permute-start(f32[512,512]{1,0:T(8,128)S(1)} %get-tuple-element.20), channel_id=1, source_target_pairs={{254,0},{3,1},{0,2},{5,3},{2,4},{7,5},{4,6},{9,7},{6,8},{11,9},{8,... | collective-permute-start | bytes 3145736 | tf_op jit(solution)/shard_map/ppermute | solution.py:703
  86.9 26.5 %shard_map.49 = f32[512,512]{1,0:T(8,128)S(1)} custom-call(s32[8,4]{1,0:T(8,128)S(1)} %get-tuple-element.17.todo, f32[14,512]{1,0:T(8,128)S(1)} %copy-done.2, f32[98,512]{1,0:T(8,128)S(1)} %copy-done.1, f32[512,512]{1,0:T(8,128)S(1)} %copy-done, f32[688,128]{1,0:T(8,128)S(1)} %collective-permute-done.outer, f32[624,384]{1,0:T(8,128)S(1)} %collective-permute-done.2.mate, ...), custom_call_target="tpu_custom_call" | custom-call | flops 40000000000 | bytes 4000000 | tf_op jit(solution)/shard_map/pallas_call | solution.py:662
  113.4 0.0 collective-permute-done.5
  113.4 0.0 collective-permute-done.4
  113.4 1.3 %select_add_fusion = f32[512,512]{1,0:T(8,128)} fusion(f32[512,384]{1,0:T(8,128)S(1)} %collective-permute-done.5, f32[512,512]{1,0:T(8,128)S(1)} %shard_map.49, f32[512,512]{1,0:T(8,128)S(1)} %collective-permute-done.4, pred[]{:T(512)S(6)} %eq.3), kind=kLoop, calls=%fused_computation | loop fusion | flops 786432 | bytes 3932161 | tf_op jit(solution)/shard_map/add | solution.py:717
Async XLA Ops:
  0.0 7.0 %copy-start.1 = (f32[98,512]{1,0:T(8,128)S(1)}, f32[98,512]{1,0:T(8,128)}, u32[]{:S(2)}) copy-start(f32[98,512]{1,0:T(8,128)} %panels.5) | copy-start | bytes 602116
  0.0 7.0 %copy-start.2 = (f32[14,512]{1,0:T(8,128)S(1)}, f32[14,512]{1,0:T(8,128)}, u32[]{:S(2)}) copy-start(f32[14,512]{1,0:T(8,128)} %test.5) | copy-start | bytes 86020
  0.0 7.0 %copy-start = (f32[512,512]{1,0:T(8,128)S(1)}, f32[512,512]{1,0:T(8,128)}, u32[]{:S(2)}) copy-start(f32[512,512]{1,0:T(8,128)} %currents.7) | copy-start | bytes 3145732
  3.7 3.3 %copy-start.6 = (f32[8,128]{1,0:T(8,128)S(1)}, f32[8,128]{1,0:T(8,128)}, u32[]{:S(2)}) copy-start(f32[8,128]{1,0:T(8,128)} %get-tuple-element.16) | copy-start | bytes 12292
  3.7 29.7 %collective-permute-start.2 = (f32[624,384]{1,0:T(8,128)}, f32[624,384]{1,0:T(8,128)S(1)}, u32[]{:S(2)}, u32[]{:S(2)}) collective-permute-start(f32[624,384]{1,0:T(8,128)} %get-tuple-element.15), channel_id=1, source_target_pairs={{0,1},{1,0},{2,3},{3,2},{4,5},{5,4},{6,7},{7,6},{8,9},{9,8},{10,11... | collective-permute-start | bytes 2875400 | tf_op jit(solution)/shard_map/ppermute | solution.py:692
  4.5 2.6 %copy-start.3 = (s32[4,7]{1,0:T(4,128)S(1)}, s32[4,7]{1,0:T(4,128)}, u32[]{:S(2)}) copy-start(s32[4,7]{1,0:T(4,128)} %mask.5) | copy-start | bytes 340
  4.5 28.9 %collective-permute-start = (f32[688,128]{1,0:T(8,128)}, f32[688,128]{1,0:T(8,128)S(1)}, u32[]{:S(2)}, u32[]{:S(2)}) collective-permute-start(f32[688,128]{1,0:T(8,128)} %get-tuple-element.13), channel_id=1, source_target_pairs={{0,255},{1,2},{2,1},{3,4},{4,3},{5,6},{6,5},{7,8},{8,7},{9,10},{10... | collective-permute-start | bytes 1056776 | tf_op jit(solution)/shard_map/ppermute | solution.py:690
  5.0 28.4 %collective-permute-start.1 = (f32[656,256]{1,0:T(8,128)}, f32[656,256]{1,0:T(8,128)S(1)}, u32[]{:S(2)}, u32[]{:S(2)}) collective-permute-start(f32[656,256]{1,0:T(8,128)} %get-tuple-element.14), channel_id=1, source_target_pairs={{0,254},{1,3},{2,0},{3,5},{4,2},{5,7},{6,4},{7,9},{8,6},{9,11},{10... | collective-permute-start | bytes 2015240 | tf_op jit(solution)/shard_map/ppermute | solution.py:691
  7.0 22.0 %collective-permute-start.3 = (f32[8,128]{1,0:T(8,128)S(1)}, f32[8,128]{1,0:T(8,128)S(1)}, u32[]{:S(2)}, u32[]{:S(2)}) collective-permute-start(f32[8,128]{1,0:T(8,128)S(1)} %copy-done.6), channel_id=1, source_target_pairs={{254,0},{3,1},{0,2},{5,3},{2,4},{7,5},{4,6},{9,7},{6,8},{11,9},{8,... | collective-permute-start | bytes 12296 | tf_op jit(solution)/shard_map/ppermute | solution.py:689
  27.9 1.0 copy-start.4
  33.4 1.2 %copy-start.5 = (f32[512,512]{1,0:T(8,128)S(1)}, f32[512,512]{1,0:T(8,128)}, u32[]{:S(2)}) copy-start(f32[512,512]{1,0:T(8,128)} %copy-done.4) | copy-start | bytes 3145732
  74.1 39.3 %collective-permute-start.5 = (f32[512,384]{1,0:T(8,128)S(1)}, f32[512,384]{1,0:T(8,128)S(1)}, u32[]{:S(2)}, u32[]{:S(2)}) collective-permute-start(f32[512,384]{1,0:T(8,128)S(1)} %get-tuple-element.19.after), channel_id=1, source_target_pairs={{0,255},{1,2},{2,1},{3,4},{4,3},{5,6},{6,5},{7,8},{8,7},{9,10},{10... | collective-permute-start | bytes 2359304 | tf_op jit(solution)/shard_map/ppermute | solution.py:702
  76.0 37.4 %collective-permute-start.4 = (f32[512,512]{1,0:T(8,128)S(1)}, f32[512,512]{1,0:T(8,128)S(1)}, u32[]{:S(2)}, u32[]{:S(2)}) collective-permute-start(f32[512,512]{1,0:T(8,128)S(1)} %get-tuple-element.20), channel_id=1, source_target_pairs={{254,0},{3,1},{0,2},{5,3},{2,4},{7,5},{4,6},{9,7},{6,8},{11,9},{8,... | collective-permute-start | bytes 3145736 | tf_op jit(solution)/shard_map/ppermute | solution.py:703

commit v5 on v4

--- a/solution.py
+++ b/solution.py
@@ -364,7 +364,18 @@
 
 def shares(load_near, load_far):
     goal = lax.div(FULL + load_near + load_far + 1, 3)
-    return jnp.clip(goal - load_near, 6, 9), jnp.clip(goal - load_far, 0, 8)
+    near = jnp.clip(goal - load_near, 3, 7)
+    far = jnp.clip(lax.div(FULL - near + load_far + 1, 2) - load_far, 0, 8)
+    return near, far
+
+
+def is_near(u, v, share):
+    option = jnp.where(u == -1, v, jnp.where(u == 0, 2 + v, FULL))
+    return (u < -1) | ((v < 2) & (option < share - 3))
+
+
+def is_far(u, v, share):
+    return (jnp.where(u == 3, v, jnp.where(u == 2, TPB + v, FULL))) < share
 
 
 PACK_COPIES = 5
@@ -483,16 +494,27 @@
             out[g * NRHS : (g + 1) * NRHS, col * BLK : (col + 1) * BLK] = acc[b, :, g * BLK : (g + 1) * BLK]
 
 
-def first_kernel(mask, test, panels, currents, out, *scratch):
+FIRST = 5
+
+
+def first_kernel(mask, test, panels, currents, out, done, *scratch):
+    scratch = scratch[:-1]
     even = is_even()
     full = load_of(mask) == FULL
     fill_tests(scratch[1], 0, own_tests(test))
     clear(scratch[12], TPB)
 
-    def wanted(n, b):
-        return (full & (mirrored(even, n) == 1)) | (jnp.logical_not(full) & (n == b))
-
-    engine(scratch, TPB, wanted, lambda n: fill(scratch, panels, currents, 0, n), lambda n: 0)
+    def plan(i, used):
+        n, b = lax.div(i, TPB), lax.rem(i, TPB)
+        u, v = mirrored(even, n), mirrored(even, b)
+        dense = (u == 1) | ((u == 0) & (v == 3))
+        wanted = (full & dense) | (jnp.logical_not(full) & (mask[b, n - b + REACH] > 0))
+        now = wanted & (used < FIRST)
+        done[n, b] = now.astype(jnp.int32)
+        return used + now.astype(jnp.int32)
+
+    lax.fori_loop(0, TPB * TPB, plan, jnp.int32(0))
+    engine(scratch, TPB, lambda n, b: done[n, b] > 0, lambda n: fill(scratch, panels, currents, 0, n), lambda n: 0)
     write_out(out, scratch[12], range(TPB))
 
 
@@ -520,7 +542,7 @@
 
 
 def second_kernel(
-    mask, test, panels, currents, outer, far, mate, load_far, part, out_near, out_far, out_own, todo, *scratch
+    mask, done, test, panels, currents, outer, far, mate, load_far, part, out_near, out_far, out_own, todo, *scratch
 ):
     plan, scratch = scratch[-1], scratch[:-1]
     even = is_even()
@@ -549,10 +571,10 @@
     def plan_help(i, used):
         n, b = lax.div(i, TPB), lax.rem(i, TPB)
         v_near, v_far = mirrored(odd, b), mirrored(even, b)
-        of_own = (n < 3) & (v_near <= 2 - n)
-        of_outer = (n == 3) & (v_near < share_near - 6)
-        of_far = (n > 3) & ((n - 4) * TPB + v_far < share_far)
-        wanted = ((near_load == FULL) & (of_own | of_outer)) | ((far_load == FULL) & of_far)
+        u_near, u_far = jnp.where(n == 3, 0, -1 - n), 7 - n
+        of_near = (n < 4) & (v_near - u_near <= REACH) & is_near(u_near, v_near, share_near)
+        of_far = (n >= 4) & is_far(u_far, v_far, share_far)
+        wanted = ((near_load == FULL) & of_near) | ((far_load == FULL) & of_far)
         plan[i] = wanted.astype(jnp.int32)
         return used + wanted.astype(jnp.int32)
 
@@ -561,12 +583,11 @@
         rel = own_place(even, n)
         column = rel - b + REACH
         inside = (column >= 0) & (column < SPAN)
-        sparse = inside & (mask[b, jnp.clip(column, 0, SPAN - 1)] > 0) & (rel != b)
+        sparse = inside & (mask[b, jnp.clip(column, 0, SPAN - 1)] > 0)
         u, v = mirrored(even, rel), mirrored(even, b)
-        given = (u == 1) | ((u == 0) & (v < give_near - 6))
-        given = given | ((u == 3) & (v < give_far)) | ((u == 2) & (TPB + v < give_far))
-        dense = inside & (u >= 0) & jnp.logical_not(given)
-        wanted = (full & dense) | (jnp.logical_not(full) & sparse)
+        dense = inside & jnp.logical_not(is_near(u, v, give_near) | is_far(u, v, give_far))
+        earlier = (n < TPB) & (done[jnp.minimum(n, TPB - 1), b] > 0)
+        wanted = ((full & dense) | (jnp.logical_not(full) & sparse)) & jnp.logical_not(earlier)
         now = wanted & (used < QUOTA)
         plan[HELP_STEPS * TPB + i] = now.astype(jnp.int32)
         todo[n, b] = (wanted & jnp.logical_not(now)).astype(jnp.int32)
@@ -599,8 +620,8 @@
         load_source,
         lambda n: jnp.where(n < 4, 0, jnp.where(n < HELP_STEPS, 1, 2)),
     )
-    shift = jnp.where(even, 1, 0)
-    write_out(out_near, acc, [b + shift for b in range(TPB - 1)])
+    shift = jnp.where(even, 2, 0)
+    write_out(out_near, acc, [b + shift for b in range(2)])
     write_out(out_far, acc, range(TPB, 2 * TPB))
     write_out(out_own, acc, range(2 * TPB, 3 * TPB))
 
@@ -641,11 +662,11 @@
     ]
 
 
-def call(kernel, outs, operands, sets=0, unread=0, tiles=1, table=False, copies=0):
+def call(kernel, outs, operands, sets=0, tables=1, unread=0, tiles=1, table=(), copies=0):
     vmem = pl.BlockSpec(memory_space=pltpu.VMEM)
     smem = pl.BlockSpec(memory_space=pltpu.SMEM)
     anywhere = pl.BlockSpec(memory_space=pl.ANY)
-    plain = len(operands) - 1 - unread
+    plain = len(operands) - tables - unread
     shapes = [jax.ShapeDtypeStruct(s, F32) for s in outs]
     specs = [vmem] * len(outs)
     scratch = scratch_for(sets) if sets else []
@@ -656,13 +677,13 @@
             pltpu.SemaphoreType.DMA((copies,)),
         ]
     if table:
-        shapes.append(jax.ShapeDtypeStruct((OWN_STEPS, TPB), jnp.int32))
+        shapes.append(jax.ShapeDtypeStruct(table, jnp.int32))
         specs.append(smem)
         scratch.append(pltpu.SMEM(((HELP_STEPS + OWN_STEPS) * TPB,), jnp.int32))
     return pl.pallas_call(
         kernel,
         out_shape=shapes,
-        in_specs=[smem] + [vmem] * plain + [anywhere] * unread,
+        in_specs=[smem] * tables + [vmem] * plain + [anywhere] * unread,
         out_specs=specs,
         scratch_shapes=scratch,
         compiler_params=pltpu.CompilerParams(vmem_limit_bytes=(60 if copies else 26) * 1024 * 1024),
@@ -690,14 +711,17 @@
     outer = lax.ppermute(outer, axes, across)
     far = lax.ppermute(far, axes, away)
     mate = lax.ppermute(mate, axes, swap)
-    (part,) = call(first_kernel, [(wide, width)], [near_mask, test_points, panels, currents], 1, tiles=4)
+    part, done = call(
+        first_kernel, [(wide, width)], [near_mask, test_points, panels, currents], 1, tiles=5, table=(TPB, TPB)
+    )
     to_near, to_far, part, todo = call(
         second_kernel,
-        [(wide, width - BLK), (wide, width), (wide, width)],
-        [near_mask, test_points, panels, currents, outer, far, mate, load_far, part],
+        [(wide, 2 * BLK), (wide, width), (wide, width)],
+        [near_mask, done, test_points, panels, currents, outer, far, mate, load_far, part],
         3,
+        tables=2,
         tiles=7,
-        table=True,
+        table=(OWN_STEPS, TPB),
     )
     from_near = lax.ppermute(to_near, axes, across)
     from_far = lax.ppermute(to_far, axes, back)
@@ -711,8 +735,8 @@
     )
     padded = jnp.where(
         lax.axis_index("narrow") == 0,
-        jnp.pad(from_near, ((0, 0), (0, BLK))),
-        jnp.pad(from_near, ((0, 0), (BLK, 0))),
+        jnp.pad(from_near, ((0, 0), (0, 2 * BLK))),
+        jnp.pad(from_near, ((0, 0), (2 * BLK, 0))),
     )
     return rest + from_far + padded
 

time: 115 us -> 107 us (0.930)
  the two profiles are of different devices: /device:TPU:74 before, /device:TPU:4 now
where the time goes in v5:
time: 107 us
  Pallas kernels  52.1 us (49%)
  waiting for transfers between devices  36.6 us (34%)
  starting transfers between devices  14.8 us (14%)
  local copies, waits for them, and re-layouts  2.2 us (2%)
  other arithmetic  1.27 us (1%)
    pallas_call x4, Pallas kernels, call(): pl.pallas_call(kernel, out_shape=shapes, in_specs=[smem] * tables + [vmem...  52.1 us
    ppermute x1, waiting for transfers between devices, body(): from_far = lax.ppermute(to_far, axes, back)  36.5 us
    ppermute x1, starting transfers between devices, body(): from_far = lax.ppermute(to_far, axes, back)  9.9 us
    unnamed x14, local copies, waits for them, and re-layouts  2.2 us
  transfers between devices with their start and end apart: 6, of which 1 were waited for; matrix products, arithmetic and copies ran while one was open for 0% of the time, Pallas kernels for 27%

profile of v5, /device:TPU:4, one launch (start us, length us, event | category | flops | bytes accessed | tf_op | source)
XLA Modules:
  0.0 107.0 jit_solution(16858057773854999871)
XLA Ops:
  0.0 0.0 copy-start.1
  0.0 0.0 copy-start.2
  0.0 0.0 copy-start
  0.0 3.8 %shard_map.47 = (f32[624,384]{1,0:T(8,128)}, f32[688,128]{1,0:T(8,128)}, f32[656,256]{1,0:T(8,128)}, f32[8,128]{1,0:T(8,128)}) custom-call(s32[4,7]{1,0:T(4,128)} %mask.5, f32[98,512]{1,0:T(8,128)} %panels.5, f32[14,512]{1,0:T(8,128)} %test.5, f32[512,512]{1,0:T(8,128)} %currents.7), custom_call_target="tpu_custom_call" | custom-call | flops 5000000000 | bytes 4000000 | tf_op jit(solution)/shard_map/pallas_call | solution.py:683
  3.8 0.0 copy-start.6
  3.9 1.2 %collective-permute-start.2 = (f32[624,384]{1,0:T(8,128)}, f32[624,384]{1,0:T(8,128)S(1)}, u32[]{:S(2)}, u32[]{:S(2)}) collective-permute-start(f32[624,384]{1,0:T(8,128)} %get-tuple-element.18), channel_id=1, source_target_pairs={{0,1},{1,0},{2,3},{3,2},{4,5},{5,4},{6,7},{7,6},{8,9},{9,8},{10,11... | collective-permute-start | bytes 2875400 | tf_op jit(solution)/shard_map/ppermute | solution.py:713
  5.0 0.0 copy-start.3
  5.0 1.6 %collective-permute-start = (f32[688,128]{1,0:T(8,128)}, f32[688,128]{1,0:T(8,128)S(1)}, u32[]{:S(2)}, u32[]{:S(2)}) collective-permute-start(f32[688,128]{1,0:T(8,128)} %get-tuple-element.16), channel_id=1, source_target_pairs={{0,255},{1,2},{2,1},{3,4},{4,3},{5,6},{6,5},{7,8},{8,7},{9,10},{10... | collective-permute-start | bytes 1056776 | tf_op jit(solution)/shard_map/ppermute | solution.py:711
  6.6 2.0 %collective-permute-start.1 = (f32[656,256]{1,0:T(8,128)}, f32[656,256]{1,0:T(8,128)S(1)}, u32[]{:S(2)}, u32[]{:S(2)}) collective-permute-start(f32[656,256]{1,0:T(8,128)} %get-tuple-element.17), channel_id=1, source_target_pairs={{0,254},{1,3},{2,0},{3,5},{4,2},{5,7},{6,4},{7,9},{8,6},{9,11},{10... | collective-permute-start | bytes 2015240 | tf_op jit(solution)/shard_map/ppermute | solution.py:712
  8.7 0.0 copy-done.6
  8.7 0.0 collective-permute-start.3
  8.7 0.0 copy-done.1
  8.7 0.0 copy-done.2
  8.7 0.0 copy-done
  8.7 0.0 copy-done.3
  8.7 27.7 %shard_map.46 = (f32[512,512]{1,0:T(8,128)S(1)}, s32[4,4]{1,0:T(4,128)S(1)}) custom-call(s32[4,7]{1,0:T(4,128)S(1)} %copy-done.3, f32[14,512]{1,0:T(8,128)S(1)} %copy-done.2, f32[98,512]{1,0:T(8,128)S(1)} %copy-done.1, f32[512,512]{1,0:T(8,128)S(1)} %copy-done), custom_call_target="tpu_custom_call" | custom-call | flops 24999999488 | bytes 4000000 | tf_op jit(solution)/shard_map/pallas_call | solution.py:683
  36.4 0.0 copy-start.4
  36.4 1.0 copy-done.4
  37.4 0.0 collective-permute-done.3.load_far
  37.4 0.0 collective-permute-done.outer
  37.4 0.0 collective-permute-done.1.far
  37.4 0.0 collective-permute-done.2.mate
  37.4 0.0 copy-start.5
  37.4 1.2 %copy-done.5 = f32[512,512]{1,0:T(8,128)S(1)} copy-done((f32[512,512]{1,0:T(8,128)S(1)}, f32[512,512]{1,0:T(8,128)}, u32[]{:S(2)}) %copy-start.5) | copy-done | bytes 1048600
  38.6 19.4 %shard_map.48 = (f32[512,256]{1,0:T(8,128)S(1)}, f32[512,512]{1,0:T(8,128)S(1)}, f32[512,512]{1,0:T(8,128)S(1)}, s32[8,4]{1,0:T(8,128)S(1)}) custom-call(s32[4,7]{1,0:T(4,128)S(1)} %copy-done.3, s32[4,4]{1,0:T(4,128)S(1)} %get-tuple-element.15.done, f32[14,512]{1,0:T(8,128)S(1)} %copy-done.2, f32[98,512]{1,0:T(8,128)S(1)} %copy-done.1, ...), custom_call_target="tpu_custom_call" | custom-call | flops 35000000512 | bytes 4000000 | tf_op jit(solution)/shard_map/pallas_call | solution.py:683
  58.1 0.1 collective-permute-start.5
  58.2 9.9 %collective-permute-start.4 = (f32[512,512]{1,0:T(8,128)S(1)}, f32[512,512]{1,0:T(8,128)S(1)}, u32[]{:S(2)}, u32[]{:S(2)}) collective-permute-start(f32[512,512]{1,0:T(8,128)S(1)} %get-tuple-element.24), channel_id=1, source_target_pairs={{254,0},{3,1},{0,2},{5,3},{2,4},{7,5},{4,6},{9,7},{6,8},{11,9},{8,... | collective-permute-start | bytes 3145736 | tf_op jit(solution)/shard_map/ppermute | solution.py:727
  68.1 1.1 %shard_map.49 = f32[512,512]{1,0:T(8,128)S(1)} custom-call(s32[8,4]{1,0:T(8,128)S(1)} %get-tuple-element.21.todo, f32[14,512]{1,0:T(8,128)S(1)} %copy-done.2, f32[98,512]{1,0:T(8,128)S(1)} %copy-done.1, f32[512,512]{1,0:T(8,128)S(1)} %copy-done, f32[688,128]{1,0:T(8,128)S(1)} %collective-permute-done.outer, f32[624,384]{1,0:T(8,128)S(1)} %collective-permute-done.2.mate, ...), custom_call_target="tpu_custom_call" | custom-call | flops 40000000000 | bytes 4000000 | tf_op jit(solution)/shard_map/pallas_call | solution.py:683
  69.2 0.0 collective-permute-done.5
  69.2 36.5 %collective-permute-done.4 = f32[512,512]{1,0:T(8,128)S(1)} collective-permute-done((f32[512,512]{1,0:T(8,128)S(1)}, f32[512,512]{1,0:T(8,128)S(1)}, u32[]{:S(2)}, u32[]{:S(2)}) %collective-permute-start.4) | collective-permute-done | bytes 1048608 | tf_op jit(solution)/shard_map/ppermute | solution.py:727
  105.8 1.3 %select_add_fusion = f32[512,512]{1,0:T(8,128)} fusion(f32[512,256]{1,0:T(8,128)S(1)} %collective-permute-done.5, f32[512,512]{1,0:T(8,128)S(1)} %shard_map.49, f32[512,512]{1,0:T(8,128)S(1)} %collective-permute-done.4, pred[]{:T(512)S(6)} %eq.3), kind=kLoop, calls=%fused_computation | loop fusion | flops 786432 | bytes 3670017 | tf_op jit(solution)/shard_map/add | solution.py:741
Async XLA Ops:
  0.0 8.7 %copy-start.1 = (f32[98,512]{1,0:T(8,128)S(1)}, f32[98,512]{1,0:T(8,128)}, u32[]{:S(2)}) copy-start(f32[98,512]{1,0:T(8,128)} %panels.5) | copy-start | bytes 602116
  0.0 8.7 %copy-start.2 = (f32[14,512]{1,0:T(8,128)S(1)}, f32[14,512]{1,0:T(8,128)}, u32[]{:S(2)}) copy-start(f32[14,512]{1,0:T(8,128)} %test.5) | copy-start | bytes 86020
  0.0 8.7 %copy-start = (f32[512,512]{1,0:T(8,128)S(1)}, f32[512,512]{1,0:T(8,128)}, u32[]{:S(2)}) copy-start(f32[512,512]{1,0:T(8,128)} %currents.7) | copy-start | bytes 3145732
  3.8 4.8 %copy-start.6 = (f32[8,128]{1,0:T(8,128)S(1)}, f32[8,128]{1,0:T(8,128)}, u32[]{:S(2)}) copy-start(f32[8,128]{1,0:T(8,128)} %get-tuple-element.19) | copy-start | bytes 12292
  3.9 33.5 %collective-permute-start.2 = (f32[624,384]{1,0:T(8,128)}, f32[624,384]{1,0:T(8,128)S(1)}, u32[]{:S(2)}, u32[]{:S(2)}) collective-permute-start(f32[624,384]{1,0:T(8,128)} %get-tuple-element.18), channel_id=1, source_target_pairs={{0,1},{1,0},{2,3},{3,2},{4,5},{5,4},{6,7},{7,6},{8,9},{9,8},{10,11... | collective-permute-start | bytes 2875400 | tf_op jit(solution)/shard_map/ppermute | solution.py:713
  5.0 3.7 %copy-start.3 = (s32[4,7]{1,0:T(4,128)S(1)}, s32[4,7]{1,0:T(4,128)}, u32[]{:S(2)}) copy-start(s32[4,7]{1,0:T(4,128)} %mask.5) | copy-start | bytes 340
  5.0 32.4 %collective-permute-start = (f32[688,128]{1,0:T(8,128)}, f32[688,128]{1,0:T(8,128)S(1)}, u32[]{:S(2)}, u32[]{:S(2)}) collective-permute-start(f32[688,128]{1,0:T(8,128)} %get-tuple-element.16), channel_id=1, source_target_pairs={{0,255},{1,2},{2,1},{3,4},{4,3},{5,6},{6,5},{7,8},{8,7},{9,10},{10... | collective-permute-start | bytes 1056776 | tf_op jit(solution)/shard_map/ppermute | solution.py:711
  6.6 30.7 %collective-permute-start.1 = (f32[656,256]{1,0:T(8,128)}, f32[656,256]{1,0:T(8,128)S(1)}, u32[]{:S(2)}, u32[]{:S(2)}) collective-permute-start(f32[656,256]{1,0:T(8,128)} %get-tuple-element.17), channel_id=1, source_target_pairs={{0,254},{1,3},{2,0},{3,5},{4,2},{5,7},{6,4},{7,9},{8,6},{9,11},{10... | collective-permute-start | bytes 2015240 | tf_op jit(solution)/shard_map/ppermute | solution.py:712
  8.7 28.7 %collective-permute-start.3 = (f32[8,128]{1,0:T(8,128)S(1)}, f32[8,128]{1,0:T(8,128)S(1)}, u32[]{:S(2)}, u32[]{:S(2)}) collective-permute-start(f32[8,128]{1,0:T(8,128)S(1)} %copy-done.6), channel_id=1, source_target_pairs={{254,0},{3,1},{0,2},{5,3},{2,4},{7,5},{4,6},{9,7},{6,8},{11,9},{8,... | collective-permute-start | bytes 12296 | tf_op jit(solution)/shard_map/ppermute | solution.py:710
  36.4 1.0 copy-start.4
  37.4 1.2 %copy-start.5 = (f32[512,512]{1,0:T(8,128)S(1)}, f32[512,512]{1,0:T(8,128)}, u32[]{:S(2)}) copy-start(f32[512,512]{1,0:T(8,128)} %copy-done.4) | copy-start | bytes 3145732
  58.1 11.2 %collective-permute-start.5 = (f32[512,256]{1,0:T(8,128)S(1)}, f32[512,256]{1,0:T(8,128)S(1)}, u32[]{:S(2)}, u32[]{:S(2)}) collective-permute-start(f32[512,256]{1,0:T(8,128)S(1)} %get-tuple-element.23.after), channel_id=1, source_target_pairs={{0,255},{1,2},{2,1},{3,4},{4,3},{5,6},{6,5},{7,8},{8,7},{9,10},{10... | collective-permute-start | bytes 1572872 | tf_op jit(solution)/shard_map/ppermute | solution.py:726
  58.2 47.6 %collective-permute-start.4 = (f32[512,512]{1,0:T(8,128)S(1)}, f32[512,512]{1,0:T(8,128)S(1)}, u32[]{:S(2)}, u32[]{:S(2)}) collective-permute-start(f32[512,512]{1,0:T(8,128)S(1)} %get-tuple-element.24), channel_id=1, source_target_pairs={{254,0},{3,1},{0,2},{5,3},{2,4},{7,5},{4,6},{9,7},{6,8},{11,9},{8,... | collective-permute-start | bytes 3145736 | tf_op jit(solution)/shard_map/ppermute | solution.py:727

commit v6 on v5

--- a/solution.py
+++ b/solution.py
@@ -337,7 +337,7 @@
 XROW = CROW + 4 * NRHS
 OUTER_ROWS = XROW + 64 + 8
 FAR_ROWS = XROW + 32 + 8
-MATE_ROWS = XROW + 8
+MATE_ROWS = XROW
 FULL = TPB * SPAN
 
 
@@ -362,26 +362,26 @@
     return jnp.max(ref[row : row + 8, 0:BLK]).astype(jnp.int32)
 
 
-def shares(load_near, load_far):
-    goal = lax.div(FULL + load_near + load_far + 1, 3)
-    near = jnp.clip(goal - load_near, 3, 7)
-    far = jnp.clip(lax.div(FULL - near + load_far + 1, 2) - load_far, 0, 8)
-    return near, far
-
-
-def is_near(u, v, share):
+def share(load):
+    return jnp.clip(lax.div(FULL - 2 * SIDE + load + 1, 2) - load, 3, 7)
+
+
+SIDE = 4
+
+
+def is_near(u, v, given):
     option = jnp.where(u == -1, v, jnp.where(u == 0, 2 + v, FULL))
-    return (u < -1) | ((v < 2) & (option < share - 3))
-
-
-def is_far(u, v, share):
-    return (jnp.where(u == 3, v, jnp.where(u == 2, TPB + v, FULL))) < share
+    return (u < -1) | ((v < 2) & (option < given - 3))
+
+
+def is_side(u):
+    return (u == 2) | (u == 3)
 
 
 PACK_COPIES = 5
 
 
-def pack_kernel(mask, panels_at, test_at, currents, mate, outer, far, load, panels, test, sems):
+def pack_kernel(mask, panels_at, test_at, currents, mate, outer, far, panels, test, sems):
     even = is_even()
     places = (
         (outer, 1, jnp.where(even, 0, 3 * BLK)),
@@ -397,8 +397,6 @@
     value = load_of(mask).astype(F32)
     outer[XROW + 64 : XROW + 72, :] = jnp.full((8, BLK), value, F32)
     far[XROW + 32 : XROW + 40, :] = jnp.full((8, 2 * BLK), value, F32)
-    mate[XROW : XROW + 8, :] = jnp.full((8, 3 * BLK), value, F32)
-    load[...] = jnp.full((8, BLK), value, F32)
     copies[0].wait()
     copies[1].wait()
     for k in range(3):
@@ -507,7 +505,7 @@
     def plan(i, used):
         n, b = lax.div(i, TPB), lax.rem(i, TPB)
         u, v = mirrored(even, n), mirrored(even, b)
-        dense = (u == 1) | ((u == 0) & (v == 3))
+        dense = (u == 1) | ((u == 0) & (v == 2))
         wanted = (full & dense) | (jnp.logical_not(full) & (mask[b, n - b + REACH] > 0))
         now = wanted & (used < FIRST)
         done[n, b] = now.astype(jnp.int32)
@@ -519,7 +517,7 @@
 
 
 QUOTA = 7
-HELP_STEPS = 6
+HELP_STEPS = 8
 OWN_STEPS = 8
 
 
@@ -542,39 +540,36 @@
 
 
 def second_kernel(
-    mask, done, test, panels, currents, outer, far, mate, load_far, part, out_near, out_far, out_own, todo, *scratch
+    mask, done, test, panels, currents, outer, far, wing, mate, out_near, out_far, out_wing, out_own, todo, *scratch
 ):
     plan, scratch = scratch[-1], scratch[:-1]
     even = is_even()
     odd = jnp.logical_not(even)
-    own_load, mate_load = load_of(mask), number(mate, XROW)
-    near_load, far_load = number(outer, XROW + 64), number(far, XROW + 32)
-    share_near, _ = shares(own_load, mate_load)
-    _, share_far = shares(mate_load, own_load)
-    give_near, give_far = shares(near_load, number(load_far, 0))
-    full = own_load == FULL
+    own_load, near_load = load_of(mask), number(outer, XROW + 64)
+    far_full, wing_full = number(far, XROW + 32) == FULL, number(wing, XROW + 32) == FULL
+    near_full, full = near_load == FULL, own_load == FULL
+    take, give = share(own_load), share(near_load)
     xt, acc = scratch[1], scratch[12]
     fill_tests(xt, 0, lambda b, row: outer[XROW + 16 * b + row : XROW + 16 * b + row + 2, :])
-    fill_tests(
-        xt,
-        1,
-        lambda b, row: far[
-            XROW + 16 * (b // 2) + row : XROW + 16 * (b // 2) + row + 2, (b % 2) * BLK : (b % 2 + 1) * BLK
-        ],
-    )
-    fill_tests(xt, 2, own_tests(test))
-    clear(acc, 2 * TPB)
-    for b in range(TPB):
-        for g in range(4):
-            acc[2 * TPB + b, :, g * BLK : (g + 1) * BLK] = part[g * NRHS : (g + 1) * NRHS, b * BLK : (b + 1) * BLK]
+    for which, ref in ((1, far), (2, wing)):
+        fill_tests(
+            xt,
+            which,
+            lambda b, row, ref=ref: ref[
+                XROW + 16 * (b // 2) + row : XROW + 16 * (b // 2) + row + 2, (b % 2) * BLK : (b % 2 + 1) * BLK
+            ],
+        )
+    fill_tests(xt, 3, own_tests(test))
+    clear(acc, 4 * TPB)
 
     def plan_help(i, used):
         n, b = lax.div(i, TPB), lax.rem(i, TPB)
-        v_near, v_far = mirrored(odd, b), mirrored(even, b)
-        u_near, u_far = jnp.where(n == 3, 0, -1 - n), 7 - n
-        of_near = (n < 4) & (v_near - u_near <= REACH) & is_near(u_near, v_near, share_near)
-        of_far = (n >= 4) & is_far(u_far, v_far, share_far)
-        wanted = ((near_load == FULL) & of_near) | ((far_load == FULL) & of_far)
+        v_near, v_side = mirrored(odd, b), mirrored(even, b)
+        u_near = jnp.where(n == 3, 0, -1 - n)
+        of_near = (n < 4) & (v_near - u_near <= REACH) & is_near(u_near, v_near, take)
+        of_far = ((n == 4) | (n == 5)) & (v_side >= 2)
+        of_wing = (n >= 6) & (v_side < 2)
+        wanted = (near_full & of_near) | (far_full & of_far) | (wing_full & of_wing)
         plan[i] = wanted.astype(jnp.int32)
         return used + wanted.astype(jnp.int32)
 
@@ -585,7 +580,7 @@
         inside = (column >= 0) & (column < SPAN)
         sparse = inside & (mask[b, jnp.clip(column, 0, SPAN - 1)] > 0)
         u, v = mirrored(even, rel), mirrored(even, b)
-        dense = inside & jnp.logical_not(is_near(u, v, give_near) | is_far(u, v, give_far))
+        dense = inside & jnp.logical_not(is_near(u, v, give) | is_side(u))
         earlier = (n < TPB) & (done[jnp.minimum(n, TPB - 1), b] > 0)
         wanted = ((full & dense) | (jnp.logical_not(full) & sparse)) & jnp.logical_not(earlier)
         now = wanted & (used < QUOTA)
@@ -605,9 +600,13 @@
         def _():
             fill(scratch, outer, outer, CROW, 0)
 
-        @pl.when((n > 3) & (n < HELP_STEPS))
+        @pl.when((n == 4) | (n == 5))
         def _():
-            fill(scratch, far, far, CROW, jnp.where(even, 5 - n, n - 4))
+            fill(scratch, far, far, CROW, n - 4)
+
+        @pl.when((n == 6) | (n == 7))
+        def _():
+            fill(scratch, wing, wing, CROW, n - 6)
 
         @pl.when(n >= HELP_STEPS)
         def _():
@@ -618,20 +617,21 @@
         HELP_STEPS + OWN_STEPS,
         lambda n, b: plan[n * TPB + b] > 0,
         load_source,
-        lambda n: jnp.where(n < 4, 0, jnp.where(n < HELP_STEPS, 1, 2)),
+        lambda n: jnp.where(n < 4, 0, jnp.where(n < 6, 1, jnp.where(n < 8, 2, 3))),
     )
     shift = jnp.where(even, 2, 0)
     write_out(out_near, acc, [b + shift for b in range(2)])
-    write_out(out_far, acc, range(TPB, 2 * TPB))
-    write_out(out_own, acc, range(2 * TPB, 3 * TPB))
-
-
-def rest_kernel(todo, test, panels, currents, outer, mate, part, after, out, *scratch):
+    shift_side = 2 - shift
+    back = shift
+    write_out(out_far, acc, [TPB + b + back for b in range(2)])
+    write_out(out_wing, acc, [2 * TPB + b + shift_side for b in range(2)])
+    write_out(out_own, acc, range(3 * TPB, 4 * TPB))
+
+
+def rest_kernel(todo, test, panels, currents, outer, mate, after, out, *scratch):
     acc = scratch[12]
     fill_tests(scratch[1], 0, own_tests(test))
-    for b in range(TPB):
-        for g in range(4):
-            acc[b, :, g * BLK : (g + 1) * BLK] = part[g * NRHS : (g + 1) * NRHS, b * BLK : (b + 1) * BLK]
+    clear(acc, TPB)
     engine(
         scratch,
         OWN_STEPS,
@@ -686,7 +686,7 @@
         in_specs=[smem] * tables + [vmem] * plain + [anywhere] * unread,
         out_specs=specs,
         scratch_shapes=scratch,
-        compiler_params=pltpu.CompilerParams(vmem_limit_bytes=(60 if copies else 26) * 1024 * 1024),
+        compiler_params=pltpu.CompilerParams(vmem_limit_bytes=(60 if copies else 20) * 1024 * 1024),
         cost_estimate=pl.CostEstimate(flops=tiles * 5 * 10**9, bytes_accessed=4 * 10**6, transcendentals=0),
     )(*operands)
 
@@ -697,48 +697,52 @@
     swap = [(i, i ^ 1) for i in range(count)]
     across = [(i, (i - 1) % count if i % 2 == 0 else (i + 1) % count) for i in range(count)]
     away = [(i, (i - 2) % count if i % 2 == 0 else (i + 2) % count) for i in range(count)]
-    back = [(target, source) for source, target in away]
+    across_wing = [(i, (i - 4) % count if i % 2 == 0 else (i + 4) % count) for i in range(count)]
     width = TPB * BLK
     wide = 4 * NRHS
-    mate, outer, far, load = call(
+    half = (wide, 2 * BLK)
+
+    def reverse(pairs):
+        return [(target, source) for source, target in pairs]
+
+    mate, outer, far = call(
         pack_kernel,
-        [(MATE_ROWS, 3 * BLK), (OUTER_ROWS, BLK), (FAR_ROWS, 2 * BLK), (8, BLK)],
+        [(MATE_ROWS, 3 * BLK), (OUTER_ROWS, BLK), (FAR_ROWS, 2 * BLK)],
         [near_mask, panels, test_points, currents],
         unread=3,
         copies=PACK_COPIES,
     )
-    load_far = lax.ppermute(load, axes, back)
     outer = lax.ppermute(outer, axes, across)
+    wing = lax.ppermute(far, axes, across_wing)
     far = lax.ppermute(far, axes, away)
     mate = lax.ppermute(mate, axes, swap)
     part, done = call(
         first_kernel, [(wide, width)], [near_mask, test_points, panels, currents], 1, tiles=5, table=(TPB, TPB)
     )
-    to_near, to_far, part, todo = call(
+    to_near, to_far, to_wing, more, todo = call(
         second_kernel,
-        [(wide, 2 * BLK), (wide, width), (wide, width)],
-        [near_mask, done, test_points, panels, currents, outer, far, mate, load_far, part],
-        3,
+        [half, half, half, (wide, width)],
+        [near_mask, done, test_points, panels, currents, outer, far, wing, mate],
+        4,
         tables=2,
         tiles=7,
         table=(OWN_STEPS, TPB),
     )
     from_near = lax.ppermute(to_near, axes, across)
-    from_far = lax.ppermute(to_far, axes, back)
+    from_far = lax.ppermute(to_far, axes, reverse(away))
+    from_wing = lax.ppermute(to_wing, axes, reverse(across_wing))
     (rest,) = call(
         rest_kernel,
         [(wide, width)],
-        [todo, test_points, panels, currents, outer, mate, part, to_near],
+        [todo, test_points, panels, currents, outer, mate, to_near],
         1,
         unread=1,
         tiles=8,
     )
-    padded = jnp.where(
-        lax.axis_index("narrow") == 0,
-        jnp.pad(from_near, ((0, 0), (0, 2 * BLK))),
-        jnp.pad(from_near, ((0, 0), (2 * BLK, 0))),
-    )
-    return rest + from_far + padded
+    even = lax.axis_index("narrow") == 0
+    inner = from_near + from_wing
+    helped = jnp.concatenate([jnp.where(even, inner, from_far), jnp.where(even, from_far, inner)], 1)
+    return part + more + rest + helped
 
 
 def solution(mesh):

time: 107 us -> 131 us (1.22)
  the two profiles are of different devices: /device:TPU:4 before, /device:TPU:5 now
where the time goes in v6:
time: 131 us; the launch traced here: 129 us
  Pallas kernels  79.3 us (61%)
  waiting for transfers between devices  32.8 us (25%)
  starting transfers between devices  14.5 us (11%)
  other arithmetic  1.53 us (1%)
    pallas_call x4, Pallas kernels, call(): pl.pallas_call(kernel, out_shape=shapes, in_specs=[smem] * tables + [vmem...  79.3 us
    ppermute x1, waiting for transfers between devices, body(): from_near = lax.ppermute(to_near, axes, across)  19.6 us
    ppermute x1, waiting for transfers between devices, body(): mate = lax.ppermute(mate, axes, swap)  11.2 us
    ppermute x1, starting transfers between devices, body(): from_near = lax.ppermute(to_near, axes, across)  8.68 us
    ppermute x1, starting transfers between devices, body(): wing = lax.ppermute(far, axes, across_wing)  2.75 us
  transfers between devices with their start and end apart: 7, of which 4 were waited for; matrix products, arithmetic and copies ran while one was open for 0% of the time, Pallas kernels for 27%

profile of v6, /device:TPU:5, one launch (start us, length us, event | category | flops | bytes accessed | tf_op | source)
XLA Modules:
  0.0 129.2 jit_solution(18120463642956613654)
XLA Ops:
  0.0 0.0 copy-start
  0.0 0.0 copy-start.3
  0.0 0.0 copy-start.1
  0.0 3.7 %shard_map.47 = (f32[616,384]{1,0:T(8,128)}, f32[688,128]{1,0:T(8,128)}, f32[656,256]{1,0:T(8,128)}) custom-call(s32[4,7]{1,0:T(4,128)} %mask.5, f32[98,512]{1,0:T(8,128)} %panels.5, f32[14,512]{1,0:T(8,128)} %test.5, f32[512,512]{1,0:T(8,128)} %currents.7), custom_call_target="tpu_custom_call" | custom-call | flops 5000000000 | bytes 4000000 | tf_op jit(solution)/shard_map/pallas_call | solution.py:683
  3.7 0.0 copy-start.4
  3.7 2.8 %collective-permute-start.2 = (f32[656,256]{1,0:T(8,128)}, f32[656,256]{1,0:T(8,128)}, u32[]{:S(2)}, u32[]{:S(2)}) collective-permute-start(f32[656,256]{1,0:T(8,128)} %get-tuple-element.18), channel_id=1, source_target_pairs={{0,252},{1,5},{2,254},{3,7},{4,0},{5,9},{6,2},{7,11},{8,4},{9,13},... | collective-permute-start | bytes 2015240 | tf_op jit(solution)/shard_map/ppermute | solution.py:716
  6.5 1.0 collective-permute-start.1
  7.4 0.0 collective-permute-start
  7.5 2.0 %collective-permute-start.3 = (f32[616,384]{1,0:T(8,128)}, f32[616,384]{1,0:T(8,128)S(1)}, u32[]{:S(2)}, u32[]{:S(2)}) collective-permute-start(f32[616,384]{1,0:T(8,128)} %get-tuple-element.19), channel_id=1, source_target_pairs={{0,1},{1,0},{2,3},{3,2},{4,5},{5,4},{6,7},{7,6},{8,9},{9,8},{10,11... | collective-permute-start | bytes 2838536 | tf_op jit(solution)/shard_map/ppermute | solution.py:718
  9.4 0.0 copy-done
  9.4 0.0 copy-done.3
  9.4 0.0 copy-done.1
  9.4 0.0 copy-done.4
  9.4 27.7 %shard_map.46 = (f32[512,512]{1,0:T(8,128)S(1)}, s32[4,4]{1,0:T(4,128)S(1)}) custom-call(s32[4,7]{1,0:T(4,128)S(1)} %copy-done.4, f32[14,512]{1,0:T(8,128)S(1)} %copy-done.3, f32[98,512]{1,0:T(8,128)S(1)} %copy-done.1, f32[512,512]{1,0:T(8,128)S(1)} %copy-done), custom_call_target="tpu_custom_call" | custom-call | flops 24999999488 | bytes 4000000 | tf_op jit(solution)/shard_map/pallas_call | solution.py:683
  37.2 0.0 collective-permute-done.outer
  37.2 0.0 collective-permute-done.2.wing
  37.2 0.0 collective-permute-done.1.far
  37.2 11.2 %collective-permute-done.3.mate = f32[616,384]{1,0:T(8,128)S(1)} collective-permute-done((f32[616,384]{1,0:T(8,128)}, f32[616,384]{1,0:T(8,128)S(1)}, u32[]{:S(2)}, u32[]{:S(2)}) %collective-permute-start.3) | collective-permute-done | bytes 946208 | tf_op jit(solution)/shard_map/ppermute | solution.py:718
  48.4 0.0 copy-start.2
  48.4 0.9 copy-done.2
  49.3 41.3 %shard_map.48 = (f32[512,256]{1,0:T(8,128)S(1)}, f32[512,256]{1,0:T(8,128)S(1)}, f32[512,256]{1,0:T(8,128)S(1)}, f32[512,512]{1,0:T(8,128)S(1)}, s32[8,4]{1,0:T(8,128)S(1)}) custom-call(s32[4,7]{1,0:T(4,128)S(1)} %copy-done.4, s32[4,4]{1,0:T(4,128)S(1)} %get-tuple-element.16.done, f32[14,512]{1,0:T(8,128)S(1)} %copy-done.3, f32[98,512]{1,0:T(8,128)S(1)} %copy-done.2, ...), custom_call_target="tpu_custom_call" | custom-call | flops 35000000512 | bytes 4000000 | tf_op jit(solution)/shard_map/pallas_call | solution.py:683
  90.6 0.1 collective-permute-start.5
  90.7 0.1 collective-permute-start.6
  90.8 8.7 %collective-permute-start.4 = (f32[512,256]{1,0:T(8,128)S(1)}, f32[512,256]{1,0:T(8,128)S(1)}, u32[]{:S(2)}, u32[]{:S(2)}) collective-permute-start(f32[512,256]{1,0:T(8,128)S(1)} %get-tuple-element.22.after), channel_id=1, source_target_pairs={{0,255},{1,2},{2,1},{3,4},{4,3},{5,6},{6,5},{7,8},{8,7},{9,10},{10... | collective-permute-start | bytes 1572872 | tf_op jit(solution)/shard_map/ppermute | solution.py:731
  99.5 6.5 %shard_map.49 = f32[512,512]{1,0:T(8,128)S(1)} custom-call(s32[8,4]{1,0:T(8,128)S(1)} %get-tuple-element.21.todo, f32[14,512]{1,0:T(8,128)S(1)} %copy-done.3, f32[98,512]{1,0:T(8,128)S(1)} %copy-done.2, f32[512,512]{1,0:T(8,128)S(1)} %copy-done, f32[688,128]{1,0:T(8,128)S(1)} %collective-permute-done.outer, f32[616,384]{1,0:T(8,128)S(1)} %collective-permute-done.3.mate, ...), custom_call_target="tpu_custom_call" | custom-call | flops 40000000000 | bytes 4000000 | tf_op jit(solution)/shard_map/pallas_call | solution.py:683
  106.1 1.7 %collective-permute-done.5 = f32[512,256]{1,0:T(8,128)S(1)} collective-permute-done((f32[512,256]{1,0:T(8,128)S(1)}, f32[512,256]{1,0:T(8,128)S(1)}, u32[]{:S(2)}, u32[]{:S(2)}) %collective-permute-start.5) | collective-permute-done | bytes 524320 | tf_op jit(solution)/shard_map/ppermute | solution.py:733
  107.8 0.3 collective-permute-done.6
  108.1 19.6 %collective-permute-done.4 = f32[512,256]{1,0:T(8,128)S(1)} collective-permute-done((f32[512,256]{1,0:T(8,128)S(1)}, f32[512,256]{1,0:T(8,128)S(1)}, u32[]{:S(2)}, u32[]{:S(2)}) %collective-permute-start.4) | collective-permute-done | bytes 524320 | tf_op jit(solution)/shard_map/ppermute | solution.py:731
  127.7 0.1 broadcast_select_fusion.1
  127.8 1.4 %maximum_add_fusion = f32[512,512]{1,0:T(8,128)} fusion(f32[512,256]{1,0:T(8,128)S(1)} %get-tuple-element.26, f32[512,256]{1,0:T(8,128)S(1)} %get-tuple-element.25, f32[512,512]{1,0:T(8,128)S(1)} %shard_map.49, f32[512,512]{1,0:T(8,128)S(1)} %get-tuple-element.15, f32[512,512]{1,0:T(8,128)S(1)} %get-tuple-element.20), kind=kLoop, calls=%fused_computation | loop fusion | flops 1048576 | bytes 5242880 | tf_op jit(solution)/shard_map/add | solution.py:745
Async XLA Ops:
  0.0 9.4 %copy-start = (f32[512,512]{1,0:T(8,128)S(1)}, f32[512,512]{1,0:T(8,128)}, u32[]{:S(2)}) copy-start(f32[512,512]{1,0:T(8,128)} %currents.7) | copy-start | bytes 3145732
  0.0 9.4 %copy-start.3 = (f32[14,512]{1,0:T(8,128)S(1)}, f32[14,512]{1,0:T(8,128)}, u32[]{:S(2)}) copy-start(f32[14,512]{1,0:T(8,128)} %test.5) | copy-start | bytes 86020
  0.0 9.4 %copy-start.1 = (f32[98,512]{1,0:T(8,128)S(1)}, f32[98,512]{1,0:T(8,128)}, u32[]{:S(2)}) copy-start(f32[98,512]{1,0:T(8,128)} %panels.5) | copy-start | bytes 602116
  3.7 5.7 %copy-start.4 = (s32[4,7]{1,0:T(4,128)S(1)}, s32[4,7]{1,0:T(4,128)}, u32[]{:S(2)}) copy-start(s32[4,7]{1,0:T(4,128)} %mask.5) | copy-start | bytes 340
  3.7 33.4 %collective-permute-start.2 = (f32[656,256]{1,0:T(8,128)}, f32[656,256]{1,0:T(8,128)}, u32[]{:S(2)}, u32[]{:S(2)}) collective-permute-start(f32[656,256]{1,0:T(8,128)} %get-tuple-element.18), channel_id=1, source_target_pairs={{0,252},{1,5},{2,254},{3,7},{4,0},{5,9},{6,2},{7,11},{8,4},{9,13},... | collective-permute-start | bytes 2015240 | tf_op jit(solution)/shard_map/ppermute | solution.py:716
  6.5 30.7 %collective-permute-start.1 = (f32[656,256]{1,0:T(8,128)}, f32[656,256]{1,0:T(8,128)}, u32[]{:S(2)}, u32[]{:S(2)}) collective-permute-start(f32[656,256]{1,0:T(8,128)} %get-tuple-element.18), channel_id=1, source_target_pairs={{0,254},{1,3},{2,0},{3,5},{4,2},{5,7},{6,4},{7,9},{8,6},{9,11},{10... | collective-permute-start | bytes 2015240 | tf_op jit(solution)/shard_map/ppermute | solution.py:717
  7.4 29.7 %collective-permute-start = (f32[688,128]{1,0:T(8,128)}, f32[688,128]{1,0:T(8,128)S(1)}, u32[]{:S(2)}, u32[]{:S(2)}) collective-permute-start(f32[688,128]{1,0:T(8,128)} %get-tuple-element.17), channel_id=1, source_target_pairs={{0,255},{1,2},{2,1},{3,4},{4,3},{5,6},{6,5},{7,8},{8,7},{9,10},{10... | collective-permute-start | bytes 1056776 | tf_op jit(solution)/shard_map/ppermute | solution.py:715
  7.5 40.9 %collective-permute-start.3 = (f32[616,384]{1,0:T(8,128)}, f32[616,384]{1,0:T(8,128)S(1)}, u32[]{:S(2)}, u32[]{:S(2)}) collective-permute-start(f32[616,384]{1,0:T(8,128)} %get-tuple-element.19), channel_id=1, source_target_pairs={{0,1},{1,0},{2,3},{3,2},{4,5},{5,4},{6,7},{7,6},{8,9},{9,8},{10,11... | collective-permute-start | bytes 2838536 | tf_op jit(solution)/shard_map/ppermute | solution.py:718
  48.4 0.9 copy-start.2
  90.6 17.1 %collective-permute-start.5 = (f32[512,256]{1,0:T(8,128)S(1)}, f32[512,256]{1,0:T(8,128)S(1)}, u32[]{:S(2)}, u32[]{:S(2)}) collective-permute-start(f32[512,256]{1,0:T(8,128)S(1)} %get-tuple-element.23), channel_id=1, source_target_pairs={{252,0},{5,1},{254,2},{7,3},{0,4},{9,5},{2,6},{11,7},{4,8},{13,9},... | collective-permute-start | bytes 1572872 | tf_op jit(solution)/shard_map/ppermute | solution.py:733
  90.7 17.4 %collective-permute-start.6 = (f32[512,256]{1,0:T(8,128)S(1)}, f32[512,256]{1,0:T(8,128)S(1)}, u32[]{:S(2)}, u32[]{:S(2)}) collective-permute-start(f32[512,256]{1,0:T(8,128)S(1)} %get-tuple-element.24), channel_id=1, source_target_pairs={{254,0},{3,1},{0,2},{5,3},{2,4},{7,5},{4,6},{9,7},{6,8},{11,9},{8,... | collective-permute-start | bytes 1572872 | tf_op jit(solution)/shard_map/ppermute | solution.py:732
  90.8 36.9 %collective-permute-start.4 = (f32[512,256]{1,0:T(8,128)S(1)}, f32[512,256]{1,0:T(8,128)S(1)}, u32[]{:S(2)}, u32[]{:S(2)}) collective-permute-start(f32[512,256]{1,0:T(8,128)S(1)} %get-tuple-element.22.after), channel_id=1, source_target_pairs={{0,255},{1,2},{2,1},{3,4},{4,3},{5,6},{6,5},{7,8},{8,7},{9,10},{10... | collective-permute-start | bytes 1572872 | tf_op jit(solution)/shard_map/ppermute | solution.py:731

commit v7 on v5

--- a/solution.py
+++ b/solution.py
@@ -238,7 +238,8 @@
         per = -(-len(work) // NOUT)
         acc, history = None, []
         for o in range(NOUT):
-            piece(next_chunk, next_buf, o)
+            if next_buf is not None:
+                piece(next_chunk, next_buf, o)
             for g, q, a in work[o * per : (o + 1) * per]:
                 if q == 0 and a == 0:
                     acc = None
@@ -259,10 +260,12 @@
 
     def step(n, carry):
         phase(2 * n, bufs[0], 2 * n + 1, bufs[1])
-        phase(2 * n + 1, bufs[1], lax.rem(2 * n + 2, NCH), bufs[0])
+        phase(2 * n + 1, bufs[1], 2 * n + 2, bufs[0])
         return carry
 
-    lax.fori_loop(0, NCH // 2, step, 0)
+    lax.fori_loop(0, NCH // 2 - 1, step, 0)
+    phase(NCH - 2, bufs[0], NCH - 1, bufs[1])
+    phase(NCH - 1, bufs[1], None, None)
 
 
 def direct_tile(stage, raw, xt, ops, b):
@@ -365,7 +368,8 @@
 def shares(load_near, load_far):
     goal = lax.div(FULL + load_near + load_far + 1, 3)
     near = jnp.clip(goal - load_near, 3, 7)
-    far = jnp.clip(lax.div(FULL - near + load_far + 1, 2) - load_far, 0, 8)
+    far = jnp.clip(lax.div(FULL - near + load_far + 1, 2) - load_far, 0, 6)
+    near = jnp.clip(lax.div(FULL - far + load_near + 1, 2) - load_near, 3, 7)
     return near, far
 
 
@@ -375,7 +379,7 @@
 
 
 def is_far(u, v, share):
-    return (jnp.where(u == 3, v, jnp.where(u == 2, TPB + v, FULL))) < share
+    return (v >= 2) & (jnp.where((u >= 1) & (u <= 3), 2 * (3 - u) + v - 2, FULL) < share)
 
 
 PACK_COPIES = 5
@@ -385,7 +389,7 @@
     even = is_even()
     places = (
         (outer, 1, jnp.where(even, 0, 3 * BLK)),
-        (far, 2, jnp.where(even, 2 * BLK, 0)),
+        (far, 3, jnp.where(even, BLK, 0)),
         (mate, 3, jnp.where(even, BLK, 0)),
     )
     lanes = [pl.ds(pl.multiple_of(begin, BLK), count * BLK) for _, count, begin in places]
@@ -396,7 +400,7 @@
         each.start()
     value = load_of(mask).astype(F32)
     outer[XROW + 64 : XROW + 72, :] = jnp.full((8, BLK), value, F32)
-    far[XROW + 32 : XROW + 40, :] = jnp.full((8, 2 * BLK), value, F32)
+    far[XROW + 32 : XROW + 40, :] = jnp.full((8, 3 * BLK), value, F32)
     mate[XROW : XROW + 8, :] = jnp.full((8, 3 * BLK), value, F32)
     load[...] = jnp.full((8, BLK), value, F32)
     copies[0].wait()
@@ -406,8 +410,8 @@
     for b in range(TPB):
         points = test[:, b * BLK : (b + 1) * BLK]
         outer[XROW + 16 * b : XROW + 16 * b + 14, :] = points
-        row = XROW + 16 * (b // 2)
-        far[row : row + 14, (b % 2) * BLK : (b % 2 + 1) * BLK] = points
+        row = XROW + 16 * (b // 3)
+        far[row : row + 14, (b % 3) * BLK : (b % 3 + 1) * BLK] = points
     for each in copies[2:]:
         each.wait()
 
@@ -507,7 +511,7 @@
     def plan(i, used):
         n, b = lax.div(i, TPB), lax.rem(i, TPB)
         u, v = mirrored(even, n), mirrored(even, b)
-        dense = (u == 1) | ((u == 0) & (v == 3))
+        dense = (u > 0) & (v < 2)
         wanted = (full & dense) | (jnp.logical_not(full) & (mask[b, n - b + REACH] > 0))
         now = wanted & (used < FIRST)
         done[n, b] = now.astype(jnp.int32)
@@ -519,7 +523,7 @@
 
 
 QUOTA = 7
-HELP_STEPS = 6
+HELP_STEPS = 7
 OWN_STEPS = 8
 
 
@@ -542,7 +546,7 @@
 
 
 def second_kernel(
-    mask, done, test, panels, currents, outer, far, mate, load_far, part, out_near, out_far, out_own, todo, *scratch
+    mask, done, test, panels, currents, outer, far, mate, load_far, out_near, out_far, out_own, todo, *scratch
 ):
     plan, scratch = scratch[-1], scratch[:-1]
     even = is_even()
@@ -559,19 +563,16 @@
         xt,
         1,
         lambda b, row: far[
-            XROW + 16 * (b // 2) + row : XROW + 16 * (b // 2) + row + 2, (b % 2) * BLK : (b % 2 + 1) * BLK
+            XROW + 16 * (b // 3) + row : XROW + 16 * (b // 3) + row + 2, (b % 3) * BLK : (b % 3 + 1) * BLK
         ],
     )
     fill_tests(xt, 2, own_tests(test))
-    clear(acc, 2 * TPB)
-    for b in range(TPB):
-        for g in range(4):
-            acc[2 * TPB + b, :, g * BLK : (g + 1) * BLK] = part[g * NRHS : (g + 1) * NRHS, b * BLK : (b + 1) * BLK]
+    clear(acc, 3 * TPB)
 
     def plan_help(i, used):
         n, b = lax.div(i, TPB), lax.rem(i, TPB)
         v_near, v_far = mirrored(odd, b), mirrored(even, b)
-        u_near, u_far = jnp.where(n == 3, 0, -1 - n), 7 - n
+        u_near, u_far = jnp.where(n == 3, 0, -1 - n), jnp.where(even, n - 3, 7 - n)
         of_near = (n < 4) & (v_near - u_near <= REACH) & is_near(u_near, v_near, share_near)
         of_far = (n >= 4) & is_far(u_far, v_far, share_far)
         wanted = ((near_load == FULL) & of_near) | ((far_load == FULL) & of_far)
@@ -607,7 +608,7 @@
 
         @pl.when((n > 3) & (n < HELP_STEPS))
         def _():
-            fill(scratch, far, far, CROW, jnp.where(even, 5 - n, n - 4))
+            fill(scratch, far, far, CROW, n - 4)
 
         @pl.when(n >= HELP_STEPS)
         def _():
@@ -622,16 +623,14 @@
     )
     shift = jnp.where(even, 2, 0)
     write_out(out_near, acc, [b + shift for b in range(2)])
-    write_out(out_far, acc, range(TPB, 2 * TPB))
+    write_out(out_far, acc, [TPB + b + shift for b in range(2)])
     write_out(out_own, acc, range(2 * TPB, 3 * TPB))
 
 
-def rest_kernel(todo, test, panels, currents, outer, mate, part, after, out, *scratch):
+def rest_kernel(todo, test, panels, currents, outer, mate, after, out, *scratch):
     acc = scratch[12]
     fill_tests(scratch[1], 0, own_tests(test))
-    for b in range(TPB):
-        for g in range(4):
-            acc[b, :, g * BLK : (g + 1) * BLK] = part[g * NRHS : (g + 1) * NRHS, b * BLK : (b + 1) * BLK]
+    clear(acc, TPB)
     engine(
         scratch,
         OWN_STEPS,
@@ -686,7 +685,7 @@
         in_specs=[smem] * tables + [vmem] * plain + [anywhere] * unread,
         out_specs=specs,
         scratch_shapes=scratch,
-        compiler_params=pltpu.CompilerParams(vmem_limit_bytes=(60 if copies else 26) * 1024 * 1024),
+        compiler_params=pltpu.CompilerParams(vmem_limit_bytes=(60 if copies else 20) * 1024 * 1024),
         cost_estimate=pl.CostEstimate(flops=tiles * 5 * 10**9, bytes_accessed=4 * 10**6, transcendentals=0),
     )(*operands)
 
@@ -702,7 +701,7 @@
     wide = 4 * NRHS
     mate, outer, far, load = call(
         pack_kernel,
-        [(MATE_ROWS, 3 * BLK), (OUTER_ROWS, BLK), (FAR_ROWS, 2 * BLK), (8, BLK)],
+        [(MATE_ROWS, 3 * BLK), (OUTER_ROWS, BLK), (FAR_ROWS, 3 * BLK), (8, BLK)],
         [near_mask, panels, test_points, currents],
         unread=3,
         copies=PACK_COPIES,
@@ -714,10 +713,10 @@
     part, done = call(
         first_kernel, [(wide, width)], [near_mask, test_points, panels, currents], 1, tiles=5, table=(TPB, TPB)
     )
-    to_near, to_far, part, todo = call(
+    to_near, to_far, more, todo = call(
         second_kernel,
-        [(wide, 2 * BLK), (wide, width), (wide, width)],
-        [near_mask, done, test_points, panels, currents, outer, far, mate, load_far, part],
+        [(wide, 2 * BLK), (wide, 2 * BLK), (wide, width)],
+        [near_mask, done, test_points, panels, currents, outer, far, mate, load_far],
         3,
         tables=2,
         tiles=7,
@@ -728,17 +727,14 @@
     (rest,) = call(
         rest_kernel,
         [(wide, width)],
-        [todo, test_points, panels, currents, outer, mate, part, to_near],
+        [todo, test_points, panels, currents, outer, mate, to_near],
         1,
         unread=1,
         tiles=8,
     )
-    padded = jnp.where(
-        lax.axis_index("narrow") == 0,
-        jnp.pad(from_near, ((0, 0), (0, 2 * BLK))),
-        jnp.pad(from_near, ((0, 0), (2 * BLK, 0))),
-    )
-    return rest + from_far + padded
+    even = lax.axis_index("narrow") == 0
+    helped = jnp.concatenate([jnp.where(even, from_near, from_far), jnp.where(even, from_far, from_near)], 1)
+    return part + more + rest + helped
 
 
 def solution(mesh):

time: 107 us -> 111 us (1.037)
  the two profiles are of different devices: /device:TPU:4 before, /device:TPU:100 now
where the time goes in v7:
time: 111 us; the launch traced here: 110 us
  Pallas kernels  93 us (84%)
  starting transfers between devices  10 us (9%)
  waiting for transfers between devices  4.72 us (4%)
  other arithmetic  1.51 us (1%)
    pallas_call x4, Pallas kernels, call(): pl.pallas_call(kernel, out_shape=shapes, in_specs=[smem] * tables + [vmem...  93 us
    ppermute x1, waiting for transfers between devices, body(): far = lax.ppermute(far, axes, away)  4.48 us
    ppermute x1, starting transfers between devices, body(): from_near = lax.ppermute(to_near, axes, across)  3.09 us
  transfers between devices with their start and end apart: 6, of which 2 were waited for; matrix products, arithmetic and copies ran while one was open for 0% of the time, Pallas kernels for 45%

profile of v7, /device:TPU:100, one launch (start us, length us, event | category | flops | bytes accessed | tf_op | source)
XLA Modules:
  0.0 110.3 jit_solution(4482727745580085004)
XLA Ops:
  0.0 0.0 copy-start.1
  0.0 0.0 copy-start.3
  0.0 0.0 copy-start
  0.0 3.9 %shard_map.47 = (f32[624,384]{1,0:T(8,128)}, f32[688,128]{1,0:T(8,128)}, f32[656,384]{1,0:T(8,128)}, f32[8,128]{1,0:T(8,128)}) custom-call(s32[4,7]{1,0:T(4,128)} %mask.5, f32[98,512]{1,0:T(8,128)} %panels.5, f32[14,512]{1,0:T(8,128)} %test.5, f32[512,512]{1,0:T(8,128)} %currents.7), custom_call_target="tpu_custom_call" | custom-call | flops 5000000000 | bytes 4000000 | tf_op jit(solution)/shard_map/pallas_call | solution.py:682
  3.9 0.0 copy-start.5
  4.0 1.2 %collective-permute-start.2 = (f32[624,384]{1,0:T(8,128)}, f32[624,384]{1,0:T(8,128)}, u32[]{:S(2)}, u32[]{:S(2)}) collective-permute-start(f32[624,384]{1,0:T(8,128)} %get-tuple-element.19), channel_id=1, source_target_pairs={{0,1},{1,0},{2,3},{3,2},{4,5},{5,4},{6,7},{7,6},{8,9},{9,8},{10,11... | collective-permute-start | bytes 2875400 | tf_op jit(solution)/shard_map/ppermute | solution.py:712
  5.2 0.0 copy-start.4
  5.2 1.5 %collective-permute-start = (f32[688,128]{1,0:T(8,128)}, f32[688,128]{1,0:T(8,128)S(1)}, u32[]{:S(2)}, u32[]{:S(2)}) collective-permute-start(f32[688,128]{1,0:T(8,128)} %get-tuple-element.17), channel_id=1, source_target_pairs={{0,255},{1,2},{2,1},{3,4},{4,3},{5,6},{6,5},{7,8},{8,7},{9,10},{10... | collective-permute-start | bytes 1056776 | tf_op jit(solution)/shard_map/ppermute | solution.py:710
  6.7 2.0 %collective-permute-start.1 = (f32[656,384]{1,0:T(8,128)}, f32[656,384]{1,0:T(8,128)S(1)}, u32[]{:S(2)}, u32[]{:S(2)}) collective-permute-start(f32[656,384]{1,0:T(8,128)} %get-tuple-element.18), channel_id=1, source_target_pairs={{0,254},{1,3},{2,0},{3,5},{4,2},{5,7},{6,4},{7,9},{8,6},{9,11},{10... | collective-permute-start | bytes 3022856 | tf_op jit(solution)/shard_map/ppermute | solution.py:711
  8.8 0.0 copy-done.5
  8.8 0.0 collective-permute-start.3
  8.8 0.0 copy-done.1
  8.8 0.0 copy-done.3
  8.8 0.0 copy-done
  8.8 0.0 copy-done.4
  8.8 27.0 %shard_map.46 = (f32[512,512]{1,0:T(8,128)S(1)}, s32[4,4]{1,0:T(4,128)S(1)}) custom-call(s32[4,7]{1,0:T(4,128)S(1)} %copy-done.4, f32[14,512]{1,0:T(8,128)S(1)} %copy-done.3, f32[98,512]{1,0:T(8,128)S(1)} %copy-done.1, f32[512,512]{1,0:T(8,128)S(1)} %copy-done), custom_call_target="tpu_custom_call" | custom-call | flops 24999999488 | bytes 4000000 | tf_op jit(solution)/shard_map/pallas_call | solution.py:682
  35.8 0.2 collective-permute-done.3.load_far
  36.1 0.0 collective-permute-done.outer
  36.1 0.0 collective-permute-done.2.mate
  36.1 4.5 %collective-permute-done.1.far = f32[656,384]{1,0:T(8,128)S(1)} collective-permute-done((f32[656,384]{1,0:T(8,128)}, f32[656,384]{1,0:T(8,128)S(1)}, u32[]{:S(2)}, u32[]{:S(2)}) %collective-permute-start.1) | collective-permute-done | bytes 1007648 | tf_op jit(solution)/shard_map/ppermute | solution.py:711
  40.6 0.0 copy-start.2
  40.6 0.9 copy-done.2
  41.5 39.8 %shard_map.48 = (f32[512,256]{1,0:T(8,128)S(1)}, f32[512,256]{1,0:T(8,128)S(1)}, f32[512,512]{1,0:T(8,128)S(1)}, s32[8,4]{1,0:T(8,128)S(1)}) custom-call(s32[4,7]{1,0:T(4,128)S(1)} %copy-done.4, s32[4,4]{1,0:T(4,128)S(1)} %get-tuple-element.16.done, f32[14,512]{1,0:T(8,128)S(1)} %copy-done.3, f32[98,512]{1,0:T(8,128)S(1)} %copy-done.2, ...), custom_call_target="tpu_custom_call" | custom-call | flops 35000000512 | bytes 4000000 | tf_op jit(solution)/shard_map/pallas_call | solution.py:682
  81.2 3.1 %collective-permute-start.4 = (f32[512,256]{1,0:T(8,128)S(1)}, f32[512,256]{1,0:T(8,128)S(1)}, u32[]{:S(2)}, u32[]{:S(2)}) collective-permute-start(f32[512,256]{1,0:T(8,128)S(1)} %get-tuple-element.23.after), channel_id=1, source_target_pairs={{0,255},{1,2},{2,1},{3,4},{4,3},{5,6},{6,5},{7,8},{8,7},{9,10},{10... | collective-permute-start | bytes 1572872 | tf_op jit(solution)/shard_map/ppermute | solution.py:725
  84.3 2.1 %collective-permute-start.5 = (f32[512,256]{1,0:T(8,128)S(1)}, f32[512,256]{1,0:T(8,128)S(1)}, u32[]{:S(2)}, u32[]{:S(2)}) collective-permute-start(f32[512,256]{1,0:T(8,128)S(1)} %get-tuple-element.24), channel_id=1, source_target_pairs={{254,0},{3,1},{0,2},{5,3},{2,4},{7,5},{4,6},{9,7},{6,8},{11,9},{8,... | collective-permute-start | bytes 1572872 | tf_op jit(solution)/shard_map/ppermute | solution.py:726
  86.5 22.3 %shard_map.49 = f32[512,512]{1,0:T(8,128)S(1)} custom-call(s32[8,4]{1,0:T(8,128)S(1)} %get-tuple-element.22.todo, f32[14,512]{1,0:T(8,128)S(1)} %copy-done.3, f32[98,512]{1,0:T(8,128)S(1)} %copy-done.2, f32[512,512]{1,0:T(8,128)S(1)} %copy-done, f32[688,128]{1,0:T(8,128)S(1)} %collective-permute-done.outer, f32[624,384]{1,0:T(8,128)} %collective-permute-done.2.mate, ...), custom_call_target="tpu_custom_call" | custom-call | flops 40000000000 | bytes 4000000 | tf_op jit(solution)/shard_map/pallas_call | solution.py:682
  108.8 0.0 collective-permute-done.4
  108.8 0.0 collective-permute-done.5
  108.8 0.1 broadcast_select_fusion.1
  108.9 1.4 %maximum_add_fusion = f32[512,512]{1,0:T(8,128)} fusion(f32[512,256]{1,0:T(8,128)S(1)} %get-tuple-element.26, f32[512,256]{1,0:T(8,128)S(1)} %get-tuple-element.25, f32[512,512]{1,0:T(8,128)S(1)} %shard_map.49, f32[512,512]{1,0:T(8,128)S(1)} %get-tuple-element.15, f32[512,512]{1,0:T(8,128)S(1)} %get-tuple-element.21), kind=kLoop, calls=%fused_computation | loop fusion | flops 1048576 | bytes 5242880 | tf_op jit(solution)/shard_map/add | solution.py:737
Async XLA Ops:
  0.0 8.8 %copy-start.1 = (f32[98,512]{1,0:T(8,128)S(1)}, f32[98,512]{1,0:T(8,128)}, u32[]{:S(2)}) copy-start(f32[98,512]{1,0:T(8,128)} %panels.5) | copy-start | bytes 602116
  0.0 8.8 %copy-start.3 = (f32[14,512]{1,0:T(8,128)S(1)}, f32[14,512]{1,0:T(8,128)}, u32[]{:S(2)}) copy-start(f32[14,512]{1,0:T(8,128)} %test.5) | copy-start | bytes 86020
  0.0 8.8 %copy-start = (f32[512,512]{1,0:T(8,128)S(1)}, f32[512,512]{1,0:T(8,128)}, u32[]{:S(2)}) copy-start(f32[512,512]{1,0:T(8,128)} %currents.7) | copy-start | bytes 3145732
  3.9 4.8 %copy-start.5 = (f32[8,128]{1,0:T(8,128)S(1)}, f32[8,128]{1,0:T(8,128)}, u32[]{:S(2)}) copy-start(f32[8,128]{1,0:T(8,128)} %get-tuple-element.20) | copy-start | bytes 12292
  4.0 32.1 %collective-permute-start.2 = (f32[624,384]{1,0:T(8,128)}, f32[624,384]{1,0:T(8,128)}, u32[]{:S(2)}, u32[]{:S(2)}) collective-permute-start(f32[624,384]{1,0:T(8,128)} %get-tuple-element.19), channel_id=1, source_target_pairs={{0,1},{1,0},{2,3},{3,2},{4,5},{5,4},{6,7},{7,6},{8,9},{9,8},{10,11... | collective-permute-start | bytes 2875400 | tf_op jit(solution)/shard_map/ppermute | solution.py:712
  5.2 3.6 %copy-start.4 = (s32[4,7]{1,0:T(4,128)S(1)}, s32[4,7]{1,0:T(4,128)}, u32[]{:S(2)}) copy-start(s32[4,7]{1,0:T(4,128)} %mask.5) | copy-start | bytes 340
  5.2 30.9 %collective-permute-start = (f32[688,128]{1,0:T(8,128)}, f32[688,128]{1,0:T(8,128)S(1)}, u32[]{:S(2)}, u32[]{:S(2)}) collective-permute-start(f32[688,128]{1,0:T(8,128)} %get-tuple-element.17), channel_id=1, source_target_pairs={{0,255},{1,2},{2,1},{3,4},{4,3},{5,6},{6,5},{7,8},{8,7},{9,10},{10... | collective-permute-start | bytes 1056776 | tf_op jit(solution)/shard_map/ppermute | solution.py:710
  6.7 33.8 %collective-permute-start.1 = (f32[656,384]{1,0:T(8,128)}, f32[656,384]{1,0:T(8,128)S(1)}, u32[]{:S(2)}, u32[]{:S(2)}) collective-permute-start(f32[656,384]{1,0:T(8,128)} %get-tuple-element.18), channel_id=1, source_target_pairs={{0,254},{1,3},{2,0},{3,5},{4,2},{5,7},{6,4},{7,9},{8,6},{9,11},{10... | collective-permute-start | bytes 3022856 | tf_op jit(solution)/shard_map/ppermute | solution.py:711
  8.8 27.3 %collective-permute-start.3 = (f32[8,128]{1,0:T(8,128)S(1)}, f32[8,128]{1,0:T(8,128)S(1)}, u32[]{:S(2)}, u32[]{:S(2)}) collective-permute-start(f32[8,128]{1,0:T(8,128)S(1)} %copy-done.5), channel_id=1, source_target_pairs={{254,0},{3,1},{0,2},{5,3},{2,4},{7,5},{4,6},{9,7},{6,8},{11,9},{8,... | collective-permute-start | bytes 12296 | tf_op jit(solution)/shard_map/ppermute | solution.py:709
  40.6 0.9 copy-start.2
  81.2 27.6 %collective-permute-start.4 = (f32[512,256]{1,0:T(8,128)S(1)}, f32[512,256]{1,0:T(8,128)S(1)}, u32[]{:S(2)}, u32[]{:S(2)}) collective-permute-start(f32[512,256]{1,0:T(8,128)S(1)} %get-tuple-element.23.after), channel_id=1, source_target_pairs={{0,255},{1,2},{2,1},{3,4},{4,3},{5,6},{6,5},{7,8},{8,7},{9,10},{10... | collective-permute-start | bytes 1572872 | tf_op jit(solution)/shard_map/ppermute | solution.py:725
  84.3 24.5 %collective-permute-start.5 = (f32[512,256]{1,0:T(8,128)S(1)}, f32[512,256]{1,0:T(8,128)S(1)}, u32[]{:S(2)}, u32[]{:S(2)}) collective-permute-start(f32[512,256]{1,0:T(8,128)S(1)} %get-tuple-element.24), channel_id=1, source_target_pairs={{254,0},{3,1},{0,2},{5,3},{2,4},{7,5},{4,6},{9,7},{6,8},{11,9},{8,... | collective-permute-start | bytes 1572872 | tf_op jit(solution)/shard_map/ppermute | solution.py:726

commit v8 on v7

--- a/solution.py
+++ b/solution.py
@@ -216,8 +216,9 @@
     l1i = k1 * s2r
     l2r = k2 * pr - k6 * qr
     l2i = k2 * qr + k6 * pr
-    kr = weight * (((c2r + pr) + (s2 + 3.0 * p)) + q)
-    ki = weight * (((s2r + qr) + (3.0 * q - c2)) - p)
+    inv3 = inv + 3.0
+    kr = weight * ((c2r + s2) + (p * inv3 + q))
+    ki = weight * ((s2r - c2) + (q * inv3 - p))
     return l1r, l1i, l2r, l2i, kr, ki
 
 
@@ -244,7 +245,7 @@
                 if q == 0 and a == 0:
                     acc = None
                 row = q * JC + g * 8
-                if len(history) >= AHEAD:
+                if len(history) >= AHEAD and len(history) % 2 == 0:
                     buf[pl.ds(spare, 8), 0:BLK] = history[-AHEAD]
                 vals = [buf[row : row + 8, k * 256 + a * BLK : k * 256 + (a + 1) * BLK] for k in range(NOUT)]
                 terms = pair_terms(*vals)
@@ -382,10 +383,12 @@
     return (v >= 2) & (jnp.where((u >= 1) & (u <= 3), 2 * (3 - u) + v - 2, FULL) < share)
 
 
-PACK_COPIES = 5
-
-
-def pack_kernel(mask, panels_at, test_at, currents, mate, outer, far, load, panels, test, sems):
+PACK_COPIES = 11
+
+
+def pack_kernel(
+    mask, panels_at, test_at, currents, mate, outer, far, load, panels, test, geo, outer_end, far_end, mate_end, sems
+):
     even = is_even()
     places = (
         (outer, 1, jnp.where(even, 0, 3 * BLK)),
@@ -393,25 +396,37 @@
         (mate, 3, jnp.where(even, BLK, 0)),
     )
     lanes = [pl.ds(pl.multiple_of(begin, BLK), count * BLK) for _, count, begin in places]
-    copies = [pltpu.make_async_copy(panels_at, panels, sems.at[0]), pltpu.make_async_copy(test_at, test, sems.at[1])]
+    copies = []
+
+    def copy(source, target):
+        copies.append(pltpu.make_async_copy(source, target, sems.at[len(copies)]))
+        copies[-1].start()
+
+    copy(panels_at, panels)
+    copy(test_at, test)
     for k in range(3):
-        copies.append(pltpu.make_async_copy(currents.at[:, lanes[k]], places[k][0].at[CROW:XROW, :], sems.at[2 + k]))
-    for each in copies:
-        each.start()
+        copy(currents.at[:, lanes[k]], places[k][0].at[CROW:XROW, :])
     value = load_of(mask).astype(F32)
-    outer[XROW + 64 : XROW + 72, :] = jnp.full((8, BLK), value, F32)
-    far[XROW + 32 : XROW + 40, :] = jnp.full((8, 3 * BLK), value, F32)
-    mate[XROW : XROW + 8, :] = jnp.full((8, 3 * BLK), value, F32)
     load[...] = jnp.full((8, BLK), value, F32)
+    mate_end[...] = jnp.full((8, 3 * BLK), value, F32)
+    copy(mate_end, mate.at[XROW:MATE_ROWS, :])
+    outer_end[0:64, :] = jnp.zeros((64, BLK), F32)
+    outer_end[64:72, :] = jnp.full((8, BLK), value, F32)
+    far_end[0:32, :] = jnp.zeros((32, 3 * BLK), F32)
+    far_end[32:40, :] = jnp.full((8, 3 * BLK), value, F32)
+    geo[GROWS - 2 : CROW, :] = jnp.zeros((CROW - GROWS + 2, TPB * BLK), F32)
     copies[0].wait()
+    geo[0:GROWS, :] = panels[...]
+    for k in range(3):
+        copy(geo.at[:, lanes[k]], places[k][0].at[0:CROW, :])
     copies[1].wait()
-    for k in range(3):
-        places[k][0][0:GROWS, :] = panels[:, lanes[k]]
     for b in range(TPB):
         points = test[:, b * BLK : (b + 1) * BLK]
-        outer[XROW + 16 * b : XROW + 16 * b + 14, :] = points
-        row = XROW + 16 * (b // 3)
-        far[row : row + 14, (b % 3) * BLK : (b % 3 + 1) * BLK] = points
+        outer_end[16 * b : 16 * b + 14, :] = points
+        row = 16 * (b // 3)
+        far_end[row : row + 14, (b % 3) * BLK : (b % 3 + 1) * BLK] = points
+    copy(outer_end, outer.at[XROW:OUTER_ROWS, :])
+    copy(far_end, far.at[XROW:FAR_ROWS, :])
     for each in copies[2:]:
         each.wait()
 
@@ -670,9 +685,14 @@
     specs = [vmem] * len(outs)
     scratch = scratch_for(sets) if sets else []
     if copies:
+        specs = [anywhere] * 3 + [vmem]
         scratch += [
             pltpu.VMEM((GROWS, TPB * BLK), F32),
             pltpu.VMEM((14, TPB * BLK), F32),
+            pltpu.VMEM((CROW, TPB * BLK), F32),
+            pltpu.VMEM((72, BLK), F32),
+            pltpu.VMEM((40, 3 * BLK), F32),
+            pltpu.VMEM((8, 3 * BLK), F32),
             pltpu.SemaphoreType.DMA((copies,)),
         ]
     if table:

time: 111 us -> 170 us (1.53)
  the two profiles are of different devices: /device:TPU:100 before, /device:TPU:5 now
where the time goes in v8:
time: 170 us
  Pallas kernels  151 us (89%)
  starting transfers between devices  15 us (9%)
    pallas_call x4, Pallas kernels, call(): pl.pallas_call(kernel, out_shape=shapes, in_specs=[smem] * tables + [vmem...  151 us
    ppermute x1, starting transfers between devices, body(): from_near = lax.ppermute(to_near, axes, across)  10.9 us
  transfers between devices with their start and end apart: 6, of which 1 were waited for; matrix products, arithmetic and copies ran while one was open for 0% of the time, Pallas kernels for 31%

profile of v8, /device:TPU:5, one launch (start us, length us, event | category | flops | bytes accessed | tf_op | source)
XLA Modules:
  0.0 169.8 jit_solution(464890497231078816)
XLA Ops:
  0.0 0.0 copy-start.1
  0.0 0.0 copy-start.3
  0.0 0.0 copy-start
  0.0 58.2 %shard_map.47 = (f32[624,384]{1,0:T(8,128)}, f32[688,128]{1,0:T(8,128)}, f32[656,384]{1,0:T(8,128)}, f32[8,128]{1,0:T(8,128)}) custom-call(s32[4,7]{1,0:T(4,128)} %mask.5, f32[98,512]{1,0:T(8,128)} %panels.5, f32[14,512]{1,0:T(8,128)} %test.5, f32[512,512]{1,0:T(8,128)} %currents.7), custom_call_target="tpu_custom_call" | custom-call | flops 5000000000 | bytes 4000000 | tf_op jit(solution)/shard_map/pallas_call | solution.py:702
  58.2 0.0 copy-start.5
  58.2 1.0 collective-permute-start.2
  59.2 0.0 copy-start.4
  59.2 1.4 collective-permute-start
  60.6 1.0 collective-permute-start.1
  61.7 0.0 copy-done.5
  61.7 0.7 collective-permute-start.3
  62.4 0.0 copy-done.1
  62.4 0.0 copy-done.3
  62.4 0.0 copy-done
  62.4 0.0 copy-done.4
  62.4 26.1 %shard_map.46 = (f32[512,512]{1,0:T(8,128)S(1)}, s32[4,4]{1,0:T(4,128)S(1)}) custom-call(s32[4,7]{1,0:T(4,128)S(1)} %copy-done.4, f32[14,512]{1,0:T(8,128)S(1)} %copy-done.3, f32[98,512]{1,0:T(8,128)S(1)} %copy-done.1, f32[512,512]{1,0:T(8,128)S(1)} %copy-done), custom_call_target="tpu_custom_call" | custom-call | flops 24999999488 | bytes 4000000 | tf_op jit(solution)/shard_map/pallas_call | solution.py:702
  88.6 0.0 collective-permute-done.3.load_far
  88.6 0.8 collective-permute-done.outer
  89.3 0.0 collective-permute-done.2.mate
  89.3 0.0 collective-permute-done.1.far
  89.3 0.0 copy-start.2
  89.3 0.9 copy-done.2
  90.3 40.3 %shard_map.48 = (f32[512,256]{1,0:T(8,128)S(1)}, f32[512,256]{1,0:T(8,128)S(1)}, f32[512,512]{1,0:T(8,128)S(1)}, s32[8,4]{1,0:T(8,128)S(1)}) custom-call(s32[4,7]{1,0:T(4,128)S(1)} %copy-done.4, s32[4,4]{1,0:T(4,128)S(1)} %get-tuple-element.16.done, f32[14,512]{1,0:T(8,128)S(1)} %copy-done.3, f32[98,512]{1,0:T(8,128)S(1)} %copy-done.2, ...), custom_call_target="tpu_custom_call" | custom-call | flops 35000000512 | bytes 4000000 | tf_op jit(solution)/shard_map/pallas_call | solution.py:702
  130.6 10.9 %collective-permute-start.4 = (f32[512,256]{1,0:T(8,128)S(1)}, f32[512,256]{1,0:T(8,128)S(1)}, u32[]{:S(2)}, u32[]{:S(2)}) collective-permute-start(f32[512,256]{1,0:T(8,128)S(1)} %get-tuple-element.23.after), channel_id=1, source_target_pairs={{0,255},{1,2},{2,1},{3,4},{4,3},{5,6},{6,5},{7,8},{8,7},{9,10},{10... | collective-permute-start | bytes 1572872 | tf_op jit(solution)/shard_map/ppermute | solution.py:745
  141.5 0.0 collective-permute-start.5
  141.5 26.7 %shard_map.49 = f32[512,512]{1,0:T(8,128)S(1)} custom-call(s32[8,4]{1,0:T(8,128)S(1)} %get-tuple-element.22.todo, f32[14,512]{1,0:T(8,128)S(1)} %copy-done.3, f32[98,512]{1,0:T(8,128)S(1)} %copy-done.2, f32[512,512]{1,0:T(8,128)S(1)} %copy-done, f32[688,128]{1,0:T(8,128)S(1)} %collective-permute-done.outer, f32[624,384]{1,0:T(8,128)} %collective-permute-done.2.mate, ...), custom_call_target="tpu_custom_call" | custom-call | flops 40000000000 | bytes 4000000 | tf_op jit(solution)/shard_map/pallas_call | solution.py:702
  168.2 0.0 collective-permute-done.4
  168.2 0.0 collective-permute-done.5
  168.3 0.1 broadcast_select_fusion.1
  168.3 1.4 maximum_add_fusion
Async XLA Ops:
  0.0 62.4 %copy-start.1 = (f32[98,512]{1,0:T(8,128)S(1)}, f32[98,512]{1,0:T(8,128)}, u32[]{:S(2)}) copy-start(f32[98,512]{1,0:T(8,128)} %panels.5) | copy-start | bytes 602116
  0.0 62.4 %copy-start.3 = (f32[14,512]{1,0:T(8,128)S(1)}, f32[14,512]{1,0:T(8,128)}, u32[]{:S(2)}) copy-start(f32[14,512]{1,0:T(8,128)} %test.5) | copy-start | bytes 86020
  0.0 62.4 %copy-start = (f32[512,512]{1,0:T(8,128)S(1)}, f32[512,512]{1,0:T(8,128)}, u32[]{:S(2)}) copy-start(f32[512,512]{1,0:T(8,128)} %currents.7) | copy-start | bytes 3145732
  58.2 3.5 %copy-start.5 = (f32[8,128]{1,0:T(8,128)S(1)}, f32[8,128]{1,0:T(8,128)}, u32[]{:S(2)}) copy-start(f32[8,128]{1,0:T(8,128)} %get-tuple-element.20) | copy-start | bytes 12292
  58.2 31.1 %collective-permute-start.2 = (f32[624,384]{1,0:T(8,128)}, f32[624,384]{1,0:T(8,128)}, u32[]{:S(2)}, u32[]{:S(2)}) collective-permute-start(f32[624,384]{1,0:T(8,128)} %get-tuple-element.19), channel_id=1, source_target_pairs={{0,1},{1,0},{2,3},{3,2},{4,5},{5,4},{6,7},{7,6},{8,9},{9,8},{10,11... | collective-permute-start | bytes 2875400 | tf_op jit(solution)/shard_map/ppermute | solution.py:732
  59.2 3.2 %copy-start.4 = (s32[4,7]{1,0:T(4,128)S(1)}, s32[4,7]{1,0:T(4,128)}, u32[]{:S(2)}) copy-start(s32[4,7]{1,0:T(4,128)} %mask.5) | copy-start | bytes 340
  59.2 30.1 %collective-permute-start = (f32[688,128]{1,0:T(8,128)}, f32[688,128]{1,0:T(8,128)S(1)}, u32[]{:S(2)}, u32[]{:S(2)}) collective-permute-start(f32[688,128]{1,0:T(8,128)} %get-tuple-element.17), channel_id=1, source_target_pairs={{0,255},{1,2},{2,1},{3,4},{4,3},{5,6},{6,5},{7,8},{8,7},{9,10},{10... | collective-permute-start | bytes 1056776 | tf_op jit(solution)/shard_map/ppermute | solution.py:730
  60.6 28.7 %collective-permute-start.1 = (f32[656,384]{1,0:T(8,128)}, f32[656,384]{1,0:T(8,128)S(1)}, u32[]{:S(2)}, u32[]{:S(2)}) collective-permute-start(f32[656,384]{1,0:T(8,128)} %get-tuple-element.18), channel_id=1, source_target_pairs={{0,254},{1,3},{2,0},{3,5},{4,2},{5,7},{6,4},{7,9},{8,6},{9,11},{10... | collective-permute-start | bytes 3022856 | tf_op jit(solution)/shard_map/ppermute | solution.py:731
  61.7 26.9 %collective-permute-start.3 = (f32[8,128]{1,0:T(8,128)S(1)}, f32[8,128]{1,0:T(8,128)S(1)}, u32[]{:S(2)}, u32[]{:S(2)}) collective-permute-start(f32[8,128]{1,0:T(8,128)S(1)} %copy-done.5), channel_id=1, source_target_pairs={{254,0},{3,1},{0,2},{5,3},{2,4},{7,5},{4,6},{9,7},{6,8},{11,9},{8,... | collective-permute-start | bytes 12296 | tf_op jit(solution)/shard_map/ppermute | solution.py:729
  89.3 0.9 copy-start.2
  130.6 37.6 %collective-permute-start.4 = (f32[512,256]{1,0:T(8,128)S(1)}, f32[512,256]{1,0:T(8,128)S(1)}, u32[]{:S(2)}, u32[]{:S(2)}) collective-permute-start(f32[512,256]{1,0:T(8,128)S(1)} %get-tuple-element.23.after), channel_id=1, source_target_pairs={{0,255},{1,2},{2,1},{3,4},{4,3},{5,6},{6,5},{7,8},{8,7},{9,10},{10... | collective-permute-start | bytes 1572872 | tf_op jit(solution)/shard_map/ppermute | solution.py:745
  141.5 26.7 %collective-permute-start.5 = (f32[512,256]{1,0:T(8,128)S(1)}, f32[512,256]{1,0:T(8,128)S(1)}, u32[]{:S(2)}, u32[]{:S(2)}) collective-permute-start(f32[512,256]{1,0:T(8,128)S(1)} %get-tuple-element.24), channel_id=1, source_target_pairs={{254,0},{3,1},{0,2},{5,3},{2,4},{7,5},{4,6},{9,7},{6,8},{11,9},{8,... | collective-permute-start | bytes 1572872 | tf_op jit(solution)/shard_map/ppermute | solution.py:746

commit v9 on v7

--- a/solution.py
+++ b/solution.py
@@ -216,8 +216,9 @@
     l1i = k1 * s2r
     l2r = k2 * pr - k6 * qr
     l2i = k2 * qr + k6 * pr
-    kr = weight * (((c2r + pr) + (s2 + 3.0 * p)) + q)
-    ki = weight * (((s2r + qr) + (3.0 * q - c2)) - p)
+    inv3 = inv + 3.0
+    kr = weight * ((c2r + s2) + (p * inv3 + q))
+    ki = weight * ((s2r - c2) + (q * inv3 - p))
     return l1r, l1i, l2r, l2i, kr, ki
 
 
@@ -244,7 +245,7 @@
                 if q == 0 and a == 0:
                     acc = None
                 row = q * JC + g * 8
-                if len(history) >= AHEAD:
+                if len(history) >= AHEAD and len(history) % 2 == 0:
                     buf[pl.ds(spare, 8), 0:BLK] = history[-AHEAD]
                 vals = [buf[row : row + 8, k * 256 + a * BLK : k * 256 + (a + 1) * BLK] for k in range(NOUT)]
                 terms = pair_terms(*vals)
@@ -461,8 +462,12 @@
         return carry
 
     tf[...] = jnp.zeros_like(tf)
-    ftt[...] = jnp.zeros_like(ftt)
-    fts[...] = jnp.zeros_like(fts)
+    spare = NTERM - len(TERMS)
+    ftt[OFF_Z * 8 :, :] = jnp.zeros(((TROWS - OFF_Z) * 8, BLK), F32)
+    for off in (OFF_C, OFF_S):
+        ftt[(off + NTERM - spare) * 8 : (off + NTERM) * 8, :] = jnp.zeros((spare * 8, BLK), F32)
+    fts[(NTERM - spare) * 16 : NTERM * 16, :] = jnp.zeros((spare * 16, BLK), F32)
+    fts[(NTERM + 7) * 16 : (NTERM + 8) * 16, :] = jnp.zeros((16, BLK), F32)
     lax.fori_loop(0, steps, source, 0)
 
 

time: 111 us -> 106 us (0.955)
  the two profiles are of different devices: /device:TPU:100 before, /device:TPU:28 now
where the time goes in v9:
time: 106 us; the launch traced here: 107 us
  Pallas kernels  92.8 us (88%)
  starting transfers between devices  6.29 us (6%)
  waiting for transfers between devices  4.87 us (5%)
  other arithmetic  1.51 us (1%)
    pallas_call x4, Pallas kernels, call(): pl.pallas_call(kernel, out_shape=shapes, in_specs=[smem] * tables + [vmem...  92.8 us
    ppermute x1, waiting for transfers between devices, body(): mate = lax.ppermute(mate, axes, swap)  4.32 us
    ppermute x1, starting transfers between devices, body(): from_far = lax.ppermute(to_far, axes, back)  3.44 us
  transfers between devices with their start and end apart: 6, of which 2 were waited for; matrix products, arithmetic and copies ran while one was open for 0% of the time, Pallas kernels for 46%

profile of v9, /device:TPU:28, one launch (start us, length us, event | category | flops | bytes accessed | tf_op | source)
XLA Modules:
  0.0 106.5 jit_solution(14782383799289608115)
XLA Ops:
  0.0 0.0 copy-start.1
  0.0 0.0 copy-start.3
  0.0 0.0 copy-start
  0.0 3.9 %shard_map.47 = (f32[624,384]{1,0:T(8,128)}, f32[688,128]{1,0:T(8,128)}, f32[656,384]{1,0:T(8,128)}, f32[8,128]{1,0:T(8,128)}) custom-call(s32[4,7]{1,0:T(4,128)} %mask.5, f32[98,512]{1,0:T(8,128)} %panels.5, f32[14,512]{1,0:T(8,128)} %test.5, f32[512,512]{1,0:T(8,128)} %currents.7), custom_call_target="tpu_custom_call" | custom-call | flops 5000000000 | bytes 4000000 | tf_op jit(solution)/shard_map/pallas_call | solution.py:687
  3.9 0.0 copy-start.5
  4.0 1.2 %collective-permute-start.2 = (f32[624,384]{1,0:T(8,128)}, f32[624,384]{1,0:T(8,128)}, u32[]{:S(2)}, u32[]{:S(2)}) collective-permute-start(f32[624,384]{1,0:T(8,128)} %get-tuple-element.19), channel_id=1, source_target_pairs={{0,1},{1,0},{2,3},{3,2},{4,5},{5,4},{6,7},{7,6},{8,9},{9,8},{10,11... | collective-permute-start | bytes 2875400 | tf_op jit(solution)/shard_map/ppermute | solution.py:717
  5.2 0.0 copy-start.4
  5.2 0.2 collective-permute-start
  5.4 1.1 %collective-permute-start.1 = (f32[656,384]{1,0:T(8,128)}, f32[656,384]{1,0:T(8,128)S(1)}, u32[]{:S(2)}, u32[]{:S(2)}) collective-permute-start(f32[656,384]{1,0:T(8,128)} %get-tuple-element.18), channel_id=1, source_target_pairs={{0,254},{1,3},{2,0},{3,5},{4,2},{5,7},{6,4},{7,9},{8,6},{9,11},{10... | collective-permute-start | bytes 3022856 | tf_op jit(solution)/shard_map/ppermute | solution.py:716
  6.5 0.0 copy-done.5
  6.5 0.0 collective-permute-start.3
  6.5 0.0 copy-done.1
  6.5 0.0 copy-done.3
  6.6 0.0 copy-done
  6.6 0.0 copy-done.4
  6.6 26.7 %shard_map.46 = (f32[512,512]{1,0:T(8,128)S(1)}, s32[4,4]{1,0:T(4,128)S(1)}) custom-call(s32[4,7]{1,0:T(4,128)S(1)} %copy-done.4, f32[14,512]{1,0:T(8,128)S(1)} %copy-done.3, f32[98,512]{1,0:T(8,128)S(1)} %copy-done.1, f32[512,512]{1,0:T(8,128)S(1)} %copy-done), custom_call_target="tpu_custom_call" | custom-call | flops 24999999488 | bytes 4000000 | tf_op jit(solution)/shard_map/pallas_call | solution.py:687
  33.3 0.0 collective-permute-done.3.load_far
  33.3 0.5 collective-permute-done.outer
  33.8 4.3 %collective-permute-done.2.mate = f32[624,384]{1,0:T(8,128)} collective-permute-done((f32[624,384]{1,0:T(8,128)}, f32[624,384]{1,0:T(8,128)}, u32[]{:S(2)}, u32[]{:S(2)}) %collective-permute-start.2) | collective-permute-done | bytes 958496 | tf_op jit(solution)/shard_map/ppermute | solution.py:717
  38.1 0.0 collective-permute-done.1.far
  38.1 0.0 copy-start.2
  38.1 0.9 copy-done.2
  39.1 39.6 %shard_map.48 = (f32[512,256]{1,0:T(8,128)S(1)}, f32[512,256]{1,0:T(8,128)S(1)}, f32[512,512]{1,0:T(8,128)S(1)}, s32[8,4]{1,0:T(8,128)S(1)}) custom-call(s32[4,7]{1,0:T(4,128)S(1)} %copy-done.4, s32[4,4]{1,0:T(4,128)S(1)} %get-tuple-element.16.done, f32[14,512]{1,0:T(8,128)S(1)} %copy-done.3, f32[98,512]{1,0:T(8,128)S(1)} %copy-done.2, ...), custom_call_target="tpu_custom_call" | custom-call | flops 35000000512 | bytes 4000000 | tf_op jit(solution)/shard_map/pallas_call | solution.py:687
  78.7 0.3 collective-permute-start.4
  79.0 3.4 %collective-permute-start.5 = (f32[512,256]{1,0:T(8,128)S(1)}, f32[512,256]{1,0:T(8,128)S(1)}, u32[]{:S(2)}, u32[]{:S(2)}) collective-permute-start(f32[512,256]{1,0:T(8,128)S(1)} %get-tuple-element.24), channel_id=1, source_target_pairs={{254,0},{3,1},{0,2},{5,3},{2,4},{7,5},{4,6},{9,7},{6,8},{11,9},{8,... | collective-permute-start | bytes 1572872 | tf_op jit(solution)/shard_map/ppermute | solution.py:731
  82.4 22.6 %shard_map.49 = f32[512,512]{1,0:T(8,128)S(1)} custom-call(s32[8,4]{1,0:T(8,128)S(1)} %get-tuple-element.22.todo, f32[14,512]{1,0:T(8,128)S(1)} %copy-done.3, f32[98,512]{1,0:T(8,128)S(1)} %copy-done.2, f32[512,512]{1,0:T(8,128)S(1)} %copy-done, f32[688,128]{1,0:T(8,128)S(1)} %collective-permute-done.outer, f32[624,384]{1,0:T(8,128)} %collective-permute-done.2.mate, ...), custom_call_target="tpu_custom_call" | custom-call | flops 40000000000 | bytes 4000000 | tf_op jit(solution)/shard_map/pallas_call | solution.py:687
  105.0 0.0 collective-permute-done.4
  105.0 0.0 collective-permute-done.5
  105.0 0.1 broadcast_select_fusion.1
  105.1 1.4 %maximum_add_fusion = f32[512,512]{1,0:T(8,128)} fusion(f32[512,256]{1,0:T(8,128)S(1)} %get-tuple-element.26, f32[512,256]{1,0:T(8,128)S(1)} %get-tuple-element.25, f32[512,512]{1,0:T(8,128)S(1)} %shard_map.49, f32[512,512]{1,0:T(8,128)S(1)} %get-tuple-element.15, f32[512,512]{1,0:T(8,128)S(1)} %get-tuple-element.21), kind=kLoop, calls=%fused_computation | loop fusion | flops 1048576 | bytes 5242880 | tf_op jit(solution)/shard_map/add | solution.py:742
Async XLA Ops:
  0.0 6.5 %copy-start.1 = (f32[98,512]{1,0:T(8,128)S(1)}, f32[98,512]{1,0:T(8,128)}, u32[]{:S(2)}) copy-start(f32[98,512]{1,0:T(8,128)} %panels.5) | copy-start | bytes 602116
  0.0 6.5 %copy-start.3 = (f32[14,512]{1,0:T(8,128)S(1)}, f32[14,512]{1,0:T(8,128)}, u32[]{:S(2)}) copy-start(f32[14,512]{1,0:T(8,128)} %test.5) | copy-start | bytes 86020
  0.0 6.6 %copy-start = (f32[512,512]{1,0:T(8,128)S(1)}, f32[512,512]{1,0:T(8,128)}, u32[]{:S(2)}) copy-start(f32[512,512]{1,0:T(8,128)} %currents.7) | copy-start | bytes 3145732
  3.9 2.6 %copy-start.5 = (f32[8,128]{1,0:T(8,128)S(1)}, f32[8,128]{1,0:T(8,128)}, u32[]{:S(2)}) copy-start(f32[8,128]{1,0:T(8,128)} %get-tuple-element.20) | copy-start | bytes 12292
  4.0 34.2 %collective-permute-start.2 = (f32[624,384]{1,0:T(8,128)}, f32[624,384]{1,0:T(8,128)}, u32[]{:S(2)}, u32[]{:S(2)}) collective-permute-start(f32[624,384]{1,0:T(8,128)} %get-tuple-element.19), channel_id=1, source_target_pairs={{0,1},{1,0},{2,3},{3,2},{4,5},{5,4},{6,7},{7,6},{8,9},{9,8},{10,11... | collective-permute-start | bytes 2875400 | tf_op jit(solution)/shard_map/ppermute | solution.py:717
  5.2 1.4 %copy-start.4 = (s32[4,7]{1,0:T(4,128)S(1)}, s32[4,7]{1,0:T(4,128)}, u32[]{:S(2)}) copy-start(s32[4,7]{1,0:T(4,128)} %mask.5) | copy-start | bytes 340
  5.2 28.6 %collective-permute-start = (f32[688,128]{1,0:T(8,128)}, f32[688,128]{1,0:T(8,128)S(1)}, u32[]{:S(2)}, u32[]{:S(2)}) collective-permute-start(f32[688,128]{1,0:T(8,128)} %get-tuple-element.17), channel_id=1, source_target_pairs={{0,255},{1,2},{2,1},{3,4},{4,3},{5,6},{6,5},{7,8},{8,7},{9,10},{10... | collective-permute-start | bytes 1056776 | tf_op jit(solution)/shard_map/ppermute | solution.py:715
  5.4 32.7 %collective-permute-start.1 = (f32[656,384]{1,0:T(8,128)}, f32[656,384]{1,0:T(8,128)S(1)}, u32[]{:S(2)}, u32[]{:S(2)}) collective-permute-start(f32[656,384]{1,0:T(8,128)} %get-tuple-element.18), channel_id=1, source_target_pairs={{0,254},{1,3},{2,0},{3,5},{4,2},{5,7},{6,4},{7,9},{8,6},{9,11},{10... | collective-permute-start | bytes 3022856 | tf_op jit(solution)/shard_map/ppermute | solution.py:716
  6.5 26.7 %collective-permute-start.3 = (f32[8,128]{1,0:T(8,128)S(1)}, f32[8,128]{1,0:T(8,128)S(1)}, u32[]{:S(2)}, u32[]{:S(2)}) collective-permute-start(f32[8,128]{1,0:T(8,128)S(1)} %copy-done.5), channel_id=1, source_target_pairs={{254,0},{3,1},{0,2},{5,3},{2,4},{7,5},{4,6},{9,7},{6,8},{11,9},{8,... | collective-permute-start | bytes 12296 | tf_op jit(solution)/shard_map/ppermute | solution.py:714
  38.1 0.9 copy-start.2
  78.7 26.3 %collective-permute-start.4 = (f32[512,256]{1,0:T(8,128)S(1)}, f32[512,256]{1,0:T(8,128)S(1)}, u32[]{:S(2)}, u32[]{:S(2)}) collective-permute-start(f32[512,256]{1,0:T(8,128)S(1)} %get-tuple-element.23.after), channel_id=1, source_target_pairs={{0,255},{1,2},{2,1},{3,4},{4,3},{5,6},{6,5},{7,8},{8,7},{9,10},{10... | collective-permute-start | bytes 1572872 | tf_op jit(solution)/shard_map/ppermute | solution.py:730
  79.0 26.1 %collective-permute-start.5 = (f32[512,256]{1,0:T(8,128)S(1)}, f32[512,256]{1,0:T(8,128)S(1)}, u32[]{:S(2)}, u32[]{:S(2)}) collective-permute-start(f32[512,256]{1,0:T(8,128)S(1)} %get-tuple-element.24), channel_id=1, source_target_pairs={{254,0},{3,1},{0,2},{5,3},{2,4},{7,5},{4,6},{9,7},{6,8},{11,9},{8,... | collective-permute-start | bytes 1572872 | tf_op jit(solution)/shard_map/ppermute | solution.py:731
